TPU v7x, 32 devices: a whole 2x2x4 slice. The times are simulated.
32 devices in a mesh: groups: 2 (over y), cls: 8 (over z, x), dom: 2 (over core).
Axes of the slice: x: 2, y: 2, z: 4, core: 2. Of those that a mesh axis runs over, the one named last changes fastest.
Arguments:
- particles: bfloat16 [128, 18432], P(('groups', 'cls', 'dom')), parts along dimension 0, may hold values from -80 to 80
- references: bfloat16 [128, 18432], P(('groups', 'cls')), parts along dimension 0, may hold values from -6 to 6
- class_lists: int32 [128, 32], P(('groups', 'cls', 'dom')), parts along dimension 0, may hold values from 0 to 63, as said below
- offsets: int32 [128, 3, 2], P(('groups', 'cls', 'dom')), parts along dimension 0, may hold values from -8 to 8
- inv_noise: float32 [64], replicated, may hold values from 0.004 to 0.03
Outputs:
- class_sums: float32 [128, 18432], P(('groups', 'cls'), 'dom'), parts along dimension 0
- log_evidence: float32 [128], P(('groups', 'cls', 'dom')), parts along dimension 0
There are 2 independent parts, one for each index of `groups`. A program takes and returns all parts, laid end to end along the dimension named above; an argument that names none is the same for every part. Nothing has to cross between parts.
Inputs may be any that keep to these rules, and one draw needn't show every extreme that they name: `class_lists`: each particle names 32 different classes, the j-th of them in [j * 2, (j + 1) * 2). Among the particles on the devices of one dom index, at most 32 name any one class, and some class is named by exactly 32 of them.
All inputs are finite; a program needn't handle non-finite values.
Results may differ from a plain program's by a relative error of at most 0.0083.
Values may be sent and summed in bfloat16 or wider, within the bound.
No kernel may reach another device: no remote copies, remote signals or barrier semaphores. Data moves between devices by JAX's collectives and lax.ppermute only.
A program may use at most 192 MiB of HBM per device.

v0:
```python
import math

import jax
import jax.numpy as jnp
from jax import lax
from jax.sharding import PartitionSpec as P

ROT = 72
CLASS_LIST_SIZE = 32
BOX = 256


LOWEST = -1e30


def angle_tables(cycles, turns):
    value_index = jnp.arange(cycles * 2 * turns, dtype=jnp.int32)
    cycle_index = value_index // (2 * turns)
    angle_index = value_index % (2 * turns)
    parity = angle_index // turns
    turn_index = angle_index % turns
    radius = (cycle_index + 1).astype(jnp.float32)
    angle_value = (2 * turn_index + parity).astype(jnp.float32) * jnp.float32(math.pi / turns)
    return (radius * jnp.cos(angle_value), radius * jnp.sin(angle_value))


def shift_rows(rows, moves, freq_x, freq_y):
    step_x = moves[..., 0:1].astype(jnp.float32)
    step_y = moves[..., 1:2].astype(jnp.float32)
    phase = (freq_x * step_x + freq_y * step_y) * jnp.float32(2.0 * math.pi / BOX)
    half_width = rows.shape[-1] // 2
    real_part = rows[:, None, :half_width].astype(jnp.float32)
    imag_part = rows[:, None, half_width:].astype(jnp.float32)
    cosine = jnp.cos(phase)
    sine = jnp.sin(phase)
    joined = jnp.concatenate(
        [real_part * cosine + imag_part * sine, imag_part * cosine - real_part * sine], axis=-1
    )
    return joined.astype(jnp.bfloat16)


def cycle_weights(inv_noise, turns):
    return jnp.tile(jnp.repeat(inv_noise, 2 * turns), 2)


def circulant(vectors):
    length = vectors.shape[-1]
    columns = jnp.arange(length, dtype=jnp.int32)
    lookup = (columns[None, :] - columns[:, None]) % length
    return jnp.take(vectors, lookup, axis=-1)


def per_device(particles, references, class_lists, offsets, inv_noise):
    holders = lax.axis_size("cls")
    per_dev = particles.shape[0]
    class_dev = references.shape[0]
    values = particles.shape[1]
    trans_count = offsets.shape[1]
    lines_count = values // ROT
    half_rows = holders * per_dev
    capacity = 2 * per_dev * CLASS_LIST_SIZE // class_dev
    freq_x, freq_y = angle_tables(values // (4 * ROT), ROT)
    every_class = jnp.arange(class_dev * holders, dtype=jnp.int32)
    wanted = jnp.any(class_lists[:, :, None] == every_class[None, None, :], axis=1)
    wanted = wanted.reshape(per_dev, holders, class_dev).transpose(1, 0, 2).astype(jnp.int32)
    needed = jnp.max(wanted, axis=2)
    outgoing = jnp.where(needed[:, :, None] > 0, particles[None], jnp.zeros((), jnp.bfloat16))
    moves_out = jnp.broadcast_to(offsets[None], (holders,) + offsets.shape)
    rows, named, moves = (
        lax.all_to_all(outgoing, "cls", split_axis=0, concat_axis=0, tiled=True),
        lax.all_to_all(wanted, "cls", split_axis=0, concat_axis=0, tiled=True),
        lax.all_to_all(moves_out, "cls", split_axis=0, concat_axis=0, tiled=True),
    )
    rows = rows.reshape(half_rows, values)
    named = named.reshape(half_rows, class_dev)
    moves = moves.reshape(half_rows, trans_count, 2)
    shifted_all = shift_rows(rows, moves, freq_x, freq_y)
    position = jnp.cumsum(named, axis=0) - 1
    row_grid = jnp.broadcast_to(
        jnp.arange(half_rows, dtype=jnp.int32)[:, None], (half_rows, class_dev)
    )
    class_cols = jnp.broadcast_to(
        jnp.arange(class_dev, dtype=jnp.int32)[None, :], (half_rows, class_dev)
    )
    slot_index = jnp.where(named > 0, position, capacity)
    table = (
        jnp.full((class_dev, capacity), half_rows, jnp.int32)
        .at[class_cols, slot_index]
        .set(row_grid, mode="drop")
    )
    valid = table < half_rows
    safe = jnp.where(valid, table, 0)
    scaled = (references.astype(jnp.float32) * cycle_weights(inv_noise, ROT)).astype(jnp.bfloat16)
    row_ids = jnp.arange(half_rows, dtype=jnp.int32)

    def one_class(inputs):
        reference_row, picks = inputs
        shifted = jnp.take(shifted_all, picks, axis=0)
        stacked = shifted.reshape(capacity, trans_count, lines_count, ROT)
        rotated = circulant(reference_row.reshape(lines_count, ROT))
        class_scores = jnp.einsum(
            "rtlk,lpk->rtp", stacked, rotated, preferred_element_type=jnp.float32
        )
        top = jnp.max(class_scores, axis=(1, 2))
        expo = jnp.exp(class_scores - top[:, None, None])
        total = jnp.sum(expo, axis=(1, 2))
        posterior_weight = expo.astype(jnp.bfloat16)
        weight_circ = circulant(posterior_weight)
        returned_sums = jnp.einsum(
            "rtlk,rtmk->rlm", stacked, weight_circ, preferred_element_type=jnp.float32
        )
        return (top, total, returned_sums.reshape(capacity, values))

    tops, totals, backs = lax.map(one_class, (scaled, safe))
    owner = table[:, :, None] == row_ids[None, None, :]
    row_max = jnp.max(jnp.where(owner, tops[:, :, None], LOWEST), axis=1).T
    row_total = jnp.sum(jnp.where(owner, totals[:, :, None], 0.0), axis=1).T
    home_max, home_total = (
        lax.all_to_all(
            row_max.reshape(holders, per_dev, class_dev),
            "cls",
            split_axis=0,
            concat_axis=0,
            tiled=True,
        ),
        lax.all_to_all(
            row_total.reshape(holders, per_dev, class_dev),
            "cls",
            split_axis=0,
            concat_axis=0,
            tiled=True,
        ),
    )
    own_best = jnp.max(home_max, axis=(0, 2))
    own_sum = jnp.sum(home_total * jnp.exp(home_max - own_best[None, :, None]), axis=(0, 2))
    log_evidence = own_best + jnp.log(own_sum)
    spread_best = jnp.broadcast_to(own_best[None], (holders, per_dev))
    spread_sum = jnp.broadcast_to(own_sum[None], (holders, per_dev))
    best, evidence = (
        lax.all_to_all(spread_best, "cls", split_axis=0, concat_axis=0, tiled=True),
        lax.all_to_all(spread_sum, "cls", split_axis=0, concat_axis=0, tiled=True),
    )
    best = best.reshape(half_rows)
    evidence = evidence.reshape(half_rows)
    slot_match = safe[:, :, None] == row_ids[None, None, :]
    slot_best = jnp.sum(jnp.where(slot_match, best[None, None, :], 0.0), axis=2)
    slot_sum = jnp.sum(jnp.where(slot_match, evidence[None, None, :], 0.0), axis=2)
    factor = jnp.where(valid, jnp.exp(tops - slot_best) / slot_sum, 0.0)
    partial_sums = jnp.sum(factor[:, :, None] * backs, axis=1)
    class_sums = lax.psum_scatter(partial_sums, "dom", scatter_dimension=1, tiled=True)
    return (class_sums, log_evidence)


def solution(mesh):
    placed = (
        P(("groups", "cls", "dom"), None),
        P(("groups", "cls"), None),
        P(("groups", "cls", "dom"), None),
        P(("groups", "cls", "dom"), None, None),
        P(),
    )
    return jax.shard_map(
        per_device,
        mesh=mesh,
        in_specs=placed,
        out_specs=(P(("groups", "cls"), "dom"), P(("groups", "cls", "dom"))),
        check_vma=False,
    )
```

profile of v0, /device:TPU:0, one launch (start us, length us, event | category | flops | bytes accessed | tf_op | source)
XLA Modules:
  0.0 941.6 jit_solution(14506565641818039444)
XLA Ops:
  8.5 7.3 all-to-all-start.2
  26.9 6.5 all-to-all-done
  39.2 11.2 %scatter_fusion = s32[8,32]{1,0:T(8,128)S(1)} fusion(s32[8,32]{1,0:T(8,128)S(1)} %broadcast.375, s32[256]{0:T(256)S(1)} %reshape.285, s32[256]{0:T(256)S(1)} %reshape.287), kind=kCustom, calls=%fused_computation.3 | custom fusion | bytes 5120 | tf_op jit(solution)/shard_map/scatter | solution.py:89
  50.4 13.6 %all-to-all-done.1 = bf16[8,4,18432]{2,1,0:T(4,128)(2,1)S(1)} async-done(((bf16[8,4,18432]{2,1,0:T(4,128)(2,1)}), bf16[8,4,18432]{2,1,0:T(4,128)(2,1)S(1)}, u32[]{:S(2)}, u32[]{:S(2)}) %all-to-all-start.1) | async-done | bytes 1179680 | tf_op jit(solution)/shard_map/all_to_all | solution.py:70
  64.5 14.0 %add_convert_fusion = (bf16[32,3,9216]{2,0,1:T(8,128)(2,1)S(1)}, bf16[32,3,9216]{2,0,1:T(8,128)(2,1)S(1)}) fusion(f32[32,9216]{1,0:T(8,128)S(1)} %get-tuple-element.129, f32[32,3]{0,1:T(4,128)S(1)} %get-tuple-element.132, f32[9216]{0:T(1024)S(1)} %get-tuple-element.134, f32[32,3]{0,1:T(4,128)S(1)} %get-tuple-element.133, f32[9216]{0:T(1024)S(1)} %get-tuple-element.135, ...), kind=kLoop, calls=%fused_computation.46 | loop fusion | flops 10616832 | bytes 5972736 | tf_op jit(solution)/shard_map/convert.2
  83.8 793.0 %while.17 = (s32[]{:T(128)}, f32[8,32]{1,0:T(8,128)S(1)}, f32[8,32]{1,0:T(8,128)S(1)}, f32[8,32,18432]{2,1,0:T(8,128)}, s32[8,32]{1,0:T(8,128)S(1)}, /*index=5*/bf16[32,3,18432]{2,1,0:T(4,128)(2,1)}, bf16[8,18432]{1,0:T(8,128)(2,1)}) while((s32[]{:T(128)}, f32[8,32]{1,0:T(8,128)S(1)}, f32[8,32]{1,0:T(8,128)S(1)}, ...), condition=%wide.region_7.8_spmd.clone, body=%wide.region_4.7_spmd.sunk.clone | while | flops 513356448 | bytes 67701744 | solution.py:114
  83.8 8.5 gather_fusion
  97.2 14.9 %gather.40 = bf16[32,3,256,72]{3,2,0,1:T(8,128)(2,1)} reshape(bf16[32,3,18432]{2,0,1:T(8,128)(2,1)S(1)} %copy.112) | data formatting | bytes 7077888 | tf_op jit(solution)/shard_map/while/body/eval_jaxpr/jit(_take)/gather | solution.py:98
  118.2 8.0 copy.113
  127.8 15.6 %gather_fusion.1 = bf16[5184,256]{1,0:T(8,128)(2,1)S(1)} fusion(bf16[256,72]{0,1:T(8,128)(2,1)S(1)} %copy.114, s32[6144]{0:T(1024)S(1)} %pad_clamp_fusion.7), kind=kCustom, calls=%fused_computation.1.clone.1.clone | custom fusion | bytes 5329152 | tf_op jit(solution)/shard_map/while/body/eval_jaxpr/jit(_take)/gather | solution.py:50
  148.0 15.3 %gather_fusion.2 = bf16[5184,32,3]{1,2,0:T(4,128)(2,1)} fusion(bf16[32,3,72]{0,1,2:T(4,128)(2,1)S(1)} %copy.116, s32[6144]{0:T(1024)S(1)} %pad_clamp_fusion.7), kind=kCustom, calls=%fused_computation.2.clone.1.clone | custom fusion | bytes 2011392 | tf_op jit(solution)/shard_map/while/body/eval_jaxpr/jit(_take)/gather | solution.py:50
  163.3 7.2 copy.117
  170.5 6.6 convolution_bitcast_fusion.3
  182.8 8.7 gather_fusion
  196.4 14.9 %gather.40 = bf16[32,3,256,72]{3,2,0,1:T(8,128)(2,1)} reshape(bf16[32,3,18432]{2,0,1:T(8,128)(2,1)S(1)} %copy.112) | data formatting | bytes 7077888 | tf_op jit(solution)/shard_map/while/body/eval_jaxpr/jit(_take)/gather | solution.py:98
  217.4 8.0 copy.113
  227.0 15.6 %gather_fusion.1 = bf16[5184,256]{1,0:T(8,128)(2,1)S(1)} fusion(bf16[256,72]{0,1:T(8,128)(2,1)S(1)} %copy.114, s32[6144]{0:T(1024)S(1)} %pad_clamp_fusion.7), kind=kCustom, calls=%fused_computation.1.clone.1.clone | custom fusion | bytes 5329152 | tf_op jit(solution)/shard_map/while/body/eval_jaxpr/jit(_take)/gather | solution.py:50
  247.1 15.3 %gather_fusion.2 = bf16[5184,32,3]{1,2,0:T(4,128)(2,1)} fusion(bf16[32,3,72]{0,1,2:T(4,128)(2,1)S(1)} %copy.116, s32[6144]{0:T(1024)S(1)} %pad_clamp_fusion.7), kind=kCustom, calls=%fused_computation.2.clone.1.clone | custom fusion | bytes 2011392 | tf_op jit(solution)/shard_map/while/body/eval_jaxpr/jit(_take)/gather | solution.py:50
  262.4 7.2 copy.117
  269.6 6.6 convolution_bitcast_fusion.3
  281.9 8.6 gather_fusion
  295.4 14.9 %gather.40 = bf16[32,3,256,72]{3,2,0,1:T(8,128)(2,1)} reshape(bf16[32,3,18432]{2,0,1:T(8,128)(2,1)S(1)} %copy.112) | data formatting | bytes 7077888 | tf_op jit(solution)/shard_map/while/body/eval_jaxpr/jit(_take)/gather | solution.py:98
  316.4 8.0 copy.113
  326.0 15.6 %gather_fusion.1 = bf16[5184,256]{1,0:T(8,128)(2,1)S(1)} fusion(bf16[256,72]{0,1:T(8,128)(2,1)S(1)} %copy.114, s32[6144]{0:T(1024)S(1)} %pad_clamp_fusion.7), kind=kCustom, calls=%fused_computation.1.clone.1.clone | custom fusion | bytes 5329152 | tf_op jit(solution)/shard_map/while/body/eval_jaxpr/jit(_take)/gather | solution.py:50
  346.2 15.3 %gather_fusion.2 = bf16[5184,32,3]{1,2,0:T(4,128)(2,1)} fusion(bf16[32,3,72]{0,1,2:T(4,128)(2,1)S(1)} %copy.116, s32[6144]{0:T(1024)S(1)} %pad_clamp_fusion.7), kind=kCustom, calls=%fused_computation.2.clone.1.clone | custom fusion | bytes 2011392 | tf_op jit(solution)/shard_map/while/body/eval_jaxpr/jit(_take)/gather | solution.py:50
  361.5 7.2 copy.117
  368.7 6.6 convolution_bitcast_fusion.3
  381.0 8.7 gather_fusion
  394.6 14.9 %gather.40 = bf16[32,3,256,72]{3,2,0,1:T(8,128)(2,1)} reshape(bf16[32,3,18432]{2,0,1:T(8,128)(2,1)S(1)} %copy.112) | data formatting | bytes 7077888 | tf_op jit(solution)/shard_map/while/body/eval_jaxpr/jit(_take)/gather | solution.py:98
  415.6 8.0 copy.113
  425.2 15.6 %gather_fusion.1 = bf16[5184,256]{1,0:T(8,128)(2,1)S(1)} fusion(bf16[256,72]{0,1:T(8,128)(2,1)S(1)} %copy.114, s32[6144]{0:T(1024)S(1)} %pad_clamp_fusion.7), kind=kCustom, calls=%fused_computation.1.clone.1.clone | custom fusion | bytes 5329152 | tf_op jit(solution)/shard_map/while/body/eval_jaxpr/jit(_take)/gather | solution.py:50
  445.4 15.3 %gather_fusion.2 = bf16[5184,32,3]{1,2,0:T(4,128)(2,1)} fusion(bf16[32,3,72]{0,1,2:T(4,128)(2,1)S(1)} %copy.116, s32[6144]{0:T(1024)S(1)} %pad_clamp_fusion.7), kind=kCustom, calls=%fused_computation.2.clone.1.clone | custom fusion | bytes 2011392 | tf_op jit(solution)/shard_map/while/body/eval_jaxpr/jit(_take)/gather | solution.py:50
  460.7 7.2 copy.117
  467.9 6.6 convolution_bitcast_fusion.3
  480.3 8.7 gather_fusion
  493.8 14.9 %gather.40 = bf16[32,3,256,72]{3,2,0,1:T(8,128)(2,1)} reshape(bf16[32,3,18432]{2,0,1:T(8,128)(2,1)S(1)} %copy.112) | data formatting | bytes 7077888 | tf_op jit(solution)/shard_map/while/body/eval_jaxpr/jit(_take)/gather | solution.py:98
  514.8 8.0 copy.113
  524.4 15.6 %gather_fusion.1 = bf16[5184,256]{1,0:T(8,128)(2,1)S(1)} fusion(bf16[256,72]{0,1:T(8,128)(2,1)S(1)} %copy.114, s32[6144]{0:T(1024)S(1)} %pad_clamp_fusion.7), kind=kCustom, calls=%fused_computation.1.clone.1.clone | custom fusion | bytes 5329152 | tf_op jit(solution)/shard_map/while/body/eval_jaxpr/jit(_take)/gather | solution.py:50
  544.6 15.3 %gather_fusion.2 = bf16[5184,32,3]{1,2,0:T(4,128)(2,1)} fusion(bf16[32,3,72]{0,1,2:T(4,128)(2,1)S(1)} %copy.116, s32[6144]{0:T(1024)S(1)} %pad_clamp_fusion.7), kind=kCustom, calls=%fused_computation.2.clone.1.clone | custom fusion | bytes 2011392 | tf_op jit(solution)/shard_map/while/body/eval_jaxpr/jit(_take)/gather | solution.py:50
  559.9 7.2 copy.117
  567.1 6.6 convolution_bitcast_fusion.3
  579.4 8.6 gather_fusion
  592.9 14.9 %gather.40 = bf16[32,3,256,72]{3,2,0,1:T(8,128)(2,1)} reshape(bf16[32,3,18432]{2,0,1:T(8,128)(2,1)S(1)} %copy.112) | data formatting | bytes 7077888 | tf_op jit(solution)/shard_map/while/body/eval_jaxpr/jit(_take)/gather | solution.py:98
  613.8 8.0 copy.113
  623.4 15.6 %gather_fusion.1 = bf16[5184,256]{1,0:T(8,128)(2,1)S(1)} fusion(bf16[256,72]{0,1:T(8,128)(2,1)S(1)} %copy.114, s32[6144]{0:T(1024)S(1)} %pad_clamp_fusion.7), kind=kCustom, calls=%fused_computation.1.clone.1.clone | custom fusion | bytes 5329152 | tf_op jit(solution)/shard_map/while/body/eval_jaxpr/jit(_take)/gather | solution.py:50
  643.6 15.3 %gather_fusion.2 = bf16[5184,32,3]{1,2,0:T(4,128)(2,1)} fusion(bf16[32,3,72]{0,1,2:T(4,128)(2,1)S(1)} %copy.116, s32[6144]{0:T(1024)S(1)} %pad_clamp_fusion.7), kind=kCustom, calls=%fused_computation.2.clone.1.clone | custom fusion | bytes 2011392 | tf_op jit(solution)/shard_map/while/body/eval_jaxpr/jit(_take)/gather | solution.py:50
  658.9 7.2 copy.117
  666.1 6.6 convolution_bitcast_fusion.3
  678.5 8.6 gather_fusion
  692.1 14.9 %gather.40 = bf16[32,3,256,72]{3,2,0,1:T(8,128)(2,1)} reshape(bf16[32,3,18432]{2,0,1:T(8,128)(2,1)S(1)} %copy.112) | data formatting | bytes 7077888 | tf_op jit(solution)/shard_map/while/body/eval_jaxpr/jit(_take)/gather | solution.py:98
  713.0 8.0 copy.113
  722.6 15.6 %gather_fusion.1 = bf16[5184,256]{1,0:T(8,128)(2,1)S(1)} fusion(bf16[256,72]{0,1:T(8,128)(2,1)S(1)} %copy.114, s32[6144]{0:T(1024)S(1)} %pad_clamp_fusion.7), kind=kCustom, calls=%fused_computation.1.clone.1.clone | custom fusion | bytes 5329152 | tf_op jit(solution)/shard_map/while/body/eval_jaxpr/jit(_take)/gather | solution.py:50
  742.8 15.3 %gather_fusion.2 = bf16[5184,32,3]{1,2,0:T(4,128)(2,1)} fusion(bf16[32,3,72]{0,1,2:T(4,128)(2,1)S(1)} %copy.116, s32[6144]{0:T(1024)S(1)} %pad_clamp_fusion.7), kind=kCustom, calls=%fused_computation.2.clone.1.clone | custom fusion | bytes 2011392 | tf_op jit(solution)/shard_map/while/body/eval_jaxpr/jit(_take)/gather | solution.py:50
  758.1 7.2 copy.117
  765.3 6.6 convolution_bitcast_fusion.3
  777.6 8.7 gather_fusion
  791.2 14.9 %gather.40 = bf16[32,3,256,72]{3,2,0,1:T(8,128)(2,1)} reshape(bf16[32,3,18432]{2,0,1:T(8,128)(2,1)S(1)} %copy.112) | data formatting | bytes 7077888 | tf_op jit(solution)/shard_map/while/body/eval_jaxpr/jit(_take)/gather | solution.py:98
  812.2 8.0 copy.113
  821.8 15.6 %gather_fusion.1 = bf16[5184,256]{1,0:T(8,128)(2,1)S(1)} fusion(bf16[256,72]{0,1:T(8,128)(2,1)S(1)} %copy.114, s32[6144]{0:T(1024)S(1)} %pad_clamp_fusion.7), kind=kCustom, calls=%fused_computation.1.clone.1.clone | custom fusion | bytes 5329152 | tf_op jit(solution)/shard_map/while/body/eval_jaxpr/jit(_take)/gather | solution.py:50
  841.9 15.3 %gather_fusion.2 = bf16[5184,32,3]{1,2,0:T(4,128)(2,1)} fusion(bf16[32,3,72]{0,1,2:T(4,128)(2,1)S(1)} %copy.116, s32[6144]{0:T(1024)S(1)} %pad_clamp_fusion.7), kind=kCustom, calls=%fused_computation.2.clone.1.clone | custom fusion | bytes 2011392 | tf_op jit(solution)/shard_map/while/body/eval_jaxpr/jit(_take)/gather | solution.py:50
  857.2 7.2 copy.117
  864.4 6.6 convolution_bitcast_fusion.3
  891.3 6.4 all-to-all-done.5
  919.1 10.0 %multiply_reduce_fusion = f32[8,18432]{1,0:T(8,128)} fusion(f32[8,32,18432]{2,1,0:T(8,128)} %get-tuple-element.96, f32[8,32]{1,0:T(8,128)S(1)} %compare_select_fusion.5), kind=kLoop, calls=%fused_computation.43 | loop fusion | flops 9289728 | bytes 19465216 | tf_op jit(solution)/shard_map/reduce_sum | solution.py:149
  (227 shorter events, 248.4 us)
Async XLA Ops:
  7.2 29.8 %copy-start.2 = (bf16[8,18432]{1,0:T(8,128)(2,1)S(1)}, bf16[8,18432]{1,0:T(8,128)(2,1)}, u32[]{:S(2)}) copy-start(bf16[8,18432]{1,0:T(8,128)(2,1)} %param.8) | copy-start | bytes 884740
  8.5 13.9 %all-to-all-start.2 = ((s32[8,4,3,2]{1,3,2,0:T(2,128)}), s32[8,4,3,2]{1,3,2,0:T(2,128)S(1)}, u32[]{:S(2)}, u32[]{:S(2)}) async-start(s32[8,4,3,2]{1,3,2,0:T(2,128)} %broadcast_in_dim.199), calls=%async_computation.2 | async-start | bytes 49152 | tf_op jit(solution)/shard_map/all_to_all | solution.py:72
  22.4 11.0 %all-to-all-start = ((s32[8,4,8]{2,1,0:T(4,128)}), s32[8,4,8]{2,1,0:T(4,128)S(1)}, u32[]{:S(2)}, u32[]{:S(2)}) async-start(s32[8,4,8]{2,1,0:T(4,128)} %copy.72), calls=%async_computation | async-start | bytes 32768 | tf_op jit(solution)/shard_map/all_to_all | solution.py:71
  33.4 30.5 %all-to-all-start.1 = ((bf16[8,4,18432]{2,1,0:T(4,128)(2,1)}), bf16[8,4,18432]{2,1,0:T(4,128)(2,1)S(1)}, u32[]{:S(2)}, u32[]{:S(2)}) async-start(bf16[8,4,18432]{2,1,0:T(4,128)(2,1)} %broadcast_select_fusion.1), calls=%async_computation.1 | async-start | bytes 2359296 | tf_op jit(solution)/shard_map/all_to_all | solution.py:70
  50.4 28.0 %copy-start = (s32[8,32]{1,0:T(8,128)}, s32[8,32]{1,0:T(8,128)S(1)}, u32[]{:S(2)}) copy-start(s32[8,32]{1,0:T(8,128)S(1)} %scatter_fusion) | copy-start | bytes 3076
  83.8 793.0 %copy-start.1 = (s32[8,32]{1,0:T(8,128)S(1)}, s32[8,32]{1,0:T(8,128)}, u32[]{:S(2)}) copy-start(s32[8,32]{1,0:T(8,128)} %copy-done) | copy-start | bytes 3076
  877.6 10.2 %all-to-all-start.3 = ((f32[8,4,8]{2,1,0:T(4,128)}), f32[8,4,8]{2,1,0:T(4,128)S(1)}, u32[]{:S(2)}, u32[]{:S(2)}) async-start(f32[8,4,8]{2,1,0:T(4,128)} %bitcast.16), calls=%async_computation.3 | async-start | bytes 32768 | tf_op jit(solution)/shard_map/all_to_all | solution.py:119
  887.8 9.8 %all-to-all-start.5 = ((f32[8,4,8]{2,1,0:T(4,128)}), f32[8,4,8]{2,1,0:T(4,128)S(1)}, u32[]{:S(2)}, u32[]{:S(2)}) async-start(f32[8,4,8]{2,1,0:T(4,128)} %bitcast.18), calls=%async_computation.5 | async-start | bytes 32768 | tf_op jit(solution)/shard_map/all_to_all | solution.py:126
  898.2 9.6 %all-to-all-start.4 = ((f32[8,1,4]{2,1,0:T(1,128)}), f32[8,1,4]{2,1,0:T(1,128)S(1)}, u32[]{:S(2)}, u32[]{:S(2)}) async-start(f32[8,1,4]{2,1,0:T(1,128)} %broadcast_in_dim.203), calls=%async_computation.4 | async-start | bytes 8192 | tf_op jit(solution)/shard_map/all_to_all | solution.py:140
  908.5 9.6 %all-to-all-start.6 = ((f32[8,1,4]{2,1,0:T(1,128)}), f32[8,1,4]{2,1,0:T(1,128)S(1)}, u32[]{:S(2)}, u32[]{:S(2)}) async-start(f32[8,1,4]{2,1,0:T(1,128)} %broadcast_in_dim.208), calls=%async_computation.6 | async-start | bytes 8192 | tf_op jit(solution)/shard_map/all_to_all | solution.py:141
  911.8 22.9 %reduce-scatter.2.cloned.1.call-start = ((), (), s32[]{:S(2)}) async-start(), calls=%async_computation.8 | async-start | bytes 884736 | tf_op jit(solution)/shard_map/reduce_scatter | solution.py:150
Sparse Core Ops, SparseCore 0:
  929.3 5.3 reduce-scatter.1
where the time goes:
time: 946 us; the launch traced here: 942 us
  local copies, waits for them, and re-layouts  680 us (72%)
  matrix products  84.7 us (9%)
  other arithmetic  83 us (9%)
  waiting for transfers between devices  50.1 us (5%)
  starting transfers between devices  28.8 us (3%)
  between operations  14.3 us (2%)
    gather x24, local copies, waits for them, and re-layouts, circulant(): return jnp.take(vectors, lookup, axis=-1)  305 us
    gather x24, local copies, waits for them, and re-layouts, one_class(): shifted = jnp.take(shifted_all, picks, axis=0)  227 us
    select_n x8, local copies, waits for them, and re-layouts, one_class(): shifted = jnp.take(shifted_all, picks, axis=0)  64.1 us
    dot_general x8, matrix products, one_class(): jnp.einsum('rtlk,rtmk->rlm', stacked, weight_circ, preferred_element_type...  52.5 us
    select_n x16, other arithmetic, one_class(): shifted = jnp.take(shifted_all, picks, axis=0)  48.7 us
    broadcast_in_dim x8, local copies, waits for them, and re-layouts, per_device(): tops, totals, backs = lax.map(one_class, (scaled, safe))  33.3 us
    dot_general x8, matrix products, one_class(): jnp.einsum('rtlk,lpk->rtp', stacked, rotated, preferred_element_type=jnp....  32.2 us
  transfers between devices with their start and end apart: 8, of which 8 were waited for; matrix products, arithmetic and copies ran while one was open for 2% of the time, Pallas kernels for 0%

commit v1 on v0

v1 whole, which is shorter than its diff:
```python
import math

import jax
import jax.numpy as jnp
import numpy as np
from jax import lax
from jax.experimental import pallas as pl
from jax.experimental.pallas import tpu as pltpu
from jax.sharding import PartitionSpec as P

ROT = 72
CYCLES = 64
CLASS_LIST_SIZE = 32
BOX = 256
TRANS = 3
PER_DEV = 4
CLS = 8
SLOTS = 8
LANES = 256
HALF = 128
GROUP = 16 * ROT
ROWS = ROT * PER_DEV
REF_ROWS = ROT * CLS
PAIRS = ROT // 2
LOWEST = -1e30
VMEM = 48 * 1024 * 1024

F32 = jnp.float32
BF16 = jnp.bfloat16


def frequency_rows():
    turn = np.arange(ROT)[:, None]
    lane = np.arange(HALF)[None, :]
    line = (lane % 8) * 16 + lane // 8
    radius = line // 2 + 1
    angle = math.pi * (2 * turn + line % 2) / ROT
    fx = radius * np.cos(angle) / BOX
    fy = radius * np.sin(angle) / BOX
    rep = lambda f: np.repeat(f, PER_DEV, axis=0).astype(np.float32)
    return rep(fx), rep(fy)


def half_turn_polynomials():
    t = np.cos(np.pi * (np.arange(400) + 0.5) / 400)
    z = (t + 1) / 8
    v = np.sqrt(z)
    sin_fit = np.polynomial.chebyshev.Chebyshev.fit(z, np.sin(np.pi * v) / v, 4, domain=[0, 0.25])
    cos_fit = np.polynomial.chebyshev.Chebyshev.fit(z, np.cos(np.pi * v), 5, domain=[0, 0.25])
    to_list = lambda f: [float(c) for c in f.convert(kind=np.polynomial.Polynomial).coef]
    return to_list(sin_fit), to_list(cos_fit)


SIN_COEF, COS_COEF = half_turn_polynomials()


def horner(coef, z):
    total = jnp.full_like(z, coef[-1])
    for c in coef[-2::-1]:
        total = total * z + c
    return total


def cos_sin_turns(u):
    v = u - jnp.round(u)
    z = v * v
    s = v * horner(SIN_COEF, z)
    c = horner(COS_COEF, z)
    s2 = s + s
    return 1.0 - s2 * s, s2 * c


def turn_major(x_ref, grid_ref, lines_ref, out_ref, count):
    for g in range(16):
        for tile in range(GROUP // HALF):
            start = g * GROUP + tile * HALF
            grid_ref[tile, pl.ds(g, count, stride=16), :] = x_ref[:, start : start + HALF].astype(F32)
    for h in range(16):
        tile, shift = divmod(ROT * h, HALF)
        if shift + ROT <= HALF:
            part = grid_ref[tile]
            if shift:
                part = pltpu.roll(part, HALF - shift, 1)
        else:
            part = jnp.concatenate([grid_ref[tile], grid_ref[tile + 1]], axis=1)
            part = pltpu.roll(part, LANES - shift, 1)[:, :HALF]
        lines_ref[:, :, h] = part.reshape(count, 2, 8, HALF)
    for p in range(count):
        for half in range(2):
            turns = lines_ref[p, half].reshape(HALF, HALF).T
            out_ref[half, pl.ds(p, ROT, stride=count), :] = turns[:ROT]


def particle_kernel(nbit, x_ref, list_ref, move_ref, out_ref, grid_ref, lines_ref, turns_ref):
    turn_major(x_ref, grid_ref, lines_ref, turns_ref, PER_DEV)
    out_ref[:ROWS] = jnp.concatenate([turns_ref[0], turns_ref[1]], axis=1).astype(BF16)
    lists = list_ref[...]
    lane = lax.broadcasted_iota(jnp.int32, (PER_DEV, LANES), 1)
    parts = []
    for b in range(nbit):
        named = jnp.zeros((PER_DEV, LANES), F32)
        for j in range(CLASS_LIST_SIZE):
            named = jnp.where(lists[:, j : j + 1] == lane + b * LANES, 1.0, named)
        parts += [named, named]
    row = lax.broadcasted_iota(jnp.int32, (8, LANES), 0) % PER_DEV
    lane = lax.broadcasted_iota(jnp.int32, (8, LANES), 1)
    moves = jnp.zeros((8, LANES), F32)
    for p in range(PER_DEV):
        for t in range(TRANS):
            for a in range(2):
                here = (row == p) & (lane == 8 * a + t)
                moves = jnp.where(here, move_ref[p, t, a].astype(F32), moves)
    parts.append(moves)
    if nbit % 2 == 0:
        parts.append(jnp.zeros((8, LANES), F32))
    out_ref[ROWS:] = jnp.concatenate(parts, axis=0).astype(BF16)


def reference_kernel(x_ref, w_ref, out_ref, grid_ref, lines_ref, turns_ref):
    turn_major(x_ref, grid_ref, lines_ref, turns_ref, CLS)
    scaled = (jnp.concatenate([turns_ref[0], turns_ref[1]], axis=1) * w_ref[...]).astype(BF16)
    out_ref[:REF_ROWS] = scaled
    out_ref[REF_ROWS:] = scaled


def xor_lanes(x, bits):
    lane = lax.broadcasted_iota(jnp.int32, x.shape, x.ndim - 1)
    width = x.shape[-1]
    for b in range(3):
        if bits >> b & 1:
            step = 8 << b
            down = pltpu.roll(x, width - step, x.ndim - 1)
            up = pltpu.roll(x, step, x.ndim - 1)
            x = jnp.where((lane // step) % 2 == 0, down, up)
    return x


def score_kernel(nbit, me_ref, *refs):
    blocks = refs[:SLOTS]
    fx_ref, fy_ref, ref_ref, x_ref, e_ref, stat_ref, acc_ref = refs[SLOTS:]
    moves = []
    for s in range(SLOTS):
        m = blocks[s][0, ROWS + 8 * nbit - 8 * (nbit % 2) : ROWS + 8 * nbit + 16 - 8 * (nbit % 2)].astype(F32)
        m = m[8 * (nbit % 2) : 8 * (nbit % 2) + 8]
        m = jnp.concatenate([m, m], axis=0)
        moves.append([
            (jnp.broadcast_to(m[:, t : t + 1], (16, HALF)), jnp.broadcast_to(m[:, 8 + t : 9 + t], (16, HALF)))
            for t in range(TRANS)
        ])
    acc_ref[...] = jnp.zeros_like(acc_ref)

    def step(q, carry):
        rows = pl.ds(pl.multiple_of(q * 16, 16), 16)
        fx = fx_ref[rows, :]
        fy = fy_ref[rows, :]
        tiles = [[None] * SLOTS for _ in range(TRANS)]
        for s in range(SLOTS):
            block = blocks[s][0, rows, :].astype(F32)
            a = block[:, :HALF]
            b = block[:, HALF:]
            for t in range(TRANS):
                dx, dy = moves[s][t]
                c, sn = cos_sin_turns(fx * dx + fy * dy)
                tiles[t][s] = (a * c + b * sn, b * c - a * sn)
        for half in range(2):
            packed = []
            for t in range(TRANS):
                for s in range(0, SLOTS, 2):
                    cols = [
                        jnp.concatenate(
                            [tiles[t][s][r][half * 8 : half * 8 + 8], tiles[t][s + 1][r][half * 8 : half * 8 + 8]],
                            axis=0,
                        )
                        for r in range(2)
                    ]
                    packed.append(jnp.concatenate(cols, axis=1).astype(BF16))
            packed.append(jnp.zeros((64, LANES), BF16))
            images = jnp.concatenate(packed, axis=0)
            x_ref[0, 2 * q + half] = images
            turned = ref_ref[pl.ds(pl.multiple_of((2 * q + half) * 16, 16), REF_ROWS), :]
            acc_ref[...] += lax.dot_general(turned, images, (((1,), (1,)), ((), ())), preferred_element_type=F32)
        return carry

    lax.fori_loop(0, PAIRS // 2, step, 0)

    me = me_ref[0]
    lane = lax.broadcasted_iota(jnp.int32, (CLS, LANES), 1)
    row = lax.broadcasted_iota(jnp.int32, (CLS, LANES), 0)
    named = jnp.zeros((CLS, SLOTS * 16), F32)
    for b in range(nbit):
        pick = (lane + b * LANES == me * CLS + row).astype(F32).astype(BF16)
        first = ROWS + 16 * (b // 2)
        bits = jnp.concatenate([blocks[s][0, first : first + 16] for s in range(SLOTS)], axis=0)
        got = lax.dot_general(pick, bits, (((1,), (1,)), ((), ())), preferred_element_type=F32)
        if b % 2:
            got = pltpu.roll(got, SLOTS * 16 - 8, 1)
        named = named + got
    src = lax.broadcasted_iota(jnp.int32, (SLOTS * 16, LANES), 0)
    dst = lax.broadcasted_iota(jnp.int32, (SLOTS * 16, LANES), 1)
    wanted_row = (dst % 64) // 8 * 16 + dst % PER_DEV
    ok = (src == wanted_row) & (dst < 64 * TRANS) & (dst % 8 < PER_DEV)
    mask = jnp.dot(named.astype(BF16), ok.astype(F32).astype(BF16), preferred_element_type=F32) > 0.5

    def body_max(i, top):
        nxt = jnp.where(i == ROT - 1, 0, i + 1)
        s = acc_ref[pl.ds(pl.multiple_of(i * 8, 8), 8), :]
        o = acc_ref[pl.ds(pl.multiple_of(nxt * 8, 8), 8), :]
        s = jnp.where(mask, s + pltpu.roll(o, LANES - 4, 1), LOWEST)
        e_ref[0, pl.ds(pl.multiple_of(i * 8, 8), 8), :] = s
        return jnp.maximum(top, s)

    top = lax.fori_loop(0, ROT, body_max, jnp.full((CLS, LANES), LOWEST, F32), unroll=8)
    top = jnp.max(top, axis=0, keepdims=True)
    top = jnp.broadcast_to(top, (8, LANES))
    for shift in (64, 128):
        top = jnp.maximum(top, pltpu.roll(top, shift, 1))

    def body_exp(i, total):
        rows = pl.ds(pl.multiple_of(i * 8, 8), 8)
        e = jnp.where(mask, jnp.exp(e_ref[0, rows, :] - top), 0.0)
        e_ref[0, rows, :] = e
        return total + e

    total = lax.fori_loop(0, ROT, body_exp, jnp.zeros((CLS, LANES), F32), unroll=8)
    total = jnp.broadcast_to(jnp.sum(total, axis=0, keepdims=True), (8, LANES))
    for shift in (64, 128):
        total = total + pltpu.roll(total, shift, 1)
    first = lax.broadcasted_iota(jnp.int32, (8, HALF), 0) == 0
    stat_ref[0] = jnp.where(first, top[:, :HALF], total[:, :HALF])


def spread_kernel(holders, me_ref, stat_ref, out_ref):
    blocks = holders // SLOTS
    me = me_ref[0]
    for low in range(SLOTS):
        for n in range(blocks):
            moved = xor_lanes(stat_ref[n], low)
            for high in range(blocks):
                out_ref[me ^ (high * SLOTS + low), n ^ high] = moved


def back_kernel(holders, me_ref, got_ref, stat_ref, e_ref, x_ref, keep_ref, send_ref, log_ref, w_ref, acc_ref):
    n = pl.program_id(0)
    top = got_ref[0, n]
    for d in range(1, holders):
        top = jnp.maximum(top, got_ref[d, n])
    best = jnp.broadcast_to(top[0:1], (8, HALF))
    evidence = jnp.zeros((8, HALF), F32)
    for d in range(holders):
        got = got_ref[d, n]
        one = jnp.broadcast_to(got[0:1], (8, HALF))
        evidence = evidence + jnp.broadcast_to(got[1:2], (8, HALF)) * jnp.exp(one - best)
    own = jnp.broadcast_to(stat_ref[0, 0:1], (8, HALF))
    factor = jnp.exp(own - best) / evidence

    @pl.when(n == 0)
    def _():
        log_ref[...] = best + jnp.log(evidence)
        acc_ref[...] = jnp.zeros_like(acc_ref)

    factor = jnp.concatenate([factor, factor], axis=1)
    lane = lax.broadcasted_iota(jnp.int32, (8, LANES), 1)
    live = (lane % 8 < PER_DEV) & (lane < 64 * TRANS)
    factor = jnp.where(live, factor, 0.0)

    def weights(i):
        return jnp.where(live, e_ref[0, i * 8 : i * 8 + 8, :] * factor, 0.0)

    before = weights(ROT - 1)
    for i in range(0, ROT, 2):
        one = weights(i)
        two = weights(i + 1)
        pair = jnp.concatenate(
            [one + pltpu.roll(before, 4, 1), two + pltpu.roll(one, 4, 1)], axis=0
        ).astype(BF16)
        w_ref[i * 8 : i * 8 + 16, :] = pair
        w_ref[REF_ROWS + i * 8 : REF_ROWS + i * 8 + 16, :] = pair
        before = two

    def step(q, carry):
        total = acc_ref[...]
        for r in range(4):
            j = 4 * q + r
            turned = w_ref[pl.ds(pl.multiple_of((PAIRS - j) * 16, 16), REF_ROWS), :]
            total = total + jnp.dot(turned, x_ref[0, j], preferred_element_type=F32)
        acc_ref[...] = total
        return carry

    lax.fori_loop(0, PAIRS // 4, step, 0)

    @pl.when((n == pl.num_programs(0) - 1) & (me_ref[1] == 0))
    def _():
        keep_ref[...] = acc_ref[:, :HALF]
        send_ref[...] = acc_ref[:, HALF:]

    @pl.when((n == pl.num_programs(0) - 1) & (me_ref[1] == 1))
    def _():
        keep_ref[...] = acc_ref[:, HALF:]
        send_ref[...] = acc_ref[:, :HALF]


def flat_kernel(a_ref, b_ref, out_ref, sum_ref, lines_ref, grid_ref):
    sum_ref[:REF_ROWS] = a_ref[...] + b_ref[...]
    lane = lax.broadcasted_iota(jnp.int32, (CLS * 8, HALF), 1)
    for c in range(CLS):
        turns = sum_ref[pl.ds(c, HALF, stride=CLS), :]
        lines_ref[c] = turns.T
    for tile in range(GROUP // HALF):
        made = None
        for h in range(16):
            start = ROT * h - tile * HALF
            if start >= HALF or start + ROT <= 0:
                continue
            part = lines_ref[:, h * 8 : h * 8 + 8, :].reshape(CLS * 8, HALF)
            if start % HALF:
                part = pltpu.roll(part, start % HALF, 1)
            made = part if made is None else jnp.where(lane >= start, part, made)
        grid_ref[tile] = made
        for g in range(8):
            start = g * GROUP + tile * HALF
            out_ref[:, start : start + HALF] = grid_ref[tile, pl.ds(g, CLS, stride=8), :]


def gather_slots(block, holders):
    def swap(x, bits):
        return lax.ppermute(x, "cls", [(i, i ^ bits) for i in range(holders)])

    if holders == 8:
        r4 = swap(block, 4)
        r2 = swap(block, 2)
        r1 = swap(block, 1)
        r3 = swap(r2, 1)
        r6 = swap(r4, 2)
        r5 = swap(r4, 1)
        r7 = swap(r6, 1)
        return [x[None] for x in (block, r1, r2, r3, r4, r5, r6, r7)]
    slots = block[None]
    bits = 1
    while bits < holders:
        slots = jnp.concatenate([slots, swap(slots, bits)], axis=0)
        bits *= 2
    return [slots[s::SLOTS] for s in range(SLOTS)]


def per_device(particles, references, class_lists, offsets, inv_noise):
    holders = lax.axis_size("cls")
    nblocks = holders // SLOTS
    nbit = -(-holders * CLS // LANES)
    rows = ROWS + -(-(8 * nbit + 8) // 16) * 16
    vm = pl.BlockSpec(memory_space=pltpu.VMEM)
    sm = pl.BlockSpec(memory_space=pltpu.SMEM)
    params = pltpu.CompilerParams(vmem_limit_bytes=VMEM)
    me = jnp.stack([lax.axis_index("cls"), lax.axis_index("dom")]).astype(jnp.int32)

    def scratch(count):
        return [
            pltpu.VMEM((GROUP // HALF, count * 16, HALF), F32),
            pltpu.VMEM((count, 2, 16, 8, HALF), F32),
            pltpu.VMEM((2, ROT * count, HALF), F32),
        ]

    block = pl.pallas_call(
        lambda *a: particle_kernel(nbit, *a),
        out_shape=jax.ShapeDtypeStruct((rows, LANES), BF16),
        in_specs=[vm, vm, sm],
        out_specs=vm,
        scratch_shapes=scratch(PER_DEV),
        compiler_params=params,
        name="particle_turns",
    )(particles, class_lists, offsets)
    slots = gather_slots(block, holders)

    weights = jnp.repeat(inv_noise.reshape(8, 8).T, 2, axis=0).reshape(1, HALF)
    weights = jnp.concatenate([weights, weights], axis=1)
    refs = pl.pallas_call(
        reference_kernel,
        out_shape=jax.ShapeDtypeStruct((2 * REF_ROWS, LANES), BF16),
        in_specs=[vm, vm],
        out_specs=vm,
        scratch_shapes=scratch(CLS),
        compiler_params=params,
        name="reference_turns",
    )(references, weights)

    fx, fy = frequency_rows()
    full = lambda *shape: pl.BlockSpec(shape, lambda n, *_: (0,) * len(shape))
    images, expo, stat = pl.pallas_call(
        lambda *a: score_kernel(nbit, *a),
        out_shape=(
            jax.ShapeDtypeStruct((nblocks, PAIRS, LANES, LANES), BF16),
            jax.ShapeDtypeStruct((nblocks, REF_ROWS, LANES), F32),
            jax.ShapeDtypeStruct((nblocks, 8, HALF), F32),
        ),
        grid_spec=pltpu.PrefetchScalarGridSpec(
            num_scalar_prefetch=1,
            grid=(nblocks,),
            in_specs=[pl.BlockSpec((1, rows, LANES), lambda n, *_: (n, 0, 0))] * SLOTS
            + [full(ROWS, HALF), full(ROWS, HALF), full(2 * REF_ROWS, LANES)],
            out_specs=[
                pl.BlockSpec((1, PAIRS, LANES, LANES), lambda n, *_: (n, 0, 0, 0)),
                pl.BlockSpec((1, REF_ROWS, LANES), lambda n, *_: (n, 0, 0)),
                pl.BlockSpec((1, 8, HALF), lambda n, *_: (n, 0, 0)),
            ],
            scratch_shapes=[pltpu.VMEM((REF_ROWS, LANES), F32)],
        ),
        compiler_params=params,
        name="scores",
    )(me, *slots, jnp.asarray(fx), jnp.asarray(fy), refs)

    spread = pl.pallas_call(
        lambda *a: spread_kernel(holders, *a),
        out_shape=jax.ShapeDtypeStruct((holders, nblocks, 8, HALF), F32),
        in_specs=[sm, vm],
        out_specs=vm,
        compiler_params=params,
        name="spread",
    )(me, stat)
    got = lax.all_to_all(
        spread.reshape(holders, nblocks * 8, HALF), "cls", split_axis=0, concat_axis=0, tiled=True
    ).reshape(holders, nblocks, 8, HALF)

    keep, send, logs = pl.pallas_call(
        lambda *a: back_kernel(holders, *a),
        out_shape=(
            jax.ShapeDtypeStruct((REF_ROWS, HALF), F32),
            jax.ShapeDtypeStruct((REF_ROWS, HALF), F32),
            jax.ShapeDtypeStruct((8, HALF), F32),
        ),
        grid_spec=pltpu.PrefetchScalarGridSpec(
            num_scalar_prefetch=1,
            grid=(nblocks,),
            in_specs=[
                full(holders, nblocks, 8, HALF),
                pl.BlockSpec((1, 8, HALF), lambda n, *_: (n, 0, 0)),
                pl.BlockSpec((1, REF_ROWS, LANES), lambda n, *_: (n, 0, 0)),
                pl.BlockSpec((1, PAIRS, LANES, LANES), lambda n, *_: (n, 0, 0, 0)),
            ],
            out_specs=[full(REF_ROWS, HALF), full(REF_ROWS, HALF), full(8, HALF)],
            scratch_shapes=[pltpu.VMEM((2 * REF_ROWS, LANES), BF16), pltpu.VMEM((REF_ROWS, LANES), F32)],
        ),
        compiler_params=params,
        name="class_sums",
    )(me, got, stat, expo, images)

    other = lax.ppermute(send, "dom", [(0, 1), (1, 0)])
    sums = pl.pallas_call(
        flat_kernel,
        out_shape=jax.ShapeDtypeStruct((CLS, GROUP * 8), F32),
        in_specs=[vm, vm],
        out_specs=vm,
        scratch_shapes=[
            pltpu.VMEM((HALF * CLS, HALF), F32),
            pltpu.VMEM((CLS, HALF, HALF), F32),
            pltpu.VMEM((GROUP // HALF, CLS * 8, HALF), F32),
        ],
        compiler_params=params,
        name="flat_rows",
    )(keep, other)
    return sums, logs[0, :PER_DEV]


def solution(mesh):
    placed = (
        P(("groups", "cls", "dom"), None),
        P(("groups", "cls"), None),
        P(("groups", "cls", "dom"), None),
        P(("groups", "cls", "dom"), None, None),
        P(),
    )
    return jax.shard_map(
        per_device,
        mesh=mesh,
        in_specs=placed,
        out_specs=(P(("groups", "cls"), "dom"), P(("groups", "cls", "dom"))),
        check_vma=False,
    )
```

time: 946 us -> 71.8 us (0.08)
  local copies, waits for them, and re-layouts: 680 us -> 8.92 us
  matrix products: 84.7 us -> 0 us
  other arithmetic: 83 us -> 0.08 us
  waiting for transfers between devices: 50.1 us -> 15 us
  Pallas kernels: 0 us -> 23.2 us
  starting transfers between devices: 28.8 us -> 11.5 us
  between operations: 14.3 us -> 0.68 us
  blocking collectives: 0 us -> 12.1 us
    gather x48 -> x0, local copies, waits for them, and re-layouts: 532 us -> none  [the longest x24 305 us: circulant(): return jnp.take(vectors, lookup, axis=-1)]
    dot_general x16 -> x0, matrix products: 84.7 us -> none  [the longest x8 52.5 us: one_class(): jnp.einsum('rtlk,rtmk->rlm', stacked, weight_circ, preferred_element_type...]
    select_n x16 -> x0, local copies, waits for them, and re-layouts: 64.8 us -> none  [the longest x8 64.1 us: one_class(): shifted = jnp.take(shifted_all, picks, axis=0)]
    select_n x27 -> x0, other arithmetic: 51.4 us -> none  [the longest x16 48.7 us: one_class(): shifted = jnp.take(shifted_all, picks, axis=0)]
    all_to_all x7 -> x0, waiting for transfers between devices: 45.1 us -> none  [the longest x1 13.6 us: per_device(): lax.all_to_all(outgoing, 'cls', split_axis=0, concat_axis=0, tiled=True)]
    broadcast_in_dim x16 -> x1, local copies, waits for them, and re-layouts: 36.8 us -> 0.01 us  [per_device(): weights = jnp.repeat(inv_noise.reshape(8, 8).T, 2, axis=0).reshape(1, HALF)]
    all_to_all x7 -> x0, starting transfers between devices: 28.8 us -> none  [the longest x1 7.25 us: per_device(): lax.all_to_all(moves_out, 'cls', split_axis=0, concat_axis=0, tiled=True)]
    pallas_call x0 -> x6, Pallas kernels: none -> 23.2 us  [the longest x1 14.5 us: per_device(): pl.pallas_call(lambda *a: score_kernel(nbit, *a), out_shape=(jax.ShapeDty...]
  transfers between devices with their start and end apart: 8 -> 8, of which waited for: 8 -> 6; matrix products, arithmetic and copies ran while one was open for 2% -> 2% of each run, Pallas kernels for 0% -> 1%
where the time goes in v1:
time: 71.8 us; the launch traced here: 71.4 us
  Pallas kernels  23.2 us (32%)
  waiting for transfers between devices  15 us (21%)
  blocking collectives  12.1 us (17%)
  starting transfers between devices  11.5 us (16%)
  local copies, waits for them, and re-layouts  8.92 us (12%)
    pallas_call x1, Pallas kernels, per_device(): pl.pallas_call(lambda *a: score_kernel(nbit, *a), out_shape=(jax.ShapeDty...  14.5 us
    ppermute x7, waiting for transfers between devices, swap(): return lax.ppermute(x, 'cls', [(i, i ^ bits) for i in range(holders)])  13.9 us
    all_to_all x1, blocking collectives, per_device(): lax.all_to_all(spread.reshape(holders, nblocks * 8, HALF), 'cls', split_a...  12.1 us
    ppermute x7, starting transfers between devices, swap(): return lax.ppermute(x, 'cls', [(i, i ^ bits) for i in range(holders)])  11.4 us
    unnamed x13, local copies, waits for them, and re-layouts  7.5 us
    pallas_call x1, Pallas kernels, per_device(): pl.pallas_call(lambda *a: back_kernel(holders, *a), out_shape=(jax.ShapeD...  5.17 us
  transfers between devices with their start and end apart: 8, of which 6 were waited for; matrix products, arithmetic and copies ran while one was open for 2% of the time, Pallas kernels for 1%

profile of v1, /device:TPU:0, one launch (start us, length us, event | category | flops | bytes accessed | tf_op | source)
XLA Modules:
  0.0 71.4 jit_solution(13733685617124840778)
XLA Ops:
  0.6 0.8 %copy.9.a_2_ = s32[4,3,2]{2,1,0:T(4,128)S(1)} copy(s32[4,3,2]{0,2,1:T(2,128)} %param.10) | data formatting | bytes 192 | tf_op args[3]
  1.4 0.0 copy-start.4
  1.4 0.9 %copy-done.4 = bf16[4,18432]{1,0:T(4,128)(2,1)S(1)} copy-done((bf16[4,18432]{1,0:T(4,128)(2,1)S(1)}, bf16[4,18432]{1,0:T(4,128)(2,1)}, u32[]{:S(2)}) %copy-start.4) | copy-done | bytes 147480
  2.3 0.0 copy-start.5
  2.3 0.7 copy-done.5
  3.0 1.1 %particle_turns.1 = bf16[304,256]{1,0:T(8,128)(2,1)S(1)} custom-call(bf16[4,18432]{1,0:T(4,128)(2,1)S(1)} %copy-done.4, s32[4,32]{1,0:T(4,128)S(1)} %copy-done.5, s32[4,3,2]{2,1,0:T(4,128)S(1)} %copy.9.a_2_), custom_call_target="tpu_custom_call" | custom-call | tf_op jit(solution)/shard_map/particle_turns/pallas_call | solution.py:362
  4.1 4.1 %collective-permute-start.3 = (bf16[304,256]{1,0:T(8,128)(2,1)S(1)}, bf16[304,256]{1,0:T(8,128)(2,1)S(1)}, u32[]{:S(2)}, u32[]{:S(2)}) collective-permute-start(bf16[304,256]{1,0:T(8,128)(2,1)S(1)} %particle_turns.1), channel_id=1, source_target_pairs={{0,8},{2,10},{4,12},{6,14},{8,0},{10,2},{12,4},{14,6},{1,9},{3,11}... | collective-permute-start | bytes 466952 | tf_op jit(solution)/shard_map/ppermute | solution.py:326
  8.2 1.6 %collective-permute-start.1 = (bf16[304,256]{1,0:T(8,128)(2,1)S(1)}, bf16[304,256]{1,0:T(8,128)(2,1)S(1)}, u32[]{:S(2)}, u32[]{:S(2)}) collective-permute-start(bf16[304,256]{1,0:T(8,128)(2,1)S(1)} %particle_turns.1), channel_id=1, source_target_pairs={{0,4},{2,6},{4,0},{6,2},{8,12},{10,14},{12,8},{14,10},{1,5},{3,7},... | collective-permute-start | bytes 466952 | tf_op jit(solution)/shard_map/ppermute | solution.py:326
  9.8 5.9 %collective-permute-done.3 = bf16[304,256]{1,0:T(8,128)(2,1)S(1)} collective-permute-done((bf16[304,256]{1,0:T(8,128)(2,1)S(1)}, bf16[304,256]{1,0:T(8,128)(2,1)S(1)}, u32[]{:S(2)}, u32[]{:S(2)}) %collective-permute-start.3) | collective-permute-done | bytes 155680 | tf_op jit(solution)/shard_map/ppermute | solution.py:326
  15.7 0.6 collective-permute-start.5
  16.3 1.5 %collective-permute-start = (bf16[304,256]{1,0:T(8,128)(2,1)S(1)}, bf16[304,256]{1,0:T(8,128)(2,1)S(1)}, u32[]{:S(2)}, u32[]{:S(2)}) collective-permute-start(bf16[304,256]{1,0:T(8,128)(2,1)S(1)} %particle_turns.1), channel_id=1, source_target_pairs={{0,2},{2,0},{4,6},{6,4},{8,10},{10,8},{12,14},{14,12},{1,3},{3,1},... | collective-permute-start | bytes 466952 | tf_op jit(solution)/shard_map/ppermute | solution.py:326
  17.8 0.7 %reshape.13 = f32[8,8]{1,0:T(8,128)S(1)} reshape(f32[64]{0:T(128)} %param.11) | data formatting | bytes 512 | tf_op jit(solution)/shard_map/reshape | solution.py:373
  18.5 0.1 copy.10
  18.6 0.1 reshape_reshape.3
  18.7 0.6 collective-permute-start.4
  19.3 0.0 collective-permute-done.1
  19.3 1.5 %collective-permute-start.2 = (bf16[304,256]{1,0:T(8,128)(2,1)S(1)}, bf16[304,256]{1,0:T(8,128)(2,1)S(1)}, u32[]{:S(2)}, u32[]{:S(2)}) collective-permute-start(bf16[304,256]{1,0:T(8,128)(2,1)S(1)} %collective-permute-done.1), channel_id=1, source_target_pairs={{0,2},{2,0},{4,6},{6,4},{8,10},{10,8},{12,14},{14,12},{1,3},{3,1},... | collective-permute-start | bytes 466952 | tf_op jit(solution)/shard_map/ppermute | solution.py:326
  20.8 0.1 collective-permute-done.5
  20.9 1.5 %collective-permute-start.6 = (bf16[304,256]{1,0:T(8,128)(2,1)S(1)}, bf16[304,256]{1,0:T(8,128)(2,1)S(1)}, u32[]{:S(2)}, u32[]{:S(2)}) collective-permute-start(bf16[304,256]{1,0:T(8,128)(2,1)S(1)} %collective-permute-done.5), channel_id=1, source_target_pairs={{0,2},{2,0},{4,6},{6,4},{8,10},{10,8},{12,14},{14,12},{1,3},{3,1},... | collective-permute-start | bytes 466952 | tf_op jit(solution)/shard_map/ppermute | solution.py:326
  22.4 0.0 copy-start.1
  22.4 1.0 %copy-done.1 = bf16[8,18432]{1,0:T(8,128)(2,1)S(1)} copy-done((bf16[8,18432]{1,0:T(8,128)(2,1)S(1)}, bf16[8,18432]{1,0:T(8,128)(2,1)}, u32[]{:S(2)}) %copy-start.1) | copy-done | bytes 294936
  23.4 0.5 reference_turns.1.a_11_
  24.0 0.1 pad_add_fusion.a_0_
  24.0 0.0 collective-permute-done
  24.0 2.4 %collective-permute-done.4 = bf16[304,256]{1,0:T(8,128)(2,1)S(1)} collective-permute-done((bf16[304,256]{1,0:T(8,128)(2,1)S(1)}, bf16[304,256]{1,0:T(8,128)(2,1)S(1)}, u32[]{:S(2)}, u32[]{:S(2)}) %collective-permute-start.4) | collective-permute-done | bytes 155680 | tf_op jit(solution)/shard_map/ppermute | solution.py:326
  26.4 3.3 %collective-permute-done.2 = bf16[304,256]{1,0:T(8,128)(2,1)S(1)} collective-permute-done((bf16[304,256]{1,0:T(8,128)(2,1)S(1)}, bf16[304,256]{1,0:T(8,128)(2,1)S(1)}, u32[]{:S(2)}, u32[]{:S(2)}) %collective-permute-start.2) | collective-permute-done | bytes 155680 | tf_op jit(solution)/shard_map/ppermute | solution.py:326
  29.8 2.2 %collective-permute-done.6 = bf16[304,256]{1,0:T(8,128)(2,1)S(1)} collective-permute-done((bf16[304,256]{1,0:T(8,128)(2,1)S(1)}, bf16[304,256]{1,0:T(8,128)(2,1)S(1)}, u32[]{:S(2)}, u32[]{:S(2)}) %collective-permute-start.6) | collective-permute-done | bytes 155680 | tf_op jit(solution)/shard_map/ppermute | solution.py:326
  31.9 0.0 copy-start.2
  31.9 0.9 %copy-done.2 = f32[288,128]{1,0:T(8,128)S(1)} copy-done((f32[288,128]{1,0:T(8,128)S(1)}, f32[288,128]{1,0:T(8,128)}, u32[]{:S(2)}) %copy-start.2) | copy-done | bytes 147480
  32.9 0.0 copy-start.3
  32.9 0.9 %copy-done.3 = f32[288,128]{1,0:T(8,128)S(1)} copy-done((f32[288,128]{1,0:T(8,128)S(1)}, f32[288,128]{1,0:T(8,128)}, u32[]{:S(2)}) %copy-start.3) | copy-done | bytes 147480
  33.8 14.5 %scores.1 = (bf16[1,36,256,256]{3,2,1,0:T(8,128)(2,1)}, f32[1,576,256]{2,1,0:T(8,128)S(1)}, f32[1,8,128]{2,1,0:T(8,128)S(1)}) custom-call(s32[2]{0:T(128)S(1)} %pad_add_fusion.a_0_, bf16[1,304,256]{2,1,0:T(8,128)(2,1)S(1)} %bitcast.15, bf16[1,304,256]{2,1,0:T(8,128)(2,1)S(1)} %bitcast.19, bf16[1,304,256]{2,1,0:T(8,128)(2,1)S(1)} %bitcast.17, ...), custom_call_target="tpu_custom_call" | custom-call | tf_op jit(solution)/shard_map/scores/pallas_call | solution.py:387
  48.3 0.7 %spread.1 = f32[8,1,8,128]{3,2,1,0:T(8,128)S(1)} custom-call(s32[2]{0:T(128)S(1)} %pad_add_fusion.a_0_, f32[1,8,128]{2,1,0:T(8,128)S(1)} %get-tuple-element.8.a_1_.a_2_), custom_call_target="tpu_custom_call" | custom-call | tf_op jit(solution)/shard_map/spread/pallas_call | solution.py:410
  49.0 12.1 %all_to_all.5 = f32[8,8,128]{2,1,0:T(8,128)S(1)} all-to-all(f32[8,8,128]{2,1,0:T(8,128)S(1)} %bitcast.24), channel_id=1, replica_groups=mesh['groups'=2,'cls'=8,'dom'=2] {'cls'}, dimensions={0} | all-to-all | bytes 65536 | tf_op jit(solution)/shard_map/all_to_all | solution.py:418
  61.1 0.0 copy-start
  61.1 2.3 %copy-done = bf16[1,36,256,256]{3,2,1,0:T(8,128)(2,1)S(1)} copy-done((bf16[1,36,256,256]{3,2,1,0:T(8,128)(2,1)S(1)}, bf16[1,36,256,256]{3,2,1,0:T(8,128)(2,1)}, u32[]{:S(2)}) %copy-start) | copy-done | bytes 4718616
  63.4 5.2 %class_sums.1 = (f32[576,128]{1,0:T(8,128)S(1)}, f32[576,128]{1,0:T(8,128)S(1)}, f32[8,128]{1,0:T(8,128)S(1)}) custom-call(s32[2]{0:T(128)S(1)} %pad_add_fusion.a_0_, f32[8,1,8,128]{3,2,1,0:T(8,128)S(1)} %bitcast.23, f32[1,8,128]{2,1,0:T(8,128)S(1)} %get-tuple-element.8.a_1_.a_2_, f32[1,576,256]{2,1,0:T(8,128)S(1)} %get-tuple-element.9.a_3_, ...), custom_call_target="tpu_custom_call" | custom-call | tf_op jit(solution)/shard_map/class_sums/pallas_call | solution.py:422
  68.6 0.1 collective-permute-start.7
  68.7 0.5 slice_bitcast_fusion
  69.2 1.1 %collective-permute-done.7.b_ref = f32[576,128]{1,0:T(8,128)S(1)} collective-permute-done((f32[576,128]{1,0:T(8,128)S(1)}, f32[576,128]{1,0:T(8,128)S(1)}, u32[]{:S(2)}, u32[]{:S(2)}) %collective-permute-start.7) | collective-permute-done | bytes 294944 | tf_op jit(solution)/shard_map/ppermute | solution.py:445
  70.2 1.2 %flat_rows.1 = f32[8,9216]{1,0:T(8,128)} custom-call(f32[576,128]{1,0:T(8,128)S(1)} %get-tuple-element.11.a_ref, f32[576,128]{1,0:T(8,128)S(1)} %collective-permute-done.7.b_ref), custom_call_target="tpu_custom_call" | custom-call | tf_op jit(solution)/shard_map/flat_rows/pallas_call | solution.py:446
  (2 shorter events, 0.0 us)
Async XLA Ops:
  1.4 0.9 %copy-start.4 = (bf16[4,18432]{1,0:T(4,128)(2,1)S(1)}, bf16[4,18432]{1,0:T(4,128)(2,1)}, u32[]{:S(2)}) copy-start(bf16[4,18432]{1,0:T(4,128)(2,1)} %a_0_.1) | copy-start | bytes 442372
  2.3 0.7 copy-start.5
  4.1 11.6 %collective-permute-start.3 = (bf16[304,256]{1,0:T(8,128)(2,1)S(1)}, bf16[304,256]{1,0:T(8,128)(2,1)S(1)}, u32[]{:S(2)}, u32[]{:S(2)}) collective-permute-start(bf16[304,256]{1,0:T(8,128)(2,1)S(1)} %particle_turns.1), channel_id=1, source_target_pairs={{0,8},{2,10},{4,12},{6,14},{8,0},{10,2},{12,4},{14,6},{1,9},{3,11}... | collective-permute-start | bytes 466952 | tf_op jit(solution)/shard_map/ppermute | solution.py:326
  8.2 11.1 %collective-permute-start.1 = (bf16[304,256]{1,0:T(8,128)(2,1)S(1)}, bf16[304,256]{1,0:T(8,128)(2,1)S(1)}, u32[]{:S(2)}, u32[]{:S(2)}) collective-permute-start(bf16[304,256]{1,0:T(8,128)(2,1)S(1)} %particle_turns.1), channel_id=1, source_target_pairs={{0,4},{2,6},{4,0},{6,2},{8,12},{10,14},{12,8},{14,10},{1,5},{3,7},... | collective-permute-start | bytes 466952 | tf_op jit(solution)/shard_map/ppermute | solution.py:326
  15.7 5.2 %collective-permute-start.5 = (bf16[304,256]{1,0:T(8,128)(2,1)S(1)}, bf16[304,256]{1,0:T(8,128)(2,1)S(1)}, u32[]{:S(2)}, u32[]{:S(2)}) collective-permute-start(bf16[304,256]{1,0:T(8,128)(2,1)S(1)} %collective-permute-done.3), channel_id=1, source_target_pairs={{0,4},{2,6},{4,0},{6,2},{8,12},{10,14},{12,8},{14,10},{1,5},{3,7},... | collective-permute-start | bytes 466952 | tf_op jit(solution)/shard_map/ppermute | solution.py:326
  16.3 7.8 %collective-permute-start = (bf16[304,256]{1,0:T(8,128)(2,1)S(1)}, bf16[304,256]{1,0:T(8,128)(2,1)S(1)}, u32[]{:S(2)}, u32[]{:S(2)}) collective-permute-start(bf16[304,256]{1,0:T(8,128)(2,1)S(1)} %particle_turns.1), channel_id=1, source_target_pairs={{0,2},{2,0},{4,6},{6,4},{8,10},{10,8},{12,14},{14,12},{1,3},{3,1},... | collective-permute-start | bytes 466952 | tf_op jit(solution)/shard_map/ppermute | solution.py:326
  18.7 7.8 %collective-permute-start.4 = (bf16[304,256]{1,0:T(8,128)(2,1)S(1)}, bf16[304,256]{1,0:T(8,128)(2,1)S(1)}, u32[]{:S(2)}, u32[]{:S(2)}) collective-permute-start(bf16[304,256]{1,0:T(8,128)(2,1)S(1)} %collective-permute-done.3), channel_id=1, source_target_pairs={{0,2},{2,0},{4,6},{6,4},{8,10},{10,8},{12,14},{14,12},{1,3},{3,1},... | collective-permute-start | bytes 466952 | tf_op jit(solution)/shard_map/ppermute | solution.py:326
  19.3 10.5 %collective-permute-start.2 = (bf16[304,256]{1,0:T(8,128)(2,1)S(1)}, bf16[304,256]{1,0:T(8,128)(2,1)S(1)}, u32[]{:S(2)}, u32[]{:S(2)}) collective-permute-start(bf16[304,256]{1,0:T(8,128)(2,1)S(1)} %collective-permute-done.1), channel_id=1, source_target_pairs={{0,2},{2,0},{4,6},{6,4},{8,10},{10,8},{12,14},{14,12},{1,3},{3,1},... | collective-permute-start | bytes 466952 | tf_op jit(solution)/shard_map/ppermute | solution.py:326
  20.9 11.1 %collective-permute-start.6 = (bf16[304,256]{1,0:T(8,128)(2,1)S(1)}, bf16[304,256]{1,0:T(8,128)(2,1)S(1)}, u32[]{:S(2)}, u32[]{:S(2)}) collective-permute-start(bf16[304,256]{1,0:T(8,128)(2,1)S(1)} %collective-permute-done.5), channel_id=1, source_target_pairs={{0,2},{2,0},{4,6},{6,4},{8,10},{10,8},{12,14},{14,12},{1,3},{3,1},... | collective-permute-start | bytes 466952 | tf_op jit(solution)/shard_map/ppermute | solution.py:326
  22.4 1.0 %copy-start.1 = (bf16[8,18432]{1,0:T(8,128)(2,1)S(1)}, bf16[8,18432]{1,0:T(8,128)(2,1)}, u32[]{:S(2)}) copy-start(bf16[8,18432]{1,0:T(8,128)(2,1)} %x_ref.1) | copy-start | bytes 884740
  31.9 0.9 %copy-start.2 = (f32[288,128]{1,0:T(8,128)S(1)}, f32[288,128]{1,0:T(8,128)}, u32[]{:S(2)}) copy-start(f32[288,128]{1,0:T(8,128)} %constant.13.clone.a_10_) | copy-start | bytes 442372
  32.9 0.9 %copy-start.3 = (f32[288,128]{1,0:T(8,128)S(1)}, f32[288,128]{1,0:T(8,128)}, u32[]{:S(2)}) copy-start(f32[288,128]{1,0:T(8,128)} %constant.12.clone.a_9_) | copy-start | bytes 442372
  61.1 2.3 %copy-start = (bf16[1,36,256,256]{3,2,1,0:T(8,128)(2,1)S(1)}, bf16[1,36,256,256]{3,2,1,0:T(8,128)(2,1)}, u32[]{:S(2)}) copy-start(bf16[1,36,256,256]{3,2,1,0:T(8,128)(2,1)} %get-tuple-element.10.a_4_) | copy-start | bytes 14155780
  68.6 1.6 %collective-permute-start.7 = (f32[576,128]{1,0:T(8,128)S(1)}, f32[576,128]{1,0:T(8,128)S(1)}, u32[]{:S(2)}, u32[]{:S(2)}) collective-permute-start(f32[576,128]{1,0:T(8,128)S(1)} %get-tuple-element.12), channel_id=1, source_target_pairs={{0,1},{1,0},{2,3},{3,2},{4,5},{5,4},{6,7},{7,6},{8,9},{9,8},{10,11... | collective-permute-start | bytes 884744 | tf_op jit(solution)/shard_map/ppermute | solution.py:445

commit v2 on v1

v2 whole, which is shorter than its diff:
```python
import math

import jax
import jax.numpy as jnp
import numpy as np
from jax import lax
from jax.experimental import pallas as pl
from jax.experimental.pallas import tpu as pltpu
from jax.sharding import PartitionSpec as P

ROT = 72
CYCLES = 64
CLASS_LIST_SIZE = 32
BOX = 256
TRANS = 3
PER_DEV = 4
CLS = 8
SLOTS = 4
LANES = 256
HALF = 128
GROUP = 16 * ROT
ROWS = ROT * PER_DEV
REF_ROWS = ROT * CLS
STEPS = ROT // 4
HALF_TURN = ROWS // 2
CODED = 3 * 16
LOWEST = -1e30
VMEM = 20 * 1024 * 1024

F32 = jnp.float32
BF16 = jnp.bfloat16


def frequency_rows():
    row = lax.broadcasted_iota(jnp.int32, (HALF_TURN, HALF), 0)
    lane = lax.broadcasted_iota(jnp.int32, (HALF_TURN, HALF), 1)
    line = (lane % 8) * 16 + lane // 8
    radius = (line // 2 + 1).astype(F32) * (1.0 / BOX)
    angle = (2 * (row // PER_DEV) + line % 2).astype(F32) * (0.5 / ROT)
    c, s = cos_sin_turns(angle)
    return radius * c, radius * s


def half_turn_polynomials():
    t = np.cos(np.pi * (np.arange(400) + 0.5) / 400)
    z = (t + 1) / 8
    v = np.sqrt(z)
    sin_fit = np.polynomial.chebyshev.Chebyshev.fit(z, np.sin(np.pi * v) / v, 4, domain=[0, 0.25])
    cos_fit = np.polynomial.chebyshev.Chebyshev.fit(z, np.cos(np.pi * v), 5, domain=[0, 0.25])
    to_list = lambda f: [float(c) for c in f.convert(kind=np.polynomial.Polynomial).coef]
    return to_list(sin_fit), to_list(cos_fit)


SIN_COEF, COS_COEF = half_turn_polynomials()


def horner(coef, z):
    total = jnp.full_like(z, coef[-1])
    for c in coef[-2::-1]:
        total = total * z + c
    return total


def cos_sin_turns(u):
    v = u - jnp.round(u)
    z = v * v
    s = v * horner(SIN_COEF, z)
    c = horner(COS_COEF, z)
    s2 = s + s
    return 1.0 - s2 * s, s2 * c


def turn_major(x_ref, grid_ref, lines_ref, out_ref, count):
    for g in range(16):
        for tile in range(GROUP // HALF):
            start = g * GROUP + tile * HALF
            grid_ref[tile, pl.ds(g, count, stride=16), :] = x_ref[:, start : start + HALF].astype(F32)
    for h in range(16):
        tile, shift = divmod(ROT * h, HALF)
        if shift + ROT <= HALF:
            part = grid_ref[tile]
            if shift:
                part = pltpu.roll(part, HALF - shift, 1)
        else:
            part = jnp.concatenate([grid_ref[tile], grid_ref[tile + 1]], axis=1)
            part = pltpu.roll(part, LANES - shift, 1)[:, :HALF]
        lines_ref[:, :, h] = part.reshape(count, 2, 8, HALF)
    for p in range(count):
        for half in range(2):
            turns = lines_ref[p, half].reshape(HALF, HALF).T
            out_ref[half, pl.ds(p, ROT, stride=count), :] = turns[:ROT]


def particle_kernel(
    nbit, x_any, list_any, move_any, out_ref, x_ref, list_ref, move_ref, grid_ref, lines_ref, turns_ref, sems
):
    pairs = ((x_any, x_ref), (list_any, list_ref), (move_any, move_ref))
    copies = [pltpu.make_async_copy(a, b, sems.at[n]) for n, (a, b) in enumerate(pairs)]
    for copy in copies:
        copy.start()
    for copy in copies:
        copy.wait()
    turn_major(x_ref, grid_ref, lines_ref, turns_ref, PER_DEV)
    out_ref[:ROWS] = jnp.concatenate([turns_ref[0], turns_ref[1]], axis=1).astype(BF16)
    lists = list_ref[...]
    lane = lax.broadcasted_iota(jnp.int32, (PER_DEV, LANES), 1)
    parts = []
    for b in range(nbit):
        named = jnp.zeros((PER_DEV, LANES), F32)
        for j in range(CLASS_LIST_SIZE):
            named = jnp.where(lists[:, j : j + 1] == lane + b * LANES, 1.0, named)
        parts += [named, named]
    row = lax.broadcasted_iota(jnp.int32, (8, LANES), 0) % PER_DEV
    lane = lax.broadcasted_iota(jnp.int32, (8, LANES), 1)
    moves = jnp.zeros((8, LANES), F32)
    for p in range(PER_DEV):
        for t in range(TRANS):
            for a in range(2):
                here = (row == p) & (lane == 8 * a + t)
                moves = jnp.where(here, move_ref[t, a, p].astype(F32), moves)
    parts.append(moves)
    if nbit % 2 == 0:
        parts.append(jnp.zeros((8, LANES), F32))
    out_ref[ROWS:] = jnp.concatenate(parts, axis=0).astype(BF16)


def reference_kernel(x_ref, w_ref, out_ref, *rest):
    freq_refs, (grid_ref, lines_ref, turns_ref) = rest[:-3], rest[-3:]
    turn_major(x_ref, grid_ref, lines_ref, turns_ref, CLS)
    scaled = (jnp.concatenate([turns_ref[0], turns_ref[1]], axis=1) * w_ref[...]).astype(BF16)
    out_ref[:REF_ROWS] = scaled
    out_ref[REF_ROWS:] = scaled
    for ref, f in zip(freq_refs, frequency_rows()):
        ref[...] = f


def shift_kernel(nbit, block_ref, fx_ref, fy_ref, x_ref, bits_ref):
    first = ROWS + 16 * (nbit // 2)
    m = block_ref[0, first : first + 16].astype(F32)[8 * (nbit % 2) : 8 * (nbit % 2) + 8]
    m = jnp.concatenate([m, m], axis=0)
    moves = [
        (jnp.broadcast_to(m[:, t : t + 1], (16, HALF)), jnp.broadcast_to(m[:, 8 + t : 9 + t], (16, HALF)))
        for t in range(TRANS)
    ]
    bits_ref[0] = block_ref[0, ROWS : ROWS + bits_ref.shape[1]]

    def step(q, carry):
        rows = pl.ds(pl.multiple_of(q * 16, 16), 16)
        later = pl.ds(pl.multiple_of(q * 16, 16) + HALF_TURN, 16)
        fx = fx_ref[rows, :]
        fy = fy_ref[rows, :]
        near = block_ref[0, rows, :].astype(F32)
        far = block_ref[0, later, :].astype(F32)
        for t in range(TRANS):
            dx, dy = moves[t]
            c, s = cos_sin_turns(fx * dx + fy * dy)
            a, b = near[:, :HALF], near[:, HALF:]
            x_ref[0, q, t * 16 : t * 16 + 16, :HALF] = (a * c + b * s).astype(BF16)
            x_ref[0, q, t * 16 : t * 16 + 16, HALF:] = (b * c - a * s).astype(BF16)
            a, b = far[:, :HALF], far[:, HALF:]
            x_ref[0, q + STEPS // 2, t * 16 : t * 16 + 16, :HALF] = (a * c - b * s).astype(BF16)
            x_ref[0, q + STEPS // 2, t * 16 : t * 16 + 16, HALF:] = (b * c + a * s).astype(BF16)
        return carry

    lax.fori_loop(0, STEPS // 2, step, 0, unroll=3)


def xor_lanes(x, step):
    lane = lax.broadcasted_iota(jnp.int32, x.shape, x.ndim - 1)
    width = x.shape[-1]
    down = pltpu.roll(x, width - step, x.ndim - 1)
    up = pltpu.roll(x, step, x.ndim - 1)
    return jnp.where((lane // step) % 2 == 0, down, up)


def xor_slots(x, bits):
    if bits & 1:
        x = xor_lanes(x, 64)
    if bits & 2:
        x = xor_lanes(x, 128)
    return x


def images_of(x_refs, q):
    empty = jnp.zeros((16, LANES), BF16)
    return jnp.concatenate([v for x in x_refs for v in (x[0, q], empty)], axis=0)


def score_kernel(nbit, me_ref, *refs):
    x_refs = refs[:SLOTS]
    bit_refs = refs[SLOTS : 2 * SLOTS]
    own_ref, other_ref, e_ref, stat_ref, acc_ref = refs[2 * SLOTS :]
    acc_ref[...] = jnp.zeros_like(acc_ref)

    def step(g, carry):
        for side, ref in enumerate((own_ref, other_ref)):
            total = acc_ref[side, :REF_ROWS]
            for r in range(3):
                q = 3 * g + r
                turned = ref[pl.ds(pl.multiple_of(q * 32, 32), REF_ROWS), :]
                total += lax.dot_general(
                    turned, images_of(x_refs, q), (((1,), (1,)), ((), ())), preferred_element_type=F32
                )
            acc_ref[side, :REF_ROWS] = total
        return carry

    lax.fori_loop(0, STEPS // 3, step, 0)

    src = lax.broadcasted_iota(jnp.int32, (SLOTS * 16, LANES), 0)
    dst = lax.broadcasted_iota(jnp.int32, (SLOTS * 16, LANES), 1)
    ok = (src == dst // 64 * 16 + dst % 4) & (dst % 64 < 48) & (dst % 16 < 4)
    place = ok.astype(F32).astype(BF16)
    lane = lax.broadcasted_iota(jnp.int32, (CLS, LANES), 1)
    row = lax.broadcasted_iota(jnp.int32, (CLS, LANES), 0)
    top = jnp.full((CLS, LANES), LOWEST, F32)
    masks = []
    for side in range(2):
        chip = me_ref[0] ^ side
        named = jnp.zeros((CLS, SLOTS * 16), F32)
        for b in range(nbit):
            pick = (lane + b * LANES == chip * CLS + row).astype(F32).astype(BF16)
            first = 16 * (b // 2)
            bits = jnp.concatenate([r[0, first : first + 16] for r in bit_refs], axis=0)
            if b % 2:
                bits = jnp.concatenate(
                    [v for s in range(SLOTS) for v in (bits[s * 16 + 8 : s * 16 + 16], bits[s * 16 : s * 16 + 8])],
                    axis=0,
                )
            named += lax.dot_general(pick, bits, (((1,), (1,)), ((), ())), preferred_element_type=F32)
        mask = jnp.dot(named.astype(BF16), place, preferred_element_type=F32) > 0.5
        masks.append(mask)
        acc_ref[side, REF_ROWS:] = acc_ref[side, :32]

        def body_max(i, top, side=side, mask=mask):
            at = lambda d: acc_ref[side, pl.ds(pl.multiple_of((i + d) * 8, 8), 8), :]
            s = at(0)
            for d in range(1, 4):
                s += pltpu.roll(at(d), LANES - 4 * d, 1)
            s = jnp.where(mask, s, LOWEST)
            e_ref[0, side, pl.ds(pl.multiple_of(i * 8, 8), 8), :] = s
            return jnp.maximum(top, s)

        top = lax.fori_loop(0, ROT, body_max, top, unroll=8)
    top = jnp.broadcast_to(jnp.max(top, axis=0, keepdims=True), (CLS, LANES))
    top = jnp.maximum(top, xor_lanes(top, 16))
    top = jnp.maximum(top, xor_lanes(top, 32))
    total = jnp.zeros((CLS, LANES), F32)
    for side in range(2):

        def body_exp(i, total, side=side):
            rows = pl.ds(pl.multiple_of(i * 8, 8), 8)
            e = jnp.where(masks[side], jnp.exp(e_ref[0, side, rows, :] - top), 0.0)
            e_ref[0, side, rows, :] = e
            return total + e

        total = lax.fori_loop(0, ROT, body_exp, total, unroll=8)
    total = jnp.broadcast_to(jnp.sum(total, axis=0, keepdims=True), (CLS, LANES))
    total = total + xor_lanes(total, 16)
    total = total + xor_lanes(total, 32)
    stat_ref[0] = jnp.where(row == 0, top, total)


def back_kernel(side, nblocks, me_ref, *refs):
    got_refs = refs[:SLOTS]
    stat_ref, e_ref = refs[SLOTS : SLOTS + 2]
    x_refs = refs[SLOTS + 2 : 2 * SLOTS + 2]
    keep_ref, send_ref, *log_ref = refs[2 * SLOTS + 2 : -2]
    w_ref, acc_ref = refs[-2:]
    n = pl.program_id(0) if nblocks > 1 else 0
    stats = [
        xor_slots(got_refs[low][high, n ^ high], low) for high in range(nblocks) for low in range(SLOTS)
    ]
    spread = lambda x, r: jnp.broadcast_to(x[r : r + 1], (8, LANES))
    tops = [spread(x, 0) for x in stats]
    best = tops[0]
    for top in tops[1:]:
        best = jnp.maximum(best, top)
    evidence = jnp.zeros((8, LANES), F32)
    for top, x in zip(tops, stats):
        evidence = evidence + spread(x, 1) * jnp.exp(top - best)
    lane = lax.broadcasted_iota(jnp.int32, (8, LANES), 1)
    live = (lane % 64 < 48) & (lane % 16 < 4)
    factor = jnp.where(live, jnp.exp(spread(stat_ref[0], 0) - best) / evidence, 0.0)

    def start():
        acc_ref[...] = jnp.zeros_like(acc_ref)
        if log_ref:
            log_ref[0][...] = best + jnp.log(evidence)

    if nblocks > 1:
        pl.when(n == 0)(start)
    else:
        start()

    def weights(i):
        i = i % ROT
        return e_ref[0, side, i * 8 : i * 8 + 8, :] * factor

    window = [weights(i) for i in (-3, -2, -1)]
    for i in range(0, ROT, 2):
        rows = []
        for d in range(2):
            now = weights(i + d)
            a, b, c = window
            rows.append(now + pltpu.roll(c, 4, 1) + pltpu.roll(b, 8, 1) + pltpu.roll(a, 12, 1))
            window = [b, c, now]
        pair = jnp.concatenate(rows, axis=0).astype(BF16)
        w_ref[i * 8 : i * 8 + 16, :] = pair
        w_ref[REF_ROWS + i * 8 : REF_ROWS + i * 8 + 16, :] = pair

    def step(g, carry):
        total = acc_ref[...]
        for r in range(3):
            q = 3 * g + r
            turned = w_ref[pl.ds(pl.multiple_of((STEPS - q) * 32, 32), REF_ROWS), :]
            total += jnp.dot(turned, images_of(x_refs, q), preferred_element_type=F32)
        acc_ref[...] = total
        return carry

    lax.fori_loop(0, STEPS // 3, step, 0)

    @pl.when((n == nblocks - 1) & (me_ref[1] == 0))
    def _():
        keep_ref[...] = acc_ref[:, :HALF]
        send_ref[...] = acc_ref[:, HALF:]

    @pl.when((n == nblocks - 1) & (me_ref[1] == 1))
    def _():
        keep_ref[...] = acc_ref[:, HALF:]
        send_ref[...] = acc_ref[:, :HALF]


def flat_kernel(a_ref, b_ref, c_ref, out_ref, sum_ref, lines_ref, grid_ref):
    sum_ref[:REF_ROWS] = a_ref[...] + b_ref[...] + c_ref[...].astype(F32)
    lane = lax.broadcasted_iota(jnp.int32, (CLS * 8, HALF), 1)
    for c in range(CLS):
        turns = sum_ref[pl.ds(c, HALF, stride=CLS), :]
        lines_ref[c] = turns.T
    for tile in range(GROUP // HALF):
        made = None
        for h in range(16):
            start = ROT * h - tile * HALF
            if start >= HALF or start + ROT <= 0:
                continue
            part = lines_ref[:, h * 8 : h * 8 + 8, :].reshape(CLS * 8, HALF)
            if start % HALF:
                part = pltpu.roll(part, start % HALF, 1)
            made = part if made is None else jnp.where(lane >= start, part, made)
        grid_ref[tile] = made
        for g in range(8):
            start = g * GROUP + tile * HALF
            out_ref[:, start : start + HALF] = grid_ref[tile, pl.ds(g, CLS, stride=8), :]


def swap(x, axis, bits):
    return lax.ppermute(x, axis, [(i, i ^ bits) for i in range(lax.axis_size(axis))])


def gather_slots(block, relay):
    if lax.axis_size("cls") == 2 * SLOTS:
        r2 = swap(block, "cls", 4)
        r1 = swap(block, "cls", 2)
        r3 = swap(r2, "cls", 2) if relay else swap(block, "cls", 6)
        return [x[None] for x in (block, r1, r2, r3)]
    slots = block[None]
    bits = 2
    while bits < lax.axis_size("cls"):
        slots = jnp.concatenate([slots, swap(slots, "cls", bits)], axis=0)
        bits *= 2
    return [slots[s::SLOTS] for s in range(SLOTS)]


def call(name, body, nblocks, inputs, outputs, scratch):
    def spec(shape, kind):
        if kind == "scalar":
            return pl.BlockSpec(memory_space=pltpu.SMEM)
        if kind == "any":
            return pl.BlockSpec(memory_space=pl.ANY)
        if nblocks == 1:
            return pl.BlockSpec(memory_space=pltpu.VMEM)
        rest = (0,) * (len(shape) - 1)
        if kind == "block":
            return pl.BlockSpec((1,) + shape[1:], lambda n: (n,) + rest)
        return pl.BlockSpec(shape, lambda n: (0,) + rest)

    grid = {"grid": (nblocks,)} if nblocks > 1 else {}
    return pl.pallas_call(
        body,
        out_shape=tuple(jax.ShapeDtypeStruct(shape, dtype) for shape, dtype, _ in outputs),
        in_specs=[spec(x.shape, kind) for x, kind in inputs],
        out_specs=tuple(spec(shape, kind) for shape, _, kind in outputs),
        scratch_shapes=scratch,
        compiler_params=pltpu.CompilerParams(vmem_limit_bytes=VMEM),
        name=name,
        **grid,
    )(*[x for x, _ in inputs])


def per_device(particles, references, class_lists, offsets, inv_noise):
    holders = lax.axis_size("cls")
    nblocks = holders // 2 // SLOTS
    nbit = -(-holders * CLS // LANES)
    extra = -(-(8 * nbit + 8) // 16) * 16
    rows = ROWS + extra
    me = jnp.stack([lax.axis_index("cls"), lax.axis_index("dom")]).astype(jnp.int32)

    def scratch(count):
        return [
            pltpu.VMEM((GROUP // HALF, count * 16, HALF), F32),
            pltpu.VMEM((count, 2, 16, 8, HALF), F32),
            pltpu.VMEM((2, ROT * count, HALF), F32),
        ]

    moves = jnp.transpose(offsets, (1, 2, 0))
    (block,) = call(
        "particle_turns",
        lambda *a: particle_kernel(nbit, *a),
        1,
        [(particles, "any"), (class_lists, "any"), (moves, "any")],
        [((rows, LANES), BF16, "all")],
        [
            pltpu.VMEM(particles.shape, BF16),
            pltpu.VMEM(class_lists.shape, jnp.int32),
            pltpu.SMEM(moves.shape, jnp.int32),
        ]
        + scratch(PER_DEV)
        + [pltpu.SemaphoreType.DMA((3,))],
    )
    slots = gather_slots(block, True)
    far_references = swap(references, "cls", 1)

    weights = jnp.repeat(inv_noise.reshape(8, 8).T, 2, axis=0).reshape(1, HALF)
    weights = jnp.concatenate([weights, weights], axis=1)
    turned = ((2 * REF_ROWS, LANES), BF16, "all")
    freq = ((HALF_TURN, HALF), F32, "all")
    own_refs, fx, fy = call(
        "own_references", reference_kernel, 1, [(references, "all"), (weights, "all")], [turned, freq, freq], scratch(CLS)
    )
    (far_refs,) = call(
        "far_references", reference_kernel, 1, [(far_references, "all"), (weights, "all")], [turned], scratch(CLS)
    )

    bit_rows = 16 * -(-nbit // 2)
    images, bits = [], []
    for slot in slots:
        x, b = call(
            "shifted",
            lambda *a: shift_kernel(nbit, *a),
            nblocks,
            [(slot, "block"), (fx, "all"), (fy, "all")],
            [((nblocks, STEPS, CODED, LANES), BF16, "block"), ((nblocks, bit_rows, LANES), BF16, "block")],
            [],
        )
        images.append(x)
        bits.append(b)

    expo, stat = call(
        "scores",
        lambda *a: score_kernel(nbit, *a),
        nblocks,
        [(me, "scalar")] + [(x, "block") for x in images + bits] + [(own_refs, "all"), (far_refs, "all")],
        [((nblocks, 2, REF_ROWS, LANES), F32, "block"), ((nblocks, 8, LANES), F32, "block")],
        [pltpu.VMEM((2, REF_ROWS + 32, LANES), F32)],
    )
    got = gather_slots(stat, False)

    def back(side):
        half = ((REF_ROWS, HALF), F32, "all")
        return call(
            "far_sums" if side else "own_sums",
            lambda *a: back_kernel(side, nblocks, *a),
            nblocks,
            [(me, "scalar")] + [(g, "all") for g in got] + [(stat, "block"), (expo, "block")] + [(x, "block") for x in images],
            [half, half] + [((8, LANES), F32, "all")] * side,
            [pltpu.VMEM((2 * REF_ROWS, LANES), BF16), pltpu.VMEM((REF_ROWS, LANES), F32)],
        )

    far_keep, far_send, logs = back(1)
    far_got = swap(far_send, "dom", 1)
    keep, send = back(0)
    own_got = swap(send, "dom", 1)
    far_sum = swap((far_keep + far_got).astype(BF16), "cls", 1)
    (sums,) = call(
        "flat_rows",
        flat_kernel,
        1,
        [(keep, "all"), (own_got, "all"), (far_sum, "all")],
        [((CLS, GROUP * 8), F32, "all")],
        [
            pltpu.VMEM((HALF * CLS, HALF), F32),
            pltpu.VMEM((CLS, HALF, HALF), F32),
            pltpu.VMEM((GROUP // HALF, CLS * 8, HALF), F32),
        ],
    )
    return sums, logs[0, :PER_DEV]


def solution(mesh):
    placed = (
        P(("groups", "cls", "dom"), None),
        P(("groups", "cls"), None),
        P(("groups", "cls", "dom"), None),
        P(("groups", "cls", "dom"), None, None),
        P(),
    )
    return jax.shard_map(
        per_device,
        mesh=mesh,
        in_specs=placed,
        out_specs=(P(("groups", "cls"), "dom"), P(("groups", "cls", "dom"))),
        check_vma=False,
    )
```

time: 71.8 us -> 53.9 us (0.75)
  blocking collectives: 12.1 us -> 0 us
  local copies, waits for them, and re-layouts: 8.92 us -> 4.66 us
  starting transfers between devices: 11.5 us -> 14.7 us
  waiting for transfers between devices: 15 us -> 12 us
  Pallas kernels: 23.2 us -> 21.4 us
    all_to_all x1 -> x0, blocking collectives: 12.1 us -> none  [per_device(): lax.all_to_all(spread.reshape(holders, nblocks * 8, HALF), 'cls', split_a...]
    unnamed x13 -> x9, local copies, waits for them, and re-layouts: 7.5 us -> 3.23 us
    ppermute x8 -> x10, starting transfers between devices: 11.5 us -> 14.7 us  [swap(): lax.ppermute(x, axis, [(i, i ^ bits) for i in range(lax.axis_size(axis))])]
    ppermute x8 -> x10, waiting for transfers between devices: 15 us -> 12 us  [swap(): lax.ppermute(x, axis, [(i, i ^ bits) for i in range(lax.axis_size(axis))])]
    pallas_call x6 -> x11, Pallas kernels: 23.2 us -> 21.4 us  [call(): pl.pallas_call(body, out_shape=tuple((jax.ShapeDtypeStruct(shape, dtype)...]
  transfers between devices with their start and end apart: 8 -> 10, of which waited for: 6 -> 4; matrix products, arithmetic and copies ran while one was open for 2% -> 3% of each run, Pallas kernels for 1% -> 11%
where the time goes in v2:
time: 53.9 us; the launch traced here: 53.7 us
  Pallas kernels  21.4 us (40%)
  starting transfers between devices  14.7 us (27%)
  waiting for transfers between devices  12 us (22%)
  local copies, waits for them, and re-layouts  4.66 us (9%)
  between operations  0.76 us (1%)
    pallas_call x11, Pallas kernels, call(): pl.pallas_call(body, out_shape=tuple((jax.ShapeDtypeStruct(shape, dtype)...  21.4 us
    ppermute x10, starting transfers between devices, swap(): lax.ppermute(x, axis, [(i, i ^ bits) for i in range(lax.axis_size(axis))])  14.7 us
    ppermute x10, waiting for transfers between devices, swap(): lax.ppermute(x, axis, [(i, i ^ bits) for i in range(lax.axis_size(axis))])  12 us
    unnamed x9, local copies, waits for them, and re-layouts  3.23 us
  transfers between devices with their start and end apart: 10, of which 4 were waited for; matrix products, arithmetic and copies ran while one was open for 3% of the time, Pallas kernels for 11%

profile of v2, /device:TPU:0, one launch (start us, length us, event | category | flops | bytes accessed | tf_op | source)
XLA Modules:
  0.0 53.7 jit_solution(12698525679048362103)
XLA Ops:
  0.6 0.0 copy-start.1
  0.6 0.9 %copy-done.1 = bf16[4,18432]{1,0:T(4,128)(2,1)S(1)} copy-done((bf16[4,18432]{1,0:T(4,128)(2,1)S(1)}, bf16[4,18432]{1,0:T(4,128)(2,1)}, u32[]{:S(2)}) %copy-start.1) | copy-done | bytes 147480
  1.5 0.0 copy-start.2
  1.5 0.7 %copy-done.2 = s32[4,3,2]{0,2,1:T(2,128)S(1)} copy-done((s32[4,3,2]{0,2,1:T(2,128)S(1)}, s32[4,3,2]{0,2,1:T(2,128)}, u32[]{:S(2)}) %copy-start.2) | copy-done | bytes 120
  2.2 0.0 copy-start.3
  2.2 0.7 %copy-done.3 = s32[4,32]{1,0:T(4,128)S(1)} copy-done((s32[4,32]{1,0:T(4,128)S(1)}, s32[4,32]{1,0:T(4,128)}, u32[]{:S(2)}) %copy-start.3) | copy-done | bytes 536
  2.9 1.2 %particle_turns.1 = bf16[304,256]{1,0:T(8,128)(2,1)S(1)} custom-call(bf16[4,18432]{1,0:T(4,128)(2,1)S(1)} %copy-done.1, s32[4,32]{1,0:T(4,128)S(1)} %copy-done.3, s32[3,2,4]{2,1,0:T(2,128)S(1)} %bitcast.26), custom_call_target="tpu_custom_call" | custom-call | tf_op jit(solution)/shard_map/particle_turns/pallas_call | solution.py:387
  4.1 4.1 %collective-permute-start.1 = (bf16[304,256]{1,0:T(8,128)(2,1)S(1)}, bf16[304,256]{1,0:T(8,128)(2,1)S(1)}, u32[]{:S(2)}, u32[]{:S(2)}) collective-permute-start(bf16[304,256]{1,0:T(8,128)(2,1)S(1)} %particle_turns.1), channel_id=1, source_target_pairs={{0,8},{2,10},{4,12},{6,14},{8,0},{10,2},{12,4},{14,6},{1,9},{3,11}... | collective-permute-start | bytes 466952 | tf_op jit(solution)/shard_map/ppermute | solution.py:356
  8.2 1.6 %collective-permute-start = (bf16[304,256]{1,0:T(8,128)(2,1)S(1)}, bf16[304,256]{1,0:T(8,128)(2,1)S(1)}, u32[]{:S(2)}, u32[]{:S(2)}) collective-permute-start(bf16[304,256]{1,0:T(8,128)(2,1)S(1)} %particle_turns.1), channel_id=1, source_target_pairs={{0,4},{2,6},{4,0},{6,2},{8,12},{10,14},{12,8},{14,10},{1,5},{3,7},... | collective-permute-start | bytes 466952 | tf_op jit(solution)/shard_map/ppermute | solution.py:356
  9.8 1.5 %collective-permute-start.3 = (bf16[8,18432]{1,0:T(8,128)(2,1)}, bf16[8,18432]{1,0:T(8,128)(2,1)S(1)}, u32[]{:S(2)}, u32[]{:S(2)}) collective-permute-start(bf16[8,18432]{1,0:T(8,128)(2,1)} %x_ref.1), channel_id=1, source_target_pairs={{0,2},{2,0},{4,6},{6,4},{8,10},{10,8},{12,14},{14,12},{1,3},{3,1},... | collective-permute-start | bytes 884744 | tf_op jit(solution)/shard_map/ppermute | solution.py:356
  11.3 0.7 %reshape.7 = f32[8,8]{1,0:T(8,128)S(1)} reshape(f32[64]{0:T(128)} %param.9) | data formatting | bytes 512 | tf_op jit(solution)/shard_map/reshape | solution.py:432
  12.0 0.1 copy.7
  12.1 0.1 reshape_reshape.3
  12.2 3.5 %collective-permute-done.1 = bf16[304,256]{1,0:T(8,128)(2,1)S(1)} collective-permute-done((bf16[304,256]{1,0:T(8,128)(2,1)S(1)}, bf16[304,256]{1,0:T(8,128)(2,1)S(1)}, u32[]{:S(2)}, u32[]{:S(2)}) %collective-permute-start.1) | collective-permute-done | bytes 155680 | tf_op jit(solution)/shard_map/ppermute | solution.py:356
  15.7 0.6 %collective-permute-start.2 = (bf16[304,256]{1,0:T(8,128)(2,1)S(1)}, bf16[304,256]{1,0:T(8,128)(2,1)S(1)}, u32[]{:S(2)}, u32[]{:S(2)}) collective-permute-start(bf16[304,256]{1,0:T(8,128)(2,1)S(1)} %collective-permute-done.1), channel_id=1, source_target_pairs={{0,4},{2,6},{4,0},{6,2},{8,12},{10,14},{12,8},{14,10},{1,5},{3,7},... | collective-permute-start | bytes 466952 | tf_op jit(solution)/shard_map/ppermute | solution.py:356
  16.3 0.0 copy-start
  16.3 1.0 %copy-done = bf16[8,18432]{1,0:T(8,128)(2,1)S(1)} copy-done((bf16[8,18432]{1,0:T(8,128)(2,1)S(1)}, bf16[8,18432]{1,0:T(8,128)(2,1)}, u32[]{:S(2)}) %copy-start) | copy-done | bytes 294936
  17.2 0.6 %own_references.1 = (bf16[1152,256]{1,0:T(8,128)(2,1)S(1)}, f32[144,128]{1,0:T(8,128)S(1)}, f32[144,128]{1,0:T(8,128)S(1)}) custom-call(bf16[8,18432]{1,0:T(8,128)(2,1)S(1)} %copy-done, f32[1,256]{1,0:T(1,128)S(1)} %constant_dynamic-update-slice_fusion.w_ref), custom_call_target="tpu_custom_call" | custom-call | tf_op jit(solution)/shard_map/own_references/pallas_call | solution.py:387
  17.9 0.4 shifted.4
  18.3 0.1 pad_add_fusion.a_0_
  18.4 0.4 shifted.6
  18.8 0.0 collective-permute-done
  18.8 0.4 shifted.5
  19.3 0.0 collective-permute-done.3.x_ref
  19.3 0.6 %far_references.1.a_10_ = bf16[1152,256]{1,0:T(8,128)(2,1)S(1)} custom-call(bf16[8,18432]{1,0:T(8,128)(2,1)S(1)} %collective-permute-done.3.x_ref, f32[1,256]{1,0:T(1,128)S(1)} %constant_dynamic-update-slice_fusion.w_ref), custom_call_target="tpu_custom_call" | custom-call | tf_op jit(solution)/shard_map/far_references/pallas_call | solution.py:387
  19.8 1.1 %collective-permute-done.2 = bf16[304,256]{1,0:T(8,128)(2,1)S(1)} collective-permute-done((bf16[304,256]{1,0:T(8,128)(2,1)S(1)}, bf16[304,256]{1,0:T(8,128)(2,1)S(1)}, u32[]{:S(2)}, u32[]{:S(2)}) %collective-permute-start.2) | collective-permute-done | bytes 155680 | tf_op jit(solution)/shard_map/ppermute | solution.py:356
  20.9 0.4 shifted.7
  21.3 9.0 %scores.1 = (f32[1,2,576,256]{3,2,1,0:T(8,128)S(1)}, f32[1,8,256]{2,1,0:T(8,128)S(1)}) custom-call(s32[2]{0:T(128)S(1)} %pad_add_fusion.a_0_, bf16[1,18,48,256]{3,2,1,0:T(8,128)(2,1)S(1)} %get-tuple-element.22.a_1_.a_7_, bf16[1,18,48,256]{3,2,1,0:T(8,128)(2,1)S(1)} %get-tuple-element.23.a_2_.a_8_, bf16[1,18,48,256]{3,2,1,0:T(8,128)(2,1)S(1)} %get-tuple-element.24.a_3_.a_9_, ...), custom_call_target="tpu_custom_call" | custom-call | tf_op jit(solution)/shard_map/scores/pallas_call | solution.py:387
  30.3 3.0 %collective-permute-start.5 = (f32[1,8,256]{2,1,0:T(8,128)S(1)}, f32[1,8,256]{2,1,0:T(8,128)S(1)}, u32[]{:S(2)}, u32[]{:S(2)}) collective-permute-start(f32[1,8,256]{2,1,0:T(8,128)S(1)} %get-tuple-element.31.a_5_), channel_id=1, source_target_pairs={{0,8},{2,10},{4,12},{6,14},{8,0},{10,2},{12,4},{14,6},{1,9},{3,11}... | collective-permute-start | bytes 24584 | tf_op jit(solution)/shard_map/ppermute | solution.py:356
  33.3 1.2 %collective-permute-start.6 = (f32[1,8,256]{2,1,0:T(8,128)S(1)}, f32[1,8,256]{2,1,0:T(8,128)S(1)}, u32[]{:S(2)}, u32[]{:S(2)}) collective-permute-start(f32[1,8,256]{2,1,0:T(8,128)S(1)} %get-tuple-element.31.a_5_), channel_id=1, source_target_pairs={{0,12},{2,14},{4,8},{6,10},{8,4},{10,6},{12,0},{14,2},{1,13},{3,15... | collective-permute-start | bytes 24584 | tf_op jit(solution)/shard_map/ppermute | solution.py:356
  34.5 0.5 collective-permute-start.4
  35.1 0.0 collective-permute-done.5
  35.1 3.7 %collective-permute-done.6 = f32[1,8,256]{2,1,0:T(8,128)S(1)} collective-permute-done((f32[1,8,256]{2,1,0:T(8,128)S(1)}, f32[1,8,256]{2,1,0:T(8,128)S(1)}, u32[]{:S(2)}, u32[]{:S(2)}) %collective-permute-start.6) | collective-permute-done | bytes 8224 | tf_op jit(solution)/shard_map/ppermute | solution.py:356
  38.8 0.0 collective-permute-done.4
  38.8 3.6 %far_sums.1 = (f32[576,128]{1,0:T(8,128)S(1)}, f32[576,128]{1,0:T(8,128)S(1)}, f32[8,256]{1,0:T(8,128)S(1)}) custom-call(s32[2]{0:T(128)S(1)} %pad_add_fusion.a_0_, f32[1,1,8,256]{3,2,1,0:T(8,128)S(1)} %bitcast.18, f32[1,1,8,256]{3,2,1,0:T(8,128)S(1)} %bitcast.24, f32[1,1,8,256]{3,2,1,0:T(8,128)S(1)} %bitcast.20, f32[1,1,8,256]{3,2,1,0:T(8,128)S(1)} %bitcast.22, ...), custom_call_target="tpu_custom_call" | custom-call | tf_op jit(solution)/shard_map/far_sums/pallas_call | solution.py:387
  42.4 0.1 collective-permute-start.8
  42.4 3.6 %own_sums.1 = (f32[576,128]{1,0:T(8,128)S(1)}, f32[576,128]{1,0:T(8,128)S(1)}) custom-call(s32[2]{0:T(128)S(1)} %pad_add_fusion.a_0_, f32[1,1,8,256]{3,2,1,0:T(8,128)S(1)} %bitcast.19, f32[1,1,8,256]{3,2,1,0:T(8,128)S(1)} %bitcast.25, f32[1,1,8,256]{3,2,1,0:T(8,128)S(1)} %bitcast.21, f32[1,1,8,256]{3,2,1,0:T(8,128)S(1)} %bitcast.23, ...), custom_call_target="tpu_custom_call" | custom-call | tf_op jit(solution)/shard_map/own_sums/pallas_call | solution.py:387
  46.0 0.6 %collective-permute-start.7 = (f32[576,128]{1,0:T(8,128)S(1)}, f32[576,128]{1,0:T(8,128)S(1)}, u32[]{:S(2)}, u32[]{:S(2)}) collective-permute-start(f32[576,128]{1,0:T(8,128)S(1)} %get-tuple-element.34), channel_id=1, source_target_pairs={{0,1},{1,0},{2,3},{3,2},{4,5},{5,4},{6,7},{7,6},{8,9},{9,8},{10,11... | collective-permute-start | bytes 884744 | tf_op jit(solution)/shard_map/ppermute | solution.py:356
  46.6 0.0 collective-permute-done.8
  46.6 1.5 %collective-permute-start.9 = (bf16[576,128]{1,0:T(8,128)(2,1)S(1)}, bf16[576,128]{1,0:T(8,128)(2,1)S(1)}, u32[]{:S(2)}, u32[]{:S(2)}) collective-permute-start(bf16[576,128]{1,0:T(8,128)(2,1)S(1)} %add_convert_fusion), channel_id=1, source_target_pairs={{0,2},{2,0},{4,6},{6,4},{8,10},{10,8},{12,14},{14,12},{1,3},{3,1},... | collective-permute-start | bytes 442376 | tf_op jit(solution)/shard_map/ppermute | solution.py:356
  48.2 0.5 slice_bitcast_fusion
  48.7 0.0 collective-permute-done.7.b_ref
  48.7 3.8 %collective-permute-done.9.c_ref = bf16[576,128]{1,0:T(8,128)(2,1)S(1)} collective-permute-done((bf16[576,128]{1,0:T(8,128)(2,1)S(1)}, bf16[576,128]{1,0:T(8,128)(2,1)S(1)}, u32[]{:S(2)}, u32[]{:S(2)}) %collective-permute-start.9) | collective-permute-done | bytes 147488 | tf_op jit(solution)/shard_map/ppermute | solution.py:356
  52.5 1.2 %flat_rows.1 = f32[8,9216]{1,0:T(8,128)} custom-call(f32[576,128]{1,0:T(8,128)S(1)} %get-tuple-element.33.a_ref, f32[576,128]{1,0:T(8,128)S(1)} %collective-permute-done.7.b_ref, bf16[576,128]{1,0:T(8,128)(2,1)S(1)} %collective-permute-done.9.c_ref), custom_call_target="tpu_custom_call" | custom-call | tf_op jit(solution)/shard_map/flat_rows/pallas_call | solution.py:387
  (4 shorter events, 0.1 us)
Async XLA Ops:
  0.6 0.9 %copy-start.1 = (bf16[4,18432]{1,0:T(4,128)(2,1)S(1)}, bf16[4,18432]{1,0:T(4,128)(2,1)}, u32[]{:S(2)}) copy-start(bf16[4,18432]{1,0:T(4,128)(2,1)} %a_0_.1) | copy-start | bytes 442372
  1.5 0.7 %copy-start.2 = (s32[4,3,2]{0,2,1:T(2,128)S(1)}, s32[4,3,2]{0,2,1:T(2,128)}, u32[]{:S(2)}) copy-start(s32[4,3,2]{0,2,1:T(2,128)} %param.8) | copy-start | bytes 292
  2.2 0.7 %copy-start.3 = (s32[4,32]{1,0:T(4,128)S(1)}, s32[4,32]{1,0:T(4,128)}, u32[]{:S(2)}) copy-start(s32[4,32]{1,0:T(4,128)} %a_1_.1) | copy-start | bytes 1540
  4.1 11.6 %collective-permute-start.1 = (bf16[304,256]{1,0:T(8,128)(2,1)S(1)}, bf16[304,256]{1,0:T(8,128)(2,1)S(1)}, u32[]{:S(2)}, u32[]{:S(2)}) collective-permute-start(bf16[304,256]{1,0:T(8,128)(2,1)S(1)} %particle_turns.1), channel_id=1, source_target_pairs={{0,8},{2,10},{4,12},{6,14},{8,0},{10,2},{12,4},{14,6},{1,9},{3,11}... | collective-permute-start | bytes 466952 | tf_op jit(solution)/shard_map/ppermute | solution.py:356
  8.2 10.6 %collective-permute-start = (bf16[304,256]{1,0:T(8,128)(2,1)S(1)}, bf16[304,256]{1,0:T(8,128)(2,1)S(1)}, u32[]{:S(2)}, u32[]{:S(2)}) collective-permute-start(bf16[304,256]{1,0:T(8,128)(2,1)S(1)} %particle_turns.1), channel_id=1, source_target_pairs={{0,4},{2,6},{4,0},{6,2},{8,12},{10,14},{12,8},{14,10},{1,5},{3,7},... | collective-permute-start | bytes 466952 | tf_op jit(solution)/shard_map/ppermute | solution.py:356
  9.8 9.5 %collective-permute-start.3 = (bf16[8,18432]{1,0:T(8,128)(2,1)}, bf16[8,18432]{1,0:T(8,128)(2,1)S(1)}, u32[]{:S(2)}, u32[]{:S(2)}) collective-permute-start(bf16[8,18432]{1,0:T(8,128)(2,1)} %x_ref.1), channel_id=1, source_target_pairs={{0,2},{2,0},{4,6},{6,4},{8,10},{10,8},{12,14},{14,12},{1,3},{3,1},... | collective-permute-start | bytes 884744 | tf_op jit(solution)/shard_map/ppermute | solution.py:356
  15.7 5.2 %collective-permute-start.2 = (bf16[304,256]{1,0:T(8,128)(2,1)S(1)}, bf16[304,256]{1,0:T(8,128)(2,1)S(1)}, u32[]{:S(2)}, u32[]{:S(2)}) collective-permute-start(bf16[304,256]{1,0:T(8,128)(2,1)S(1)} %collective-permute-done.1), channel_id=1, source_target_pairs={{0,4},{2,6},{4,0},{6,2},{8,12},{10,14},{12,8},{14,10},{1,5},{3,7},... | collective-permute-start | bytes 466952 | tf_op jit(solution)/shard_map/ppermute | solution.py:356
  16.3 1.0 %copy-start = (bf16[8,18432]{1,0:T(8,128)(2,1)S(1)}, bf16[8,18432]{1,0:T(8,128)(2,1)}, u32[]{:S(2)}) copy-start(bf16[8,18432]{1,0:T(8,128)(2,1)} %x_ref.1) | copy-start | bytes 884740
  30.3 4.8 %collective-permute-start.5 = (f32[1,8,256]{2,1,0:T(8,128)S(1)}, f32[1,8,256]{2,1,0:T(8,128)S(1)}, u32[]{:S(2)}, u32[]{:S(2)}) collective-permute-start(f32[1,8,256]{2,1,0:T(8,128)S(1)} %get-tuple-element.31.a_5_), channel_id=1, source_target_pairs={{0,8},{2,10},{4,12},{6,14},{8,0},{10,2},{12,4},{14,6},{1,9},{3,11}... | collective-permute-start | bytes 24584 | tf_op jit(solution)/shard_map/ppermute | solution.py:356
  33.3 5.4 %collective-permute-start.6 = (f32[1,8,256]{2,1,0:T(8,128)S(1)}, f32[1,8,256]{2,1,0:T(8,128)S(1)}, u32[]{:S(2)}, u32[]{:S(2)}) collective-permute-start(f32[1,8,256]{2,1,0:T(8,128)S(1)} %get-tuple-element.31.a_5_), channel_id=1, source_target_pairs={{0,12},{2,14},{4,8},{6,10},{8,4},{10,6},{12,0},{14,2},{1,13},{3,15... | collective-permute-start | bytes 24584 | tf_op jit(solution)/shard_map/ppermute | solution.py:356
  34.5 4.2 %collective-permute-start.4 = (f32[1,8,256]{2,1,0:T(8,128)S(1)}, f32[1,8,256]{2,1,0:T(8,128)S(1)}, u32[]{:S(2)}, u32[]{:S(2)}) collective-permute-start(f32[1,8,256]{2,1,0:T(8,128)S(1)} %get-tuple-element.31.a_5_), channel_id=1, source_target_pairs={{0,4},{2,6},{4,0},{6,2},{8,12},{10,14},{12,8},{14,10},{1,5},{3,7},... | collective-permute-start | bytes 24584 | tf_op jit(solution)/shard_map/ppermute | solution.py:356
  42.4 4.2 %collective-permute-start.8 = (f32[576,128]{1,0:T(8,128)S(1)}, f32[576,128]{1,0:T(8,128)S(1)}, u32[]{:S(2)}, u32[]{:S(2)}) collective-permute-start(f32[576,128]{1,0:T(8,128)S(1)} %get-tuple-element.36), channel_id=1, source_target_pairs={{0,1},{1,0},{2,3},{3,2},{4,5},{5,4},{6,7},{7,6},{8,9},{9,8},{10,11... | collective-permute-start | bytes 884744 | tf_op jit(solution)/shard_map/ppermute | solution.py:356
  46.0 2.7 %collective-permute-start.7 = (f32[576,128]{1,0:T(8,128)S(1)}, f32[576,128]{1,0:T(8,128)S(1)}, u32[]{:S(2)}, u32[]{:S(2)}) collective-permute-start(f32[576,128]{1,0:T(8,128)S(1)} %get-tuple-element.34), channel_id=1, source_target_pairs={{0,1},{1,0},{2,3},{3,2},{4,5},{5,4},{6,7},{7,6},{8,9},{9,8},{10,11... | collective-permute-start | bytes 884744 | tf_op jit(solution)/shard_map/ppermute | solution.py:356
  46.6 5.8 %collective-permute-start.9 = (bf16[576,128]{1,0:T(8,128)(2,1)S(1)}, bf16[576,128]{1,0:T(8,128)(2,1)S(1)}, u32[]{:S(2)}, u32[]{:S(2)}) collective-permute-start(bf16[576,128]{1,0:T(8,128)(2,1)S(1)} %add_convert_fusion), channel_id=1, source_target_pairs={{0,2},{2,0},{4,6},{6,4},{8,10},{10,8},{12,14},{14,12},{1,3},{3,1},... | collective-permute-start | bytes 442376 | tf_op jit(solution)/shard_map/ppermute | solution.py:356

commit v3 on v2

--- a/solution.py
+++ b/solution.py
@@ -98,10 +98,11 @@
     copies = [pltpu.make_async_copy(a, b, sems.at[n]) for n, (a, b) in enumerate(pairs)]
     for copy in copies:
         copy.start()
-    for copy in copies:
-        copy.wait()
+    copies[0].wait()
     turn_major(x_ref, grid_ref, lines_ref, turns_ref, PER_DEV)
     out_ref[:ROWS] = jnp.concatenate([turns_ref[0], turns_ref[1]], axis=1).astype(BF16)
+    copies[1].wait()
+    copies[2].wait()
     lists = list_ref[...]
     lane = lax.broadcasted_iota(jnp.int32, (PER_DEV, LANES), 1)
     parts = []
@@ -177,8 +178,13 @@
     if bits & 1:
         x = xor_lanes(x, 64)
     if bits & 2:
-        x = xor_lanes(x, 128)
+        x = xor_lanes(x, 4)
     return x
+
+
+def live_lanes(shape):
+    lane = lax.broadcasted_iota(jnp.int32, shape, 1)
+    return (lane % 64 < 16 * TRANS) & (lane % 16 < 8)
 
 
 def images_of(x_refs, q):
@@ -189,34 +195,23 @@
 def score_kernel(nbit, me_ref, *refs):
     x_refs = refs[:SLOTS]
     bit_refs = refs[SLOTS : 2 * SLOTS]
-    own_ref, other_ref, e_ref, stat_ref, acc_ref = refs[2 * SLOTS :]
-    acc_ref[...] = jnp.zeros_like(acc_ref)
-
-    def step(g, carry):
-        for side, ref in enumerate((own_ref, other_ref)):
-            total = acc_ref[side, :REF_ROWS]
-            for r in range(3):
-                q = 3 * g + r
-                turned = ref[pl.ds(pl.multiple_of(q * 32, 32), REF_ROWS), :]
-                total += lax.dot_general(
-                    turned, images_of(x_refs, q), (((1,), (1,)), ((), ())), preferred_element_type=F32
-                )
-            acc_ref[side, :REF_ROWS] = total
-        return carry
-
-    lax.fori_loop(0, STEPS // 3, step, 0)
-
-    src = lax.broadcasted_iota(jnp.int32, (SLOTS * 16, LANES), 0)
-    dst = lax.broadcasted_iota(jnp.int32, (SLOTS * 16, LANES), 1)
-    ok = (src == dst // 64 * 16 + dst % 4) & (dst % 64 < 48) & (dst % 16 < 4)
-    place = ok.astype(F32).astype(BF16)
+    own_ref, far_ref, e_ref, stat_ref, acc_ref, pair_ref = refs[2 * SLOTS :]
+
+    src = lax.broadcasted_iota(jnp.int32, (SLOTS * 16, HALF), 0)
+    dst = lax.broadcasted_iota(jnp.int32, (SLOTS * 16, HALF), 1)
+    slot = dst // 64 + 2 * (dst % 16 // 4)
+    place = ((src == slot * 16 + dst % 4) & live_lanes(src.shape)).astype(F32).astype(BF16)
     lane = lax.broadcasted_iota(jnp.int32, (CLS, LANES), 1)
     row = lax.broadcasted_iota(jnp.int32, (CLS, LANES), 0)
-    top = jnp.full((CLS, LANES), LOWEST, F32)
-    masks = []
-    for side in range(2):
+    turn = lax.broadcasted_iota(jnp.int32, (CLS, HALF), 1) % 16 // 4
+    images = jnp.concatenate([images_of(x_refs, q) for q in range(STEPS)], axis=1)
+    top = jnp.full((CLS, HALF), LOWEST, F32)
+    for side, ref in enumerate((own_ref, far_ref)):
+        turned = jnp.concatenate([ref[q * 32 : q * 32 + REF_ROWS] for q in range(STEPS)], axis=1)
+        acc_ref[...] = lax.dot_general(turned, images, (((1,), (1,)), ((), ())), preferred_element_type=F32)
+
+        named = jnp.zeros((CLS, SLOTS * 16), F32)
         chip = me_ref[0] ^ side
-        named = jnp.zeros((CLS, SLOTS * 16), F32)
         for b in range(nbit):
             pick = (lane + b * LANES == chip * CLS + row).astype(F32).astype(BF16)
             first = 16 * (b // 2)
@@ -228,96 +223,121 @@
                 )
             named += lax.dot_general(pick, bits, (((1,), (1,)), ((), ())), preferred_element_type=F32)
         mask = jnp.dot(named.astype(BF16), place, preferred_element_type=F32) > 0.5
-        masks.append(mask)
-        acc_ref[side, REF_ROWS:] = acc_ref[side, :32]
-
-        def body_max(i, top, side=side, mask=mask):
-            at = lambda d: acc_ref[side, pl.ds(pl.multiple_of((i + d) * 8, 8), 8), :]
-            s = at(0)
-            for d in range(1, 4):
-                s += pltpu.roll(at(d), LANES - 4 * d, 1)
+
+        def at(i):
+            i = i % ROT
+            return acc_ref[i * 8 : i * 8 + 8, :HALF], acc_ref[i * 8 : i * 8 + 8, HALF:]
+
+        for i in range(ROT):
+            (a, b), (c, d) = at(i), at(i + 1)
+            low = a + pltpu.roll(c, HALF - 4, 1)
+            high = b + pltpu.roll(d, HALF - 4, 1)
+            pair_ref[i * 8 : i * 8 + 8] = jnp.where(turn % 2 == 0, low, pltpu.roll(high, 4, 1))
+        for i in range(ROT):
+            n = (i + 2) % ROT
+            s = pair_ref[i * 8 : i * 8 + 8] + pltpu.roll(pair_ref[n * 8 : n * 8 + 8], HALF - 8, 1)
             s = jnp.where(mask, s, LOWEST)
-            e_ref[0, side, pl.ds(pl.multiple_of(i * 8, 8), 8), :] = s
-            return jnp.maximum(top, s)
-
-        top = lax.fori_loop(0, ROT, body_max, top, unroll=8)
-    top = jnp.broadcast_to(jnp.max(top, axis=0, keepdims=True), (CLS, LANES))
+            e_ref[0, side, i * 8 : i * 8 + 8] = s
+            top = jnp.maximum(top, s)
+    top = jnp.broadcast_to(jnp.max(top, axis=0, keepdims=True), (CLS, HALF))
     top = jnp.maximum(top, xor_lanes(top, 16))
     top = jnp.maximum(top, xor_lanes(top, 32))
-    total = jnp.zeros((CLS, LANES), F32)
+    base = jnp.where(top == LOWEST, 0.0, top)
+    total = jnp.zeros((CLS, HALF), F32)
     for side in range(2):
-
-        def body_exp(i, total, side=side):
-            rows = pl.ds(pl.multiple_of(i * 8, 8), 8)
-            e = jnp.where(masks[side], jnp.exp(e_ref[0, side, rows, :] - top), 0.0)
-            e_ref[0, side, rows, :] = e
-            return total + e
-
-        total = lax.fori_loop(0, ROT, body_exp, total, unroll=8)
-    total = jnp.broadcast_to(jnp.sum(total, axis=0, keepdims=True), (CLS, LANES))
+        for i in range(ROT):
+            e = jnp.exp(e_ref[0, side, i * 8 : i * 8 + 8] - base)
+            e_ref[0, side, i * 8 : i * 8 + 8] = e
+            total += e
+    total = jnp.broadcast_to(jnp.sum(total, axis=0, keepdims=True), (CLS, HALF))
     total = total + xor_lanes(total, 16)
     total = total + xor_lanes(total, 32)
-    stat_ref[0] = jnp.where(row == 0, top, total)
-
-
-def back_kernel(side, nblocks, me_ref, *refs):
+    stat_ref[0] = jnp.where(lax.broadcasted_iota(jnp.int32, (CLS, HALF), 0) == 0, top, total)
+
+
+def factors(got_refs, stat_ref, nblocks, n):
+    stats = [
+        xor_slots(got_refs[low][high, n ^ high], low) for high in range(nblocks) for low in range(SLOTS)
+    ]
+    spread = lambda x, r: jnp.broadcast_to(x[r : r + 1], (8, HALF))
+    tops = [spread(x, 0) for x in stats]
+    best = tops[0]
+    for top in tops[1:]:
+        best = jnp.maximum(best, top)
+    evidence = jnp.zeros((8, HALF), F32)
+    for top, x in zip(tops, stats):
+        evidence = evidence + spread(x, 1) * jnp.exp(top - best)
+    factor = jnp.where(live_lanes((8, HALF)), jnp.exp(spread(stat_ref[0], 0) - best) / evidence, 0.0)
+    return factor, best + jnp.log(evidence)
+
+
+def spread_kernel(e_ref, far_ref, own_ref):
+    turn = lax.broadcasted_iota(jnp.int32, (8, HALF), 1) % 16 // 4
+    for side, out_ref in enumerate((own_ref, far_ref)):
+
+        def weights(i):
+            i = i % ROT
+            w = e_ref[0, side, i * 8 : i * 8 + 8]
+            return jnp.where(turn == 0, w, 0.0), jnp.where(turn == 1, w, 0.0)
+
+        def two_turns(now, before):
+            return now[0] + pltpu.roll(before[0], 4, 1), pltpu.roll(now[1], HALF - 4, 1) + before[1]
+
+        plain = [weights(i) for i in (-3, -2, -1)]
+        pairs = [two_turns(plain[1], plain[0]), two_turns(plain[2], plain[1])]
+        before = plain[2]
+        for i in range(ROT):
+            now = weights(i)
+            pairs.append(two_turns(now, before))
+            before = now
+            last = pairs.pop(0)
+            (a, b), (c, d) = pairs[-1], last
+            out_ref[0, i * 8 : i * 8 + 8, :HALF] = a + pltpu.roll(c, 8, 1)
+            out_ref[0, i * 8 : i * 8 + 8, HALF:] = b + pltpu.roll(d, 8, 1)
+
+
+def back_kernel(nblocks, me_ref, *refs):
     got_refs = refs[:SLOTS]
     stat_ref, e_ref = refs[SLOTS : SLOTS + 2]
     x_refs = refs[SLOTS + 2 : 2 * SLOTS + 2]
     keep_ref, send_ref, *log_ref = refs[2 * SLOTS + 2 : -2]
     w_ref, acc_ref = refs[-2:]
     n = pl.program_id(0) if nblocks > 1 else 0
-    stats = [
-        xor_slots(got_refs[low][high, n ^ high], low) for high in range(nblocks) for low in range(SLOTS)
-    ]
-    spread = lambda x, r: jnp.broadcast_to(x[r : r + 1], (8, LANES))
-    tops = [spread(x, 0) for x in stats]
-    best = tops[0]
-    for top in tops[1:]:
-        best = jnp.maximum(best, top)
-    evidence = jnp.zeros((8, LANES), F32)
-    for top, x in zip(tops, stats):
-        evidence = evidence + spread(x, 1) * jnp.exp(top - best)
-    lane = lax.broadcasted_iota(jnp.int32, (8, LANES), 1)
-    live = (lane % 64 < 48) & (lane % 16 < 4)
-    factor = jnp.where(live, jnp.exp(spread(stat_ref[0], 0) - best) / evidence, 0.0)
-
-    def start():
-        acc_ref[...] = jnp.zeros_like(acc_ref)
-        if log_ref:
-            log_ref[0][...] = best + jnp.log(evidence)
-
-    if nblocks > 1:
-        pl.when(n == 0)(start)
+    factor, logs = factors(got_refs, stat_ref, nblocks, n)
+    if log_ref:
+
+        @pl.when(n == 0)
+        def _():
+            log_ref[0][...] = logs
+
+    turn = lax.broadcasted_iota(jnp.int32, (8, HALF), 1) % 16 // 4
+    low = jnp.where(turn == 0, factor, 0.0)
+    high = pltpu.roll(jnp.where(turn == 1, factor, 0.0), HALF - 4, 1)
+    low, high = (f + pltpu.roll(f, 4, 1) for f in (low, high))
+    low, high = (f + pltpu.roll(f, 8, 1) for f in (low, high))
+    both = jnp.concatenate([low, high], axis=1)
+    both = jnp.concatenate([both, both], axis=0)
+    for i in range(0, REF_ROWS, 16):
+        pair = (e_ref[0, i : i + 16] * both).astype(BF16)
+        w_ref[i : i + 16] = pair
+        w_ref[REF_ROWS + i : REF_ROWS + i + 16] = pair
+
+    turned = jnp.concatenate(
+        [w_ref[(STEPS - q) * 32 : (STEPS - q) * 32 + REF_ROWS] for q in range(STEPS)], axis=1
+    )
+    images = jnp.concatenate([images_of(x_refs, q) for q in range(STEPS)], axis=0)
+    made = jnp.dot(turned, images, preferred_element_type=F32)
+    if nblocks == 1:
+        acc_ref[...] = made
     else:
-        start()
-
-    def weights(i):
-        i = i % ROT
-        return e_ref[0, side, i * 8 : i * 8 + 8, :] * factor
-
-    window = [weights(i) for i in (-3, -2, -1)]
-    for i in range(0, ROT, 2):
-        rows = []
-        for d in range(2):
-            now = weights(i + d)
-            a, b, c = window
-            rows.append(now + pltpu.roll(c, 4, 1) + pltpu.roll(b, 8, 1) + pltpu.roll(a, 12, 1))
-            window = [b, c, now]
-        pair = jnp.concatenate(rows, axis=0).astype(BF16)
-        w_ref[i * 8 : i * 8 + 16, :] = pair
-        w_ref[REF_ROWS + i * 8 : REF_ROWS + i * 8 + 16, :] = pair
-
-    def step(g, carry):
-        total = acc_ref[...]
-        for r in range(3):
-            q = 3 * g + r
-            turned = w_ref[pl.ds(pl.multiple_of((STEPS - q) * 32, 32), REF_ROWS), :]
-            total += jnp.dot(turned, images_of(x_refs, q), preferred_element_type=F32)
-        acc_ref[...] = total
-        return carry
-
-    lax.fori_loop(0, STEPS // 3, step, 0)
+
+        @pl.when(n == 0)
+        def _():
+            acc_ref[...] = made
+
+        @pl.when(n > 0)
+        def _():
+            acc_ref[...] += made
 
     @pl.when((n == nblocks - 1) & (me_ref[1] == 0))
     def _():
@@ -370,12 +390,12 @@
     return [slots[s::SLOTS] for s in range(SLOTS)]
 
 
-def call(name, body, nblocks, inputs, outputs, scratch):
+def call(name, body, nblocks, inputs, outputs, scratch, micros=1, vmem=VMEM):
     def spec(shape, kind):
         if kind == "scalar":
             return pl.BlockSpec(memory_space=pltpu.SMEM)
         if kind == "any":
-            return pl.BlockSpec(memory_space=pl.ANY)
+            return pl.BlockSpec(memory_space=pltpu.HBM)
         if nblocks == 1:
             return pl.BlockSpec(memory_space=pltpu.VMEM)
         rest = (0,) * (len(shape) - 1)
@@ -390,7 +410,8 @@
         in_specs=[spec(x.shape, kind) for x, kind in inputs],
         out_specs=tuple(spec(shape, kind) for shape, _, kind in outputs),
         scratch_shapes=scratch,
-        compiler_params=pltpu.CompilerParams(vmem_limit_bytes=VMEM),
+        compiler_params=pltpu.CompilerParams(vmem_limit_bytes=vmem),
+        cost_estimate=pl.CostEstimate(flops=micros * 10**9, bytes_accessed=micros * 10**6, transcendentals=0),
         name=name,
         **grid,
     )(*[x for x, _ in inputs])
@@ -425,6 +446,7 @@
         ]
         + scratch(PER_DEV)
         + [pltpu.SemaphoreType.DMA((3,))],
+        vmem=60 * 1024 * 1024,
     )
     slots = gather_slots(block, True)
     far_references = swap(references, "cls", 1)
@@ -459,25 +481,29 @@
         lambda *a: score_kernel(nbit, *a),
         nblocks,
         [(me, "scalar")] + [(x, "block") for x in images + bits] + [(own_refs, "all"), (far_refs, "all")],
-        [((nblocks, 2, REF_ROWS, LANES), F32, "block"), ((nblocks, 8, LANES), F32, "block")],
-        [pltpu.VMEM((2, REF_ROWS + 32, LANES), F32)],
+        [((nblocks, 2, REF_ROWS, HALF), F32, "block"), ((nblocks, 8, HALF), F32, "block")],
+        [pltpu.VMEM((REF_ROWS, LANES), F32), pltpu.VMEM((REF_ROWS, HALF), F32)],
     )
     got = gather_slots(stat, False)
 
-    def back(side):
+    wide = ((nblocks, REF_ROWS, LANES), F32, "block")
+    far_expo, own_expo = call("spread", spread_kernel, nblocks, [(expo, "block")], [wide, wide], [])
+
+    def back(name, expo, more):
         half = ((REF_ROWS, HALF), F32, "all")
         return call(
-            "far_sums" if side else "own_sums",
-            lambda *a: back_kernel(side, nblocks, *a),
+            name,
+            lambda *a: back_kernel(nblocks, *a),
             nblocks,
             [(me, "scalar")] + [(g, "all") for g in got] + [(stat, "block"), (expo, "block")] + [(x, "block") for x in images],
-            [half, half] + [((8, LANES), F32, "all")] * side,
+            [half, half] + more,
             [pltpu.VMEM((2 * REF_ROWS, LANES), BF16), pltpu.VMEM((REF_ROWS, LANES), F32)],
+            4,
         )
 
-    far_keep, far_send, logs = back(1)
+    far_keep, far_send, logs = back("far_sums", far_expo, [((8, HALF), F32, "all")])
     far_got = swap(far_send, "dom", 1)
-    keep, send = back(0)
+    keep, send = back("own_sums", own_expo, [])
     own_got = swap(send, "dom", 1)
     far_sum = swap((far_keep + far_got).astype(BF16), "cls", 1)
     (sums,) = call(

time: 53.9 us -> 46.3 us (0.86)
  local copies, waits for them, and re-layouts: 4.66 us -> 1.73 us
  Pallas kernels: 21.4 us -> 18.6 us
  waiting for transfers between devices: 12 us -> 10.1 us
    pallas_call x11 -> x12, Pallas kernels: 21.4 us -> 18.6 us  [call(): pl.pallas_call(body, out_shape=tuple((jax.ShapeDtypeStruct(shape, dtype)...]
    unnamed x9 -> x7, local copies, waits for them, and re-layouts: 3.23 us -> 0.96 us
    ppermute x10, waiting for transfers between devices: 12 us -> 10.1 us  [swap(): lax.ppermute(x, axis, [(i, i ^ bits) for i in range(lax.axis_size(axis))])]
    reshape x1, local copies, waits for them, and re-layouts: 0.73 us -> 0.08 us  [per_device(): weights = jnp.repeat(inv_noise.reshape(8, 8).T, 2, axis=0).reshape(1, HALF)]
  transfers between devices with their start and end apart: 10 -> 10, of which waited for: 4 -> 5; matrix products, arithmetic and copies ran while one was open for 3% -> 2% of each run, Pallas kernels for 11% -> 17%
where the time goes in v3:
time: 46.3 us; the launch traced here: 46.1 us
  Pallas kernels  18.6 us (40%)
  starting transfers between devices  14.8 us (32%)
  waiting for transfers between devices  10.1 us (22%)
  local copies, waits for them, and re-layouts  1.73 us (4%)
  between operations  0.77 us (2%)
    pallas_call x12, Pallas kernels, call(): pl.pallas_call(body, out_shape=tuple((jax.ShapeDtypeStruct(shape, dtype)...  18.6 us
    ppermute x10, starting transfers between devices, swap(): lax.ppermute(x, axis, [(i, i ^ bits) for i in range(lax.axis_size(axis))])  14.8 us
    ppermute x10, waiting for transfers between devices, swap(): lax.ppermute(x, axis, [(i, i ^ bits) for i in range(lax.axis_size(axis))])  10.1 us
    unnamed x7, local copies, waits for them, and re-layouts  0.96 us
  transfers between devices with their start and end apart: 10, of which 5 were waited for; matrix products, arithmetic and copies ran while one was open for 2% of the time, Pallas kernels for 17%

profile of v3, /device:TPU:0, one launch (start us, length us, event | category | flops | bytes accessed | tf_op | source)
XLA Modules:
  0.0 46.1 jit_solution(12901000231364317344)
XLA Ops:
  0.6 0.0 copy-start
  0.6 2.2 %particle_turns.1 = bf16[304,256]{1,0:T(8,128)(2,1)} custom-call(bf16[4,18432]{1,0:T(4,128)(2,1)} %a_0_.1, s32[4,32]{1,0:T(4,128)} %a_1_.1, s32[3,2,4]{2,1,0:T(2,128)} %bitcast.27), custom_call_target="tpu_custom_call" | custom-call | flops 1000000000 | bytes 1000000 | tf_op jit(solution)/shard_map/particle_turns/pallas_call | solution.py:407
  2.9 4.1 %collective-permute-start.1 = (bf16[304,256]{1,0:T(8,128)(2,1)}, bf16[304,256]{1,0:T(8,128)(2,1)S(1)}, u32[]{:S(2)}, u32[]{:S(2)}) collective-permute-start(bf16[304,256]{1,0:T(8,128)(2,1)} %particle_turns.1), channel_id=1, source_target_pairs={{0,8},{2,10},{4,12},{6,14},{8,0},{10,2},{12,4},{14,6},{1,9},{3,11}... | collective-permute-start | bytes 466952 | tf_op jit(solution)/shard_map/ppermute | solution.py:376
  7.0 1.6 %collective-permute-start = (bf16[304,256]{1,0:T(8,128)(2,1)}, bf16[304,256]{1,0:T(8,128)(2,1)S(1)}, u32[]{:S(2)}, u32[]{:S(2)}) collective-permute-start(bf16[304,256]{1,0:T(8,128)(2,1)} %particle_turns.1), channel_id=1, source_target_pairs={{0,4},{2,6},{4,0},{6,2},{8,12},{10,14},{12,8},{14,10},{1,5},{3,7},... | collective-permute-start | bytes 466952 | tf_op jit(solution)/shard_map/ppermute | solution.py:376
  8.6 0.0 copy-done
  8.6 1.5 %collective-permute-start.3 = (bf16[8,18432]{1,0:T(8,128)(2,1)S(1)}, bf16[8,18432]{1,0:T(8,128)(2,1)S(1)}, u32[]{:S(2)}, u32[]{:S(2)}) collective-permute-start(bf16[8,18432]{1,0:T(8,128)(2,1)S(1)} %copy-done), channel_id=1, source_target_pairs={{0,2},{2,0},{4,6},{6,4},{8,10},{10,8},{12,14},{14,12},{1,3},{3,1},... | collective-permute-start | bytes 884744 | tf_op jit(solution)/shard_map/ppermute | solution.py:376
  10.1 0.0 copy-start.2
  10.1 0.7 %copy-done.2 = f32[64]{0:T(128)S(1)} copy-done((f32[64]{0:T(128)S(1)}, f32[64]{0:T(128)}, u32[]{:S(2)}) %copy-start.2) | copy-done | bytes 280
  10.7 0.1 reshape.7
  10.8 0.1 copy.7
  10.9 0.1 reshape_reshape.3
  11.0 0.1 pad_add_fusion.a_0_
  11.1 0.0 copy-start.1
  11.1 0.6 %own_references.1 = (bf16[1152,256]{1,0:T(8,128)(2,1)S(1)}, f32[144,128]{1,0:T(8,128)S(1)}, f32[144,128]{1,0:T(8,128)S(1)}) custom-call(bf16[8,18432]{1,0:T(8,128)(2,1)S(1)} %copy-done, f32[1,256]{1,0:T(1,128)S(1)} %constant_dynamic-update-slice_fusion.w_ref), custom_call_target="tpu_custom_call" | custom-call | flops 1000000000 | bytes 1000000 | tf_op jit(solution)/shard_map/own_references/pallas_call | solution.py:407
  11.7 0.3 copy-done.1
  12.0 0.4 shifted.4
  12.4 2.2 %collective-permute-done.1 = bf16[304,256]{1,0:T(8,128)(2,1)S(1)} collective-permute-done((bf16[304,256]{1,0:T(8,128)(2,1)}, bf16[304,256]{1,0:T(8,128)(2,1)S(1)}, u32[]{:S(2)}, u32[]{:S(2)}) %collective-permute-start.1) | collective-permute-done | bytes 155680 | tf_op jit(solution)/shard_map/ppermute | solution.py:376
  14.7 0.7 %collective-permute-start.2 = (bf16[304,256]{1,0:T(8,128)(2,1)S(1)}, bf16[304,256]{1,0:T(8,128)(2,1)S(1)}, u32[]{:S(2)}, u32[]{:S(2)}) collective-permute-start(bf16[304,256]{1,0:T(8,128)(2,1)S(1)} %collective-permute-done.1), channel_id=1, source_target_pairs={{0,4},{2,6},{4,0},{6,2},{8,12},{10,14},{12,8},{14,10},{1,5},{3,7},... | collective-permute-start | bytes 466952 | tf_op jit(solution)/shard_map/ppermute | solution.py:376
  15.4 0.4 shifted.6
  15.8 0.0 collective-permute-done
  15.8 0.4 shifted.5
  16.3 0.5 %collective-permute-done.3.x_ref = bf16[8,18432]{1,0:T(8,128)(2,1)S(1)} collective-permute-done((bf16[8,18432]{1,0:T(8,128)(2,1)S(1)}, bf16[8,18432]{1,0:T(8,128)(2,1)S(1)}, u32[]{:S(2)}, u32[]{:S(2)}) %collective-permute-start.3) | collective-permute-done | bytes 294944 | tf_op jit(solution)/shard_map/ppermute | solution.py:376
  16.8 0.6 %far_references.1.a_10_ = bf16[1152,256]{1,0:T(8,128)(2,1)S(1)} custom-call(bf16[8,18432]{1,0:T(8,128)(2,1)S(1)} %collective-permute-done.3.x_ref, f32[1,256]{1,0:T(1,128)S(1)} %constant_dynamic-update-slice_fusion.w_ref), custom_call_target="tpu_custom_call" | custom-call | flops 1000000000 | bytes 1000000 | tf_op jit(solution)/shard_map/far_references/pallas_call | solution.py:407
  17.3 2.6 %collective-permute-done.2 = bf16[304,256]{1,0:T(8,128)(2,1)S(1)} collective-permute-done((bf16[304,256]{1,0:T(8,128)(2,1)S(1)}, bf16[304,256]{1,0:T(8,128)(2,1)S(1)}, u32[]{:S(2)}, u32[]{:S(2)}) %collective-permute-start.2) | collective-permute-done | bytes 155680 | tf_op jit(solution)/shard_map/ppermute | solution.py:376
  19.9 0.4 shifted.7
  20.3 4.5 %scores.1 = (f32[1,2,576,128]{3,2,1,0:T(8,128)S(1)}, f32[1,8,128]{2,1,0:T(8,128)S(1)}) custom-call(s32[2]{0:T(128)S(1)} %pad_add_fusion.a_0_, bf16[1,18,48,256]{3,2,1,0:T(8,128)(2,1)S(1)} %get-tuple-element.24.a_1_.a_7_, bf16[1,18,48,256]{3,2,1,0:T(8,128)(2,1)S(1)} %get-tuple-element.25.a_2_.a_8_, bf16[1,18,48,256]{3,2,1,0:T(8,128)(2,1)S(1)} %get-tuple-element.26.a_3_.a_9_, ...), custom_call_target="tpu_custom_call" | custom-call | flops 1000000000 | bytes 1000000 | tf_op jit(solution)/shard_map/scores/pallas_call | solution.py:407
  24.8 4.2 %collective-permute-start.6 = (f32[1,8,128]{2,1,0:T(8,128)S(1)}, f32[1,8,128]{2,1,0:T(8,128)S(1)}, u32[]{:S(2)}, u32[]{:S(2)}) collective-permute-start(f32[1,8,128]{2,1,0:T(8,128)S(1)} %get-tuple-element.33.a_5_), channel_id=1, source_target_pairs={{0,12},{2,14},{4,8},{6,10},{8,4},{10,6},{12,0},{14,2},{1,13},{3,15... | collective-permute-start | bytes 12296 | tf_op jit(solution)/shard_map/ppermute | solution.py:376
  28.9 0.0 collective-permute-start.5
  28.9 0.6 %collective-permute-start.4 = (f32[1,8,128]{2,1,0:T(8,128)S(1)}, f32[1,8,128]{2,1,0:T(8,128)S(1)}, u32[]{:S(2)}, u32[]{:S(2)}) collective-permute-start(f32[1,8,128]{2,1,0:T(8,128)S(1)} %get-tuple-element.33.a_5_), channel_id=1, source_target_pairs={{0,4},{2,6},{4,0},{6,2},{8,12},{10,14},{12,8},{14,10},{1,5},{3,7},... | collective-permute-start | bytes 12296 | tf_op jit(solution)/shard_map/ppermute | solution.py:376
  29.5 2.9 %spread.1 = (f32[1,576,256]{2,1,0:T(8,128)S(1)}, f32[1,576,256]{2,1,0:T(8,128)S(1)}) custom-call(f32[1,2,576,128]{3,2,1,0:T(8,128)S(1)} %get-tuple-element.34.e_ref), custom_call_target="tpu_custom_call" | custom-call | flops 1000000000 | bytes 1000000 | tf_op jit(solution)/shard_map/spread/pallas_call | solution.py:407
  32.4 0.0 collective-permute-done.6
  32.4 1.0 %collective-permute-done.5 = f32[1,8,128]{2,1,0:T(8,128)S(1)} collective-permute-done((f32[1,8,128]{2,1,0:T(8,128)S(1)}, f32[1,8,128]{2,1,0:T(8,128)S(1)}, u32[]{:S(2)}, u32[]{:S(2)}) %collective-permute-start.5) | collective-permute-done | bytes 4128 | tf_op jit(solution)/shard_map/ppermute | solution.py:376
  33.5 0.0 collective-permute-done.4
  33.5 2.4 %far_sums.1 = (f32[576,128]{1,0:T(8,128)S(1)}, f32[576,128]{1,0:T(8,128)S(1)}, f32[8,128]{1,0:T(8,128)S(1)}) custom-call(s32[2]{0:T(128)S(1)} %pad_add_fusion.a_0_, f32[1,1,8,128]{3,2,1,0:T(8,128)S(1)} %bitcast.18, f32[1,1,8,128]{3,2,1,0:T(8,128)S(1)} %bitcast.24, f32[1,1,8,128]{3,2,1,0:T(8,128)S(1)} %bitcast.22, f32[1,1,8,128]{3,2,1,0:T(8,128)S(1)} %bitcast.20, ...), custom_call_target="tpu_custom_call" | custom-call | flops 4000000000 | bytes 4000000 | tf_op jit(solution)/shard_map/far_sums/pallas_call | solution.py:407
  35.9 0.1 collective-permute-start.8
  36.0 2.4 %own_sums.1 = (f32[576,128]{1,0:T(8,128)S(1)}, f32[576,128]{1,0:T(8,128)S(1)}) custom-call(s32[2]{0:T(128)S(1)} %pad_add_fusion.a_0_, f32[1,1,8,128]{3,2,1,0:T(8,128)S(1)} %bitcast.19, f32[1,1,8,128]{3,2,1,0:T(8,128)S(1)} %bitcast.25, f32[1,1,8,128]{3,2,1,0:T(8,128)S(1)} %bitcast.23, f32[1,1,8,128]{3,2,1,0:T(8,128)S(1)} %bitcast.21, ...), custom_call_target="tpu_custom_call" | custom-call | flops 4000000000 | bytes 4000000 | tf_op jit(solution)/shard_map/own_sums/pallas_call | solution.py:407
  38.4 0.6 %collective-permute-start.7 = (f32[576,128]{1,0:T(8,128)S(1)}, f32[576,128]{1,0:T(8,128)S(1)}, u32[]{:S(2)}, u32[]{:S(2)}) collective-permute-start(f32[576,128]{1,0:T(8,128)S(1)} %get-tuple-element.37), channel_id=1, source_target_pairs={{0,1},{1,0},{2,3},{3,2},{4,5},{5,4},{6,7},{7,6},{8,9},{9,8},{10,11... | collective-permute-start | bytes 884744 | tf_op jit(solution)/shard_map/ppermute | solution.py:376
  39.0 0.0 collective-permute-done.8
  39.0 1.6 %collective-permute-start.9 = (bf16[576,128]{1,0:T(8,128)(2,1)S(1)}, bf16[576,128]{1,0:T(8,128)(2,1)S(1)}, u32[]{:S(2)}, u32[]{:S(2)}) collective-permute-start(bf16[576,128]{1,0:T(8,128)(2,1)S(1)} %add_convert_fusion), channel_id=1, source_target_pairs={{0,2},{2,0},{4,6},{6,4},{8,10},{10,8},{12,14},{14,12},{1,3},{3,1},... | collective-permute-start | bytes 442376 | tf_op jit(solution)/shard_map/ppermute | solution.py:376
  40.6 0.5 %slice_bitcast_fusion = f32[4]{0:T(128)} fusion(f32[8,128]{1,0:T(8,128)S(1)} %get-tuple-element.41), kind=kLoop, calls=%fused_computation.4 | loop fusion | bytes 32 | tf_op jit(solution)/shard_map/squeeze | solution.py:521
  41.1 0.0 collective-permute-done.7.b_ref
  41.1 3.8 %collective-permute-done.9.c_ref = bf16[576,128]{1,0:T(8,128)(2,1)S(1)} collective-permute-done((bf16[576,128]{1,0:T(8,128)(2,1)S(1)}, bf16[576,128]{1,0:T(8,128)(2,1)S(1)}, u32[]{:S(2)}, u32[]{:S(2)}) %collective-permute-start.9) | collective-permute-done | bytes 147488 | tf_op jit(solution)/shard_map/ppermute | solution.py:376
  44.9 1.2 %flat_rows.1 = f32[8,9216]{1,0:T(8,128)} custom-call(f32[576,128]{1,0:T(8,128)S(1)} %get-tuple-element.36.a_ref, f32[576,128]{1,0:T(8,128)S(1)} %collective-permute-done.7.b_ref, bf16[576,128]{1,0:T(8,128)(2,1)S(1)} %collective-permute-done.9.c_ref), custom_call_target="tpu_custom_call" | custom-call | flops 1000000000 | bytes 1000000 | tf_op jit(solution)/shard_map/flat_rows/pallas_call | solution.py:407
  (4 shorter events, 0.1 us)
Async XLA Ops:
  0.6 7.9 %copy-start = (bf16[8,18432]{1,0:T(8,128)(2,1)S(1)}, bf16[8,18432]{1,0:T(8,128)(2,1)}, u32[]{:S(2)}) copy-start(bf16[8,18432]{1,0:T(8,128)(2,1)} %x_ref.1) | copy-start | bytes 884740
  2.9 11.8 %collective-permute-start.1 = (bf16[304,256]{1,0:T(8,128)(2,1)}, bf16[304,256]{1,0:T(8,128)(2,1)S(1)}, u32[]{:S(2)}, u32[]{:S(2)}) collective-permute-start(bf16[304,256]{1,0:T(8,128)(2,1)} %particle_turns.1), channel_id=1, source_target_pairs={{0,8},{2,10},{4,12},{6,14},{8,0},{10,2},{12,4},{14,6},{1,9},{3,11}... | collective-permute-start | bytes 466952 | tf_op jit(solution)/shard_map/ppermute | solution.py:376
  7.0 8.8 %collective-permute-start = (bf16[304,256]{1,0:T(8,128)(2,1)}, bf16[304,256]{1,0:T(8,128)(2,1)S(1)}, u32[]{:S(2)}, u32[]{:S(2)}) collective-permute-start(bf16[304,256]{1,0:T(8,128)(2,1)} %particle_turns.1), channel_id=1, source_target_pairs={{0,4},{2,6},{4,0},{6,2},{8,12},{10,14},{12,8},{14,10},{1,5},{3,7},... | collective-permute-start | bytes 466952 | tf_op jit(solution)/shard_map/ppermute | solution.py:376
  8.6 8.2 %collective-permute-start.3 = (bf16[8,18432]{1,0:T(8,128)(2,1)S(1)}, bf16[8,18432]{1,0:T(8,128)(2,1)S(1)}, u32[]{:S(2)}, u32[]{:S(2)}) collective-permute-start(bf16[8,18432]{1,0:T(8,128)(2,1)S(1)} %copy-done), channel_id=1, source_target_pairs={{0,2},{2,0},{4,6},{6,4},{8,10},{10,8},{12,14},{14,12},{1,3},{3,1},... | collective-permute-start | bytes 884744 | tf_op jit(solution)/shard_map/ppermute | solution.py:376
  10.1 0.7 %copy-start.2 = (f32[64]{0:T(128)S(1)}, f32[64]{0:T(128)}, u32[]{:S(2)}) copy-start(f32[64]{0:T(128)} %param.9) | copy-start | bytes 772
  11.1 0.9 %copy-start.1 = (bf16[304,256]{1,0:T(8,128)(2,1)S(1)}, bf16[304,256]{1,0:T(8,128)(2,1)}, u32[]{:S(2)}) copy-start(bf16[304,256]{1,0:T(8,128)(2,1)} %particle_turns.1) | copy-start | bytes 466948
  14.7 5.2 %collective-permute-start.2 = (bf16[304,256]{1,0:T(8,128)(2,1)S(1)}, bf16[304,256]{1,0:T(8,128)(2,1)S(1)}, u32[]{:S(2)}, u32[]{:S(2)}) collective-permute-start(bf16[304,256]{1,0:T(8,128)(2,1)S(1)} %collective-permute-done.1), channel_id=1, source_target_pairs={{0,4},{2,6},{4,0},{6,2},{8,12},{10,14},{12,8},{14,10},{1,5},{3,7},... | collective-permute-start | bytes 466952 | tf_op jit(solution)/shard_map/ppermute | solution.py:376
  24.8 7.6 %collective-permute-start.6 = (f32[1,8,128]{2,1,0:T(8,128)S(1)}, f32[1,8,128]{2,1,0:T(8,128)S(1)}, u32[]{:S(2)}, u32[]{:S(2)}) collective-permute-start(f32[1,8,128]{2,1,0:T(8,128)S(1)} %get-tuple-element.33.a_5_), channel_id=1, source_target_pairs={{0,12},{2,14},{4,8},{6,10},{8,4},{10,6},{12,0},{14,2},{1,13},{3,15... | collective-permute-start | bytes 12296 | tf_op jit(solution)/shard_map/ppermute | solution.py:376
  28.9 4.5 %collective-permute-start.5 = (f32[1,8,128]{2,1,0:T(8,128)S(1)}, f32[1,8,128]{2,1,0:T(8,128)S(1)}, u32[]{:S(2)}, u32[]{:S(2)}) collective-permute-start(f32[1,8,128]{2,1,0:T(8,128)S(1)} %get-tuple-element.33.a_5_), channel_id=1, source_target_pairs={{0,8},{2,10},{4,12},{6,14},{8,0},{10,2},{12,4},{14,6},{1,9},{3,11}... | collective-permute-start | bytes 12296 | tf_op jit(solution)/shard_map/ppermute | solution.py:376
  28.9 4.5 %collective-permute-start.4 = (f32[1,8,128]{2,1,0:T(8,128)S(1)}, f32[1,8,128]{2,1,0:T(8,128)S(1)}, u32[]{:S(2)}, u32[]{:S(2)}) collective-permute-start(f32[1,8,128]{2,1,0:T(8,128)S(1)} %get-tuple-element.33.a_5_), channel_id=1, source_target_pairs={{0,4},{2,6},{4,0},{6,2},{8,12},{10,14},{12,8},{14,10},{1,5},{3,7},... | collective-permute-start | bytes 12296 | tf_op jit(solution)/shard_map/ppermute | solution.py:376
  35.9 3.1 %collective-permute-start.8 = (f32[576,128]{1,0:T(8,128)S(1)}, f32[576,128]{1,0:T(8,128)S(1)}, u32[]{:S(2)}, u32[]{:S(2)}) collective-permute-start(f32[576,128]{1,0:T(8,128)S(1)} %get-tuple-element.40), channel_id=1, source_target_pairs={{0,1},{1,0},{2,3},{3,2},{4,5},{5,4},{6,7},{7,6},{8,9},{9,8},{10,11... | collective-permute-start | bytes 884744 | tf_op jit(solution)/shard_map/ppermute | solution.py:376
  38.4 2.7 %collective-permute-start.7 = (f32[576,128]{1,0:T(8,128)S(1)}, f32[576,128]{1,0:T(8,128)S(1)}, u32[]{:S(2)}, u32[]{:S(2)}) collective-permute-start(f32[576,128]{1,0:T(8,128)S(1)} %get-tuple-element.37), channel_id=1, source_target_pairs={{0,1},{1,0},{2,3},{3,2},{4,5},{5,4},{6,7},{7,6},{8,9},{9,8},{10,11... | collective-permute-start | bytes 884744 | tf_op jit(solution)/shard_map/ppermute | solution.py:376
  39.0 5.8 %collective-permute-start.9 = (bf16[576,128]{1,0:T(8,128)(2,1)S(1)}, bf16[576,128]{1,0:T(8,128)(2,1)S(1)}, u32[]{:S(2)}, u32[]{:S(2)}) collective-permute-start(bf16[576,128]{1,0:T(8,128)(2,1)S(1)} %add_convert_fusion), channel_id=1, source_target_pairs={{0,2},{2,0},{4,6},{6,4},{8,10},{10,8},{12,14},{14,12},{1,3},{3,1},... | collective-permute-start | bytes 442376 | tf_op jit(solution)/shard_map/ppermute | solution.py:376

commit v4 on v3

--- a/solution.py
+++ b/solution.py
@@ -192,7 +192,7 @@
     return jnp.concatenate([v for x in x_refs for v in (x[0, q], empty)], axis=0)
 
 
-def score_kernel(nbit, me_ref, *refs):
+def score_kernel(nbit, *refs):
     x_refs = refs[:SLOTS]
     bit_refs = refs[SLOTS : 2 * SLOTS]
     own_ref, far_ref, e_ref, stat_ref, acc_ref, pair_ref = refs[2 * SLOTS :]
@@ -201,73 +201,81 @@
     dst = lax.broadcasted_iota(jnp.int32, (SLOTS * 16, HALF), 1)
     slot = dst // 64 + 2 * (dst % 16 // 4)
     place = ((src == slot * 16 + dst % 4) & live_lanes(src.shape)).astype(F32).astype(BF16)
-    lane = lax.broadcasted_iota(jnp.int32, (CLS, LANES), 1)
-    row = lax.broadcasted_iota(jnp.int32, (CLS, LANES), 0)
+    lane = lax.broadcasted_iota(jnp.int32, (2 * CLS, LANES), 1)
+    row = lax.broadcasted_iota(jnp.int32, (2 * CLS, LANES), 0)
+    wanted = (lax.axis_index("cls") ^ row // CLS) * CLS + row % CLS
+    named = jnp.zeros((2 * CLS, SLOTS * 16), F32)
+    for b in range(nbit):
+        pick = (lane + b * LANES == wanted).astype(F32).astype(BF16)
+        first = 16 * (b // 2)
+        bits = jnp.concatenate([r[0, first : first + 16] for r in bit_refs], axis=0)
+        if b % 2:
+            bits = jnp.concatenate(
+                [v for s in range(SLOTS) for v in (bits[s * 16 + 8 : s * 16 + 16], bits[s * 16 : s * 16 + 8])],
+                axis=0,
+            )
+        named += lax.dot_general(pick, bits, (((1,), (1,)), ((), ())), preferred_element_type=F32)
+    masks = jnp.dot(named.astype(BF16), place, preferred_element_type=F32)
     turn = lax.broadcasted_iota(jnp.int32, (CLS, HALF), 1) % 16 // 4
     images = jnp.concatenate([images_of(x_refs, q) for q in range(STEPS)], axis=1)
-    top = jnp.full((CLS, HALF), LOWEST, F32)
     for side, ref in enumerate((own_ref, far_ref)):
         turned = jnp.concatenate([ref[q * 32 : q * 32 + REF_ROWS] for q in range(STEPS)], axis=1)
-        acc_ref[...] = lax.dot_general(turned, images, (((1,), (1,)), ((), ())), preferred_element_type=F32)
-
-        named = jnp.zeros((CLS, SLOTS * 16), F32)
-        chip = me_ref[0] ^ side
-        for b in range(nbit):
-            pick = (lane + b * LANES == chip * CLS + row).astype(F32).astype(BF16)
-            first = 16 * (b // 2)
-            bits = jnp.concatenate([r[0, first : first + 16] for r in bit_refs], axis=0)
-            if b % 2:
-                bits = jnp.concatenate(
-                    [v for s in range(SLOTS) for v in (bits[s * 16 + 8 : s * 16 + 16], bits[s * 16 : s * 16 + 8])],
-                    axis=0,
-                )
-            named += lax.dot_general(pick, bits, (((1,), (1,)), ((), ())), preferred_element_type=F32)
-        mask = jnp.dot(named.astype(BF16), place, preferred_element_type=F32) > 0.5
-
-        def at(i):
+        acc_ref[side] = lax.dot_general(turned, images, (((1,), (1,)), ((), ())), preferred_element_type=F32)
+    stats = []
+    for side in range(2):
+        mask = masks[side * CLS : side * CLS + CLS] > 0.5
+
+        def at(i, side=side):
             i = i % ROT
-            return acc_ref[i * 8 : i * 8 + 8, :HALF], acc_ref[i * 8 : i * 8 + 8, HALF:]
+            return acc_ref[side, i * 8 : i * 8 + 8, :HALF], acc_ref[side, i * 8 : i * 8 + 8, HALF:]
 
         for i in range(ROT):
             (a, b), (c, d) = at(i), at(i + 1)
             low = a + pltpu.roll(c, HALF - 4, 1)
             high = b + pltpu.roll(d, HALF - 4, 1)
-            pair_ref[i * 8 : i * 8 + 8] = jnp.where(turn % 2 == 0, low, pltpu.roll(high, 4, 1))
+            pair_ref[side, i * 8 : i * 8 + 8] = jnp.where(turn % 2 == 0, low, pltpu.roll(high, 4, 1))
+        tops = [jnp.full((CLS, HALF), LOWEST, F32)] * 4
         for i in range(ROT):
             n = (i + 2) % ROT
-            s = pair_ref[i * 8 : i * 8 + 8] + pltpu.roll(pair_ref[n * 8 : n * 8 + 8], HALF - 8, 1)
+            s = pair_ref[side, i * 8 : i * 8 + 8] + pltpu.roll(pair_ref[side, n * 8 : n * 8 + 8], HALF - 8, 1)
             s = jnp.where(mask, s, LOWEST)
             e_ref[0, side, i * 8 : i * 8 + 8] = s
-            top = jnp.maximum(top, s)
-    top = jnp.broadcast_to(jnp.max(top, axis=0, keepdims=True), (CLS, HALF))
-    top = jnp.maximum(top, xor_lanes(top, 16))
-    top = jnp.maximum(top, xor_lanes(top, 32))
-    base = jnp.where(top == LOWEST, 0.0, top)
-    total = jnp.zeros((CLS, HALF), F32)
-    for side in range(2):
+            tops[i % 4] = jnp.maximum(tops[i % 4], s)
+        top = jnp.maximum(jnp.maximum(tops[0], tops[1]), jnp.maximum(tops[2], tops[3]))
+        top = jnp.broadcast_to(jnp.max(top, axis=0, keepdims=True), (CLS, HALF))
+        top = jnp.maximum(top, xor_lanes(top, 16))
+        top = jnp.maximum(top, xor_lanes(top, 32))
+        base = jnp.where(top == LOWEST, 0.0, top)
+        totals = [jnp.zeros((CLS, HALF), F32)] * 4
         for i in range(ROT):
             e = jnp.exp(e_ref[0, side, i * 8 : i * 8 + 8] - base)
             e_ref[0, side, i * 8 : i * 8 + 8] = e
-            total += e
-    total = jnp.broadcast_to(jnp.sum(total, axis=0, keepdims=True), (CLS, HALF))
-    total = total + xor_lanes(total, 16)
-    total = total + xor_lanes(total, 32)
-    stat_ref[0] = jnp.where(lax.broadcasted_iota(jnp.int32, (CLS, HALF), 0) == 0, top, total)
-
-
-def factors(got_refs, stat_ref, nblocks, n):
+            totals[i % 4] += e
+        total = (totals[0] + totals[1]) + (totals[2] + totals[3])
+        total = jnp.broadcast_to(jnp.sum(total, axis=0, keepdims=True), (CLS, HALF))
+        total = total + xor_lanes(total, 16)
+        total = total + xor_lanes(total, 32)
+        stats += [top, total]
+    out = stats[3]
+    line = lax.broadcasted_iota(jnp.int32, (CLS, HALF), 0)
+    for r in (2, 1, 0):
+        out = jnp.where(line == r, stats[r], out)
+    stat_ref[0] = out
+
+
+def factors(side, got_refs, stat_ref, nblocks, n):
     stats = [
         xor_slots(got_refs[low][high, n ^ high], low) for high in range(nblocks) for low in range(SLOTS)
     ]
     spread = lambda x, r: jnp.broadcast_to(x[r : r + 1], (8, HALF))
-    tops = [spread(x, 0) for x in stats]
-    best = tops[0]
-    for top in tops[1:]:
+    pairs = [(spread(x, r), spread(x, r + 1)) for x in stats for r in (0, 2)]
+    best = pairs[0][0]
+    for top, _ in pairs[1:]:
         best = jnp.maximum(best, top)
     evidence = jnp.zeros((8, HALF), F32)
-    for top, x in zip(tops, stats):
-        evidence = evidence + spread(x, 1) * jnp.exp(top - best)
-    factor = jnp.where(live_lanes((8, HALF)), jnp.exp(spread(stat_ref[0], 0) - best) / evidence, 0.0)
+    for top, total in pairs:
+        evidence = evidence + total * jnp.exp(top - best)
+    factor = jnp.where(live_lanes((8, HALF)), jnp.exp(spread(stat_ref[0], 2 * side) - best) / evidence, 0.0)
     return factor, best + jnp.log(evidence)
 
 
@@ -296,14 +304,14 @@
             out_ref[0, i * 8 : i * 8 + 8, HALF:] = b + pltpu.roll(d, 8, 1)
 
 
-def back_kernel(nblocks, me_ref, *refs):
-    got_refs = refs[:SLOTS]
+def back_kernel(side, nblocks, *refs):
+    got_refs = [refs[k] for k in (0, 1, 3, 2)]
     stat_ref, e_ref = refs[SLOTS : SLOTS + 2]
     x_refs = refs[SLOTS + 2 : 2 * SLOTS + 2]
     keep_ref, send_ref, *log_ref = refs[2 * SLOTS + 2 : -2]
     w_ref, acc_ref = refs[-2:]
     n = pl.program_id(0) if nblocks > 1 else 0
-    factor, logs = factors(got_refs, stat_ref, nblocks, n)
+    factor, logs = factors(side, got_refs, stat_ref, nblocks, n)
     if log_ref:
 
         @pl.when(n == 0)
@@ -327,27 +335,12 @@
     )
     images = jnp.concatenate([images_of(x_refs, q) for q in range(STEPS)], axis=0)
     made = jnp.dot(turned, images, preferred_element_type=F32)
-    if nblocks == 1:
-        acc_ref[...] = made
-    else:
-
-        @pl.when(n == 0)
-        def _():
-            acc_ref[...] = made
-
-        @pl.when(n > 0)
-        def _():
-            acc_ref[...] += made
-
-    @pl.when((n == nblocks - 1) & (me_ref[1] == 0))
-    def _():
-        keep_ref[...] = acc_ref[:, :HALF]
-        send_ref[...] = acc_ref[:, HALF:]
-
-    @pl.when((n == nblocks - 1) & (me_ref[1] == 1))
-    def _():
-        keep_ref[...] = acc_ref[:, HALF:]
-        send_ref[...] = acc_ref[:, :HALF]
+    if nblocks > 1:
+        acc_ref[...] = jnp.where(n == 0, made, acc_ref[...] + made)
+        made = acc_ref[...]
+    first = lax.axis_index("dom") == 0
+    keep_ref[...] = jnp.where(first, made[:, :HALF], made[:, HALF:])
+    send_ref[...] = jnp.where(first, made[:, HALF:], made[:, :HALF])
 
 
 def flat_kernel(a_ref, b_ref, c_ref, out_ref, sum_ref, lines_ref, grid_ref):
@@ -378,9 +371,12 @@
 
 def gather_slots(block, relay):
     if lax.axis_size("cls") == 2 * SLOTS:
-        r2 = swap(block, "cls", 4)
-        r1 = swap(block, "cls", 2)
-        r3 = swap(r2, "cls", 2) if relay else swap(block, "cls", 6)
+        if relay:
+            r2 = swap(block, "cls", 4)
+            r1 = swap(block, "cls", 2)
+            r3 = swap(r2, "cls", 2)
+        else:
+            r1, r2, r3 = (swap(block, "cls", bits) for bits in (2, 4, 6))
         return [x[None] for x in (block, r1, r2, r3)]
     slots = block[None]
     bits = 2
@@ -392,8 +388,6 @@
 
 def call(name, body, nblocks, inputs, outputs, scratch, micros=1, vmem=VMEM):
     def spec(shape, kind):
-        if kind == "scalar":
-            return pl.BlockSpec(memory_space=pltpu.SMEM)
         if kind == "any":
             return pl.BlockSpec(memory_space=pltpu.HBM)
         if nblocks == 1:
@@ -423,7 +417,6 @@
     nbit = -(-holders * CLS // LANES)
     extra = -(-(8 * nbit + 8) // 16) * 16
     rows = ROWS + extra
-    me = jnp.stack([lax.axis_index("cls"), lax.axis_index("dom")]).astype(jnp.int32)
 
     def scratch(count):
         return [
@@ -464,7 +457,9 @@
 
     bit_rows = 16 * -(-nbit // 2)
     images, bits = [], []
-    for slot in slots:
+    for s, slot in enumerate(slots):
+        if s == SLOTS - 1:
+            fx, far_refs = lax.optimization_barrier((fx, far_refs))
         x, b = call(
             "shifted",
             lambda *a: shift_kernel(nbit, *a),
@@ -480,30 +475,30 @@
         "scores",
         lambda *a: score_kernel(nbit, *a),
         nblocks,
-        [(me, "scalar")] + [(x, "block") for x in images + bits] + [(own_refs, "all"), (far_refs, "all")],
+        [(x, "block") for x in images + bits] + [(own_refs, "all"), (far_refs, "all")],
         [((nblocks, 2, REF_ROWS, HALF), F32, "block"), ((nblocks, 8, HALF), F32, "block")],
-        [pltpu.VMEM((REF_ROWS, LANES), F32), pltpu.VMEM((REF_ROWS, HALF), F32)],
+        [pltpu.VMEM((2, REF_ROWS, LANES), F32), pltpu.VMEM((2, REF_ROWS, HALF), F32)],
     )
     got = gather_slots(stat, False)
 
     wide = ((nblocks, REF_ROWS, LANES), F32, "block")
     far_expo, own_expo = call("spread", spread_kernel, nblocks, [(expo, "block")], [wide, wide], [])
 
-    def back(name, expo, more):
+    def back(name, side, expo, more):
         half = ((REF_ROWS, HALF), F32, "all")
         return call(
             name,
-            lambda *a: back_kernel(nblocks, *a),
+            lambda *a: back_kernel(side, nblocks, *a),
             nblocks,
-            [(me, "scalar")] + [(g, "all") for g in got] + [(stat, "block"), (expo, "block")] + [(x, "block") for x in images],
+            [(g, "all") for g in [got[k] for k in (0, 1, 3, 2)]] + [(stat, "block"), (expo, "block")] + [(x, "block") for x in images],
             [half, half] + more,
             [pltpu.VMEM((2 * REF_ROWS, LANES), BF16), pltpu.VMEM((REF_ROWS, LANES), F32)],
             4,
         )
 
-    far_keep, far_send, logs = back("far_sums", far_expo, [((8, HALF), F32, "all")])
+    far_keep, far_send = back("far_sums", 1, far_expo, [])
     far_got = swap(far_send, "dom", 1)
-    keep, send = back("own_sums", own_expo, [])
+    keep, send, logs = back("own_sums", 0, own_expo, [((8, HALF), F32, "all")])
     own_got = swap(send, "dom", 1)
     far_sum = swap((far_keep + far_got).astype(BF16), "cls", 1)
     (sums,) = call(

time: 46.3 us -> 44.2 us (0.955)
  Pallas kernels: 18.6 us -> 16.8 us
  local copies, waits for them, and re-layouts: 1.73 us -> 1.08 us
  waiting for transfers between devices: 10.1 us -> 10.6 us
    pallas_call x12, Pallas kernels: 18.6 us -> 16.8 us  [call(): pl.pallas_call(body, out_shape=tuple((jax.ShapeDtypeStruct(shape, dtype)...]
    unnamed x7, local copies, waits for them, and re-layouts: 0.96 us -> 0.3 us
  transfers between devices with their start and end apart: 10 -> 10, of which waited for: 5 -> 5; matrix products, arithmetic and copies ran while one was open for 2% -> 2% of each run, Pallas kernels for 17% -> 16%
where the time goes in v4:
time: 44.2 us; the launch traced here: 44.1 us
  Pallas kernels  16.8 us (38%)
  starting transfers between devices  14.8 us (33%)
  waiting for transfers between devices  10.6 us (24%)
  local copies, waits for them, and re-layouts  1.08 us (2%)
  between operations  0.79 us (2%)
    pallas_call x12, Pallas kernels, call(): pl.pallas_call(body, out_shape=tuple((jax.ShapeDtypeStruct(shape, dtype)...  16.8 us
    ppermute x10, starting transfers between devices, swap(): lax.ppermute(x, axis, [(i, i ^ bits) for i in range(lax.axis_size(axis))])  14.8 us
    ppermute x10, waiting for transfers between devices, swap(): lax.ppermute(x, axis, [(i, i ^ bits) for i in range(lax.axis_size(axis))])  10.6 us
  transfers between devices with their start and end apart: 10, of which 5 were waited for; matrix products, arithmetic and copies ran while one was open for 2% of the time, Pallas kernels for 16%

profile of v4, /device:TPU:0, one launch (start us, length us, event | category | flops | bytes accessed | tf_op | source)
XLA Modules:
  0.0 44.1 jit_solution(6528275561610767755)
XLA Ops:
  0.6 0.0 copy-start
  0.6 0.0 copy-start.2
  0.7 2.2 %particle_turns.1 = bf16[304,256]{1,0:T(8,128)(2,1)} custom-call(bf16[4,18432]{1,0:T(4,128)(2,1)} %a_0_.1, s32[4,32]{1,0:T(4,128)} %a_1_.1, s32[3,2,4]{2,1,0:T(2,128)} %bitcast.25), custom_call_target="tpu_custom_call" | custom-call | flops 1000000000 | bytes 1000000 | tf_op jit(solution)/shard_map/particle_turns/pallas_call | solution.py:401
  2.9 4.1 %collective-permute-start.1 = (bf16[304,256]{1,0:T(8,128)(2,1)}, bf16[304,256]{1,0:T(8,128)(2,1)S(1)}, u32[]{:S(2)}, u32[]{:S(2)}) collective-permute-start(bf16[304,256]{1,0:T(8,128)(2,1)} %particle_turns.1), channel_id=1, source_target_pairs={{0,8},{2,10},{4,12},{6,14},{8,0},{10,2},{12,4},{14,6},{1,9},{3,11}... | collective-permute-start | bytes 466952 | tf_op jit(solution)/shard_map/ppermute | solution.py:369
  7.0 1.6 %collective-permute-start = (bf16[304,256]{1,0:T(8,128)(2,1)}, bf16[304,256]{1,0:T(8,128)(2,1)S(1)}, u32[]{:S(2)}, u32[]{:S(2)}) collective-permute-start(bf16[304,256]{1,0:T(8,128)(2,1)} %particle_turns.1), channel_id=1, source_target_pairs={{0,4},{2,6},{4,0},{6,2},{8,12},{10,14},{12,8},{14,10},{1,5},{3,7},... | collective-permute-start | bytes 466952 | tf_op jit(solution)/shard_map/ppermute | solution.py:369
  8.6 0.0 copy-done
  8.6 1.5 %collective-permute-start.3 = (bf16[8,18432]{1,0:T(8,128)(2,1)S(1)}, bf16[8,18432]{1,0:T(8,128)(2,1)S(1)}, u32[]{:S(2)}, u32[]{:S(2)}) collective-permute-start(bf16[8,18432]{1,0:T(8,128)(2,1)S(1)} %copy-done), channel_id=1, source_target_pairs={{0,2},{2,0},{4,6},{6,4},{8,10},{10,8},{12,14},{14,12},{1,3},{3,1},... | collective-permute-start | bytes 884744 | tf_op jit(solution)/shard_map/ppermute | solution.py:369
  10.1 0.0 copy-done.2
  10.1 0.1 reshape.7
  10.1 0.1 copy.7
  10.2 0.1 reshape_reshape.3
  10.3 0.0 copy-start.1
  10.4 0.6 %own_references.1 = (bf16[1152,256]{1,0:T(8,128)(2,1)S(1)}, f32[144,128]{1,0:T(8,128)S(1)}, f32[144,128]{1,0:T(8,128)S(1)}) custom-call(bf16[8,18432]{1,0:T(8,128)(2,1)S(1)} %copy-done, f32[1,256]{1,0:T(1,128)S(1)} %constant_dynamic-update-slice_fusion.w_ref), custom_call_target="tpu_custom_call" | custom-call | flops 1000000000 | bytes 1000000 | tf_op jit(solution)/shard_map/own_references/pallas_call | solution.py:401
  11.0 0.3 copy-done.1
  11.3 0.4 shifted.4
  11.7 3.0 %collective-permute-done.1 = bf16[304,256]{1,0:T(8,128)(2,1)S(1)} collective-permute-done((bf16[304,256]{1,0:T(8,128)(2,1)}, bf16[304,256]{1,0:T(8,128)(2,1)S(1)}, u32[]{:S(2)}, u32[]{:S(2)}) %collective-permute-start.1) | collective-permute-done | bytes 155680 | tf_op jit(solution)/shard_map/ppermute | solution.py:369
  14.7 0.7 %collective-permute-start.2 = (bf16[304,256]{1,0:T(8,128)(2,1)S(1)}, bf16[304,256]{1,0:T(8,128)(2,1)S(1)}, u32[]{:S(2)}, u32[]{:S(2)}) collective-permute-start(bf16[304,256]{1,0:T(8,128)(2,1)S(1)} %collective-permute-done.1), channel_id=1, source_target_pairs={{0,4},{2,6},{4,0},{6,2},{8,12},{10,14},{12,8},{14,10},{1,5},{3,7},... | collective-permute-start | bytes 466952 | tf_op jit(solution)/shard_map/ppermute | solution.py:369
  15.4 0.4 shifted.6
  15.8 0.0 collective-permute-done
  15.8 0.4 shifted.5
  16.3 0.5 %collective-permute-done.3.x_ref = bf16[8,18432]{1,0:T(8,128)(2,1)S(1)} collective-permute-done((bf16[8,18432]{1,0:T(8,128)(2,1)S(1)}, bf16[8,18432]{1,0:T(8,128)(2,1)S(1)}, u32[]{:S(2)}, u32[]{:S(2)}) %collective-permute-start.3) | collective-permute-done | bytes 294944 | tf_op jit(solution)/shard_map/ppermute | solution.py:369
  16.8 0.6 %far_references.1.a_9_ = bf16[1152,256]{1,0:T(8,128)(2,1)S(1)} custom-call(bf16[8,18432]{1,0:T(8,128)(2,1)S(1)} %collective-permute-done.3.x_ref, f32[1,256]{1,0:T(1,128)S(1)} %constant_dynamic-update-slice_fusion.w_ref), custom_call_target="tpu_custom_call" | custom-call | flops 1000000000 | bytes 1000000 | tf_op jit(solution)/shard_map/far_references/pallas_call | solution.py:401
  17.3 2.6 %collective-permute-done.2 = bf16[304,256]{1,0:T(8,128)(2,1)S(1)} collective-permute-done((bf16[304,256]{1,0:T(8,128)(2,1)S(1)}, bf16[304,256]{1,0:T(8,128)(2,1)S(1)}, u32[]{:S(2)}, u32[]{:S(2)}) %collective-permute-start.2) | collective-permute-done | bytes 155680 | tf_op jit(solution)/shard_map/ppermute | solution.py:369
  19.9 0.4 shifted.7
  20.3 3.8 %scores.1 = (f32[1,2,576,128]{3,2,1,0:T(8,128)S(1)}, f32[1,8,128]{2,1,0:T(8,128)S(1)}) custom-call(bf16[1,18,48,256]{3,2,1,0:T(8,128)(2,1)S(1)} %get-tuple-element.26.a_0_.a_6_, bf16[1,18,48,256]{3,2,1,0:T(8,128)(2,1)S(1)} %get-tuple-element.27.a_1_.a_7_, bf16[1,18,48,256]{3,2,1,0:T(8,128)(2,1)S(1)} %get-tuple-element.28.a_2_.a_8_, ...), custom_call_target="tpu_custom_call" | custom-call | flops 1000000000 | bytes 1000000 | tf_op jit(solution)/shard_map/scores/pallas_call | solution.py:401
  24.2 3.0 %collective-permute-start.6 = (f32[1,8,128]{2,1,0:T(8,128)S(1)}, f32[1,8,128]{2,1,0:T(8,128)S(1)}, u32[]{:S(2)}, u32[]{:S(2)}) collective-permute-start(f32[1,8,128]{2,1,0:T(8,128)S(1)} %get-tuple-element.37.a_4_), channel_id=1, source_target_pairs={{0,8},{2,10},{4,12},{6,14},{8,0},{10,2},{12,4},{14,6},{1,9},{3,11}... | collective-permute-start | bytes 12296 | tf_op jit(solution)/shard_map/ppermute | solution.py:369
  27.2 1.2 %collective-permute-start.5 = (f32[1,8,128]{2,1,0:T(8,128)S(1)}, f32[1,8,128]{2,1,0:T(8,128)S(1)}, u32[]{:S(2)}, u32[]{:S(2)}) collective-permute-start(f32[1,8,128]{2,1,0:T(8,128)S(1)} %get-tuple-element.37.a_4_), channel_id=1, source_target_pairs={{0,12},{2,14},{4,8},{6,10},{8,4},{10,6},{12,0},{14,2},{1,13},{3,15... | collective-permute-start | bytes 12296 | tf_op jit(solution)/shard_map/ppermute | solution.py:369
  28.4 0.5 %collective-permute-start.4 = (f32[1,8,128]{2,1,0:T(8,128)S(1)}, f32[1,8,128]{2,1,0:T(8,128)S(1)}, u32[]{:S(2)}, u32[]{:S(2)}) collective-permute-start(f32[1,8,128]{2,1,0:T(8,128)S(1)} %get-tuple-element.37.a_4_), channel_id=1, source_target_pairs={{0,4},{2,6},{4,0},{6,2},{8,12},{10,14},{12,8},{14,10},{1,5},{3,7},... | collective-permute-start | bytes 12296 | tf_op jit(solution)/shard_map/ppermute | solution.py:369
  28.9 2.9 %spread.1 = (f32[1,576,256]{2,1,0:T(8,128)S(1)}, f32[1,576,256]{2,1,0:T(8,128)S(1)}) custom-call(f32[1,2,576,128]{3,2,1,0:T(8,128)S(1)} %get-tuple-element.38.e_ref), custom_call_target="tpu_custom_call" | custom-call | flops 1000000000 | bytes 1000000 | tf_op jit(solution)/shard_map/spread/pallas_call | solution.py:401
  31.8 0.0 collective-permute-done.6
  31.8 0.8 %collective-permute-done.5 = f32[1,8,128]{2,1,0:T(8,128)S(1)} collective-permute-done((f32[1,8,128]{2,1,0:T(8,128)S(1)}, f32[1,8,128]{2,1,0:T(8,128)S(1)}, u32[]{:S(2)}, u32[]{:S(2)}) %collective-permute-start.5) | collective-permute-done | bytes 4128 | tf_op jit(solution)/shard_map/ppermute | solution.py:369
  32.6 0.0 collective-permute-done.4
  32.6 1.9 %far_sums.1 = (f32[576,128]{1,0:T(8,128)S(1)}, f32[576,128]{1,0:T(8,128)S(1)}) custom-call(f32[1,1,8,128]{3,2,1,0:T(8,128)S(1)} %bitcast.16, f32[1,1,8,128]{3,2,1,0:T(8,128)S(1)} %bitcast.22, f32[1,1,8,128]{3,2,1,0:T(8,128)S(1)} %bitcast.20, f32[1,1,8,128]{3,2,1,0:T(8,128)S(1)} %bitcast.18, f32[1,8,128]{2,1,0:T(8,128)S(1)} %get-tuple-element.37.a_4_, ...), custom_call_target="tpu_custom_call" | custom-call | flops 4000000000 | bytes 4000000 | tf_op jit(solution)/shard_map/far_sums/pallas_call | solution.py:401
  34.5 0.1 collective-permute-start.8
  34.5 1.9 %own_sums.1 = (f32[576,128]{1,0:T(8,128)S(1)}, f32[576,128]{1,0:T(8,128)S(1)}, f32[8,128]{1,0:T(8,128)S(1)}) custom-call(f32[1,1,8,128]{3,2,1,0:T(8,128)S(1)} %bitcast.17, f32[1,1,8,128]{3,2,1,0:T(8,128)S(1)} %bitcast.23, f32[1,1,8,128]{3,2,1,0:T(8,128)S(1)} %bitcast.21, f32[1,1,8,128]{3,2,1,0:T(8,128)S(1)} %bitcast.19, ...), custom_call_target="tpu_custom_call" | custom-call | flops 4000000000 | bytes 4000000 | tf_op jit(solution)/shard_map/own_sums/pallas_call | solution.py:401
  36.4 0.6 %collective-permute-start.7 = (f32[576,128]{1,0:T(8,128)S(1)}, f32[576,128]{1,0:T(8,128)S(1)}, u32[]{:S(2)}, u32[]{:S(2)}) collective-permute-start(f32[576,128]{1,0:T(8,128)S(1)} %get-tuple-element.41), channel_id=1, source_target_pairs={{0,1},{1,0},{2,3},{3,2},{4,5},{5,4},{6,7},{7,6},{8,9},{9,8},{10,11... | collective-permute-start | bytes 884744 | tf_op jit(solution)/shard_map/ppermute | solution.py:369
  37.0 0.0 collective-permute-done.8
  37.0 1.6 %collective-permute-start.9 = (bf16[576,128]{1,0:T(8,128)(2,1)S(1)}, bf16[576,128]{1,0:T(8,128)(2,1)S(1)}, u32[]{:S(2)}, u32[]{:S(2)}) collective-permute-start(bf16[576,128]{1,0:T(8,128)(2,1)S(1)} %add_convert_fusion), channel_id=1, source_target_pairs={{0,2},{2,0},{4,6},{6,4},{8,10},{10,8},{12,14},{14,12},{1,3},{3,1},... | collective-permute-start | bytes 442376 | tf_op jit(solution)/shard_map/ppermute | solution.py:369
  38.6 0.5 %slice_bitcast_fusion = f32[4]{0:T(128)} fusion(f32[8,128]{1,0:T(8,128)S(1)} %get-tuple-element.45), kind=kLoop, calls=%fused_computation.3 | loop fusion | bytes 32 | tf_op jit(solution)/shard_map/squeeze | solution.py:516
  39.1 0.0 collective-permute-done.7.b_ref
  39.1 3.8 %collective-permute-done.9.c_ref = bf16[576,128]{1,0:T(8,128)(2,1)S(1)} collective-permute-done((bf16[576,128]{1,0:T(8,128)(2,1)S(1)}, bf16[576,128]{1,0:T(8,128)(2,1)S(1)}, u32[]{:S(2)}, u32[]{:S(2)}) %collective-permute-start.9) | collective-permute-done | bytes 147488 | tf_op jit(solution)/shard_map/ppermute | solution.py:369
  42.9 1.2 %flat_rows.1 = f32[8,9216]{1,0:T(8,128)} custom-call(f32[576,128]{1,0:T(8,128)S(1)} %get-tuple-element.40.a_ref, f32[576,128]{1,0:T(8,128)S(1)} %collective-permute-done.7.b_ref, bf16[576,128]{1,0:T(8,128)(2,1)S(1)} %collective-permute-done.9.c_ref), custom_call_target="tpu_custom_call" | custom-call | flops 1000000000 | bytes 1000000 | tf_op jit(solution)/shard_map/flat_rows/pallas_call | solution.py:401
  (4 shorter events, 0.1 us)
Async XLA Ops:
  0.6 7.9 %copy-start = (bf16[8,18432]{1,0:T(8,128)(2,1)S(1)}, bf16[8,18432]{1,0:T(8,128)(2,1)}, u32[]{:S(2)}) copy-start(bf16[8,18432]{1,0:T(8,128)(2,1)} %x_ref.1) | copy-start | bytes 884740
  0.6 9.4 %copy-start.2 = (f32[64]{0:T(128)S(1)}, f32[64]{0:T(128)}, u32[]{:S(2)}) copy-start(f32[64]{0:T(128)} %param.9) | copy-start | bytes 772
  2.9 11.8 %collective-permute-start.1 = (bf16[304,256]{1,0:T(8,128)(2,1)}, bf16[304,256]{1,0:T(8,128)(2,1)S(1)}, u32[]{:S(2)}, u32[]{:S(2)}) collective-permute-start(bf16[304,256]{1,0:T(8,128)(2,1)} %particle_turns.1), channel_id=1, source_target_pairs={{0,8},{2,10},{4,12},{6,14},{8,0},{10,2},{12,4},{14,6},{1,9},{3,11}... | collective-permute-start | bytes 466952 | tf_op jit(solution)/shard_map/ppermute | solution.py:369
  7.0 8.8 %collective-permute-start = (bf16[304,256]{1,0:T(8,128)(2,1)}, bf16[304,256]{1,0:T(8,128)(2,1)S(1)}, u32[]{:S(2)}, u32[]{:S(2)}) collective-permute-start(bf16[304,256]{1,0:T(8,128)(2,1)} %particle_turns.1), channel_id=1, source_target_pairs={{0,4},{2,6},{4,0},{6,2},{8,12},{10,14},{12,8},{14,10},{1,5},{3,7},... | collective-permute-start | bytes 466952 | tf_op jit(solution)/shard_map/ppermute | solution.py:369
  8.6 8.2 %collective-permute-start.3 = (bf16[8,18432]{1,0:T(8,128)(2,1)S(1)}, bf16[8,18432]{1,0:T(8,128)(2,1)S(1)}, u32[]{:S(2)}, u32[]{:S(2)}) collective-permute-start(bf16[8,18432]{1,0:T(8,128)(2,1)S(1)} %copy-done), channel_id=1, source_target_pairs={{0,2},{2,0},{4,6},{6,4},{8,10},{10,8},{12,14},{14,12},{1,3},{3,1},... | collective-permute-start | bytes 884744 | tf_op jit(solution)/shard_map/ppermute | solution.py:369
  10.3 0.9 %copy-start.1 = (bf16[304,256]{1,0:T(8,128)(2,1)S(1)}, bf16[304,256]{1,0:T(8,128)(2,1)}, u32[]{:S(2)}) copy-start(bf16[304,256]{1,0:T(8,128)(2,1)} %particle_turns.1) | copy-start | bytes 466948
  14.7 5.2 %collective-permute-start.2 = (bf16[304,256]{1,0:T(8,128)(2,1)S(1)}, bf16[304,256]{1,0:T(8,128)(2,1)S(1)}, u32[]{:S(2)}, u32[]{:S(2)}) collective-permute-start(bf16[304,256]{1,0:T(8,128)(2,1)S(1)} %collective-permute-done.1), channel_id=1, source_target_pairs={{0,4},{2,6},{4,0},{6,2},{8,12},{10,14},{12,8},{14,10},{1,5},{3,7},... | collective-permute-start | bytes 466952 | tf_op jit(solution)/shard_map/ppermute | solution.py:369
  24.2 7.6 %collective-permute-start.6 = (f32[1,8,128]{2,1,0:T(8,128)S(1)}, f32[1,8,128]{2,1,0:T(8,128)S(1)}, u32[]{:S(2)}, u32[]{:S(2)}) collective-permute-start(f32[1,8,128]{2,1,0:T(8,128)S(1)} %get-tuple-element.37.a_4_), channel_id=1, source_target_pairs={{0,8},{2,10},{4,12},{6,14},{8,0},{10,2},{12,4},{14,6},{1,9},{3,11}... | collective-permute-start | bytes 12296 | tf_op jit(solution)/shard_map/ppermute | solution.py:369
  27.2 5.4 %collective-permute-start.5 = (f32[1,8,128]{2,1,0:T(8,128)S(1)}, f32[1,8,128]{2,1,0:T(8,128)S(1)}, u32[]{:S(2)}, u32[]{:S(2)}) collective-permute-start(f32[1,8,128]{2,1,0:T(8,128)S(1)} %get-tuple-element.37.a_4_), channel_id=1, source_target_pairs={{0,12},{2,14},{4,8},{6,10},{8,4},{10,6},{12,0},{14,2},{1,13},{3,15... | collective-permute-start | bytes 12296 | tf_op jit(solution)/shard_map/ppermute | solution.py:369
  28.4 4.2 %collective-permute-start.4 = (f32[1,8,128]{2,1,0:T(8,128)S(1)}, f32[1,8,128]{2,1,0:T(8,128)S(1)}, u32[]{:S(2)}, u32[]{:S(2)}) collective-permute-start(f32[1,8,128]{2,1,0:T(8,128)S(1)} %get-tuple-element.37.a_4_), channel_id=1, source_target_pairs={{0,4},{2,6},{4,0},{6,2},{8,12},{10,14},{12,8},{14,10},{1,5},{3,7},... | collective-permute-start | bytes 12296 | tf_op jit(solution)/shard_map/ppermute | solution.py:369
  34.5 2.5 %collective-permute-start.8 = (f32[576,128]{1,0:T(8,128)S(1)}, f32[576,128]{1,0:T(8,128)S(1)}, u32[]{:S(2)}, u32[]{:S(2)}) collective-permute-start(f32[576,128]{1,0:T(8,128)S(1)} %get-tuple-element.44), channel_id=1, source_target_pairs={{0,1},{1,0},{2,3},{3,2},{4,5},{5,4},{6,7},{7,6},{8,9},{9,8},{10,11... | collective-permute-start | bytes 884744 | tf_op jit(solution)/shard_map/ppermute | solution.py:369
  36.4 2.7 %collective-permute-start.7 = (f32[576,128]{1,0:T(8,128)S(1)}, f32[576,128]{1,0:T(8,128)S(1)}, u32[]{:S(2)}, u32[]{:S(2)}) collective-permute-start(f32[576,128]{1,0:T(8,128)S(1)} %get-tuple-element.41), channel_id=1, source_target_pairs={{0,1},{1,0},{2,3},{3,2},{4,5},{5,4},{6,7},{7,6},{8,9},{9,8},{10,11... | collective-permute-start | bytes 884744 | tf_op jit(solution)/shard_map/ppermute | solution.py:369
  37.0 5.8 %collective-permute-start.9 = (bf16[576,128]{1,0:T(8,128)(2,1)S(1)}, bf16[576,128]{1,0:T(8,128)(2,1)S(1)}, u32[]{:S(2)}, u32[]{:S(2)}) collective-permute-start(bf16[576,128]{1,0:T(8,128)(2,1)S(1)} %add_convert_fusion), channel_id=1, source_target_pairs={{0,2},{2,0},{4,6},{6,4},{8,10},{10,8},{12,14},{14,12},{1,3},{3,1},... | collective-permute-start | bytes 442376 | tf_op jit(solution)/shard_map/ppermute | solution.py:369

commit v5 on v4

--- a/solution.py
+++ b/solution.py
@@ -163,7 +163,7 @@
             x_ref[0, q + STEPS // 2, t * 16 : t * 16 + 16, HALF:] = (b * c + a * s).astype(BF16)
         return carry
 
-    lax.fori_loop(0, STEPS // 2, step, 0, unroll=3)
+    lax.fori_loop(0, STEPS // 2, step, 0, unroll=9)
 
 
 def xor_lanes(x, step):
@@ -193,9 +193,11 @@
 
 
 def score_kernel(nbit, *refs):
-    x_refs = refs[:SLOTS]
-    bit_refs = refs[SLOTS : 2 * SLOTS]
-    own_ref, far_ref, e_ref, stat_ref, acc_ref, pair_ref = refs[2 * SLOTS :]
+    early = SLOTS - 1
+    block_ref, fx_ref, fy_ref, own_ref, far_ref, x_ref, e_ref, stat_ref, bits_ref, acc_ref, pair_ref = refs[2 * early :]
+    x_refs = refs[:early] + (x_ref,)
+    bit_refs = refs[early : 2 * early] + (bits_ref,)
+    shift_kernel(nbit, block_ref, fx_ref, fy_ref, x_ref, bits_ref)
 
     src = lax.broadcasted_iota(jnp.int32, (SLOTS * 16, HALF), 0)
     dst = lax.broadcasted_iota(jnp.int32, (SLOTS * 16, HALF), 1)
@@ -457,9 +459,7 @@
 
     bit_rows = 16 * -(-nbit // 2)
     images, bits = [], []
-    for s, slot in enumerate(slots):
-        if s == SLOTS - 1:
-            fx, far_refs = lax.optimization_barrier((fx, far_refs))
+    for slot in slots[:-1]:
         x, b = call(
             "shifted",
             lambda *a: shift_kernel(nbit, *a),
@@ -471,14 +471,19 @@
         images.append(x)
         bits.append(b)
 
-    expo, stat = call(
+    last, expo, stat = call(
         "scores",
         lambda *a: score_kernel(nbit, *a),
         nblocks,
-        [(x, "block") for x in images + bits] + [(own_refs, "all"), (far_refs, "all")],
-        [((nblocks, 2, REF_ROWS, HALF), F32, "block"), ((nblocks, 8, HALF), F32, "block")],
-        [pltpu.VMEM((2, REF_ROWS, LANES), F32), pltpu.VMEM((2, REF_ROWS, HALF), F32)],
-    )
+        [(x, "block") for x in images + bits + slots[-1:]] + [(fx, "all"), (fy, "all")] + [(own_refs, "all"), (far_refs, "all")],
+        [((nblocks, STEPS, CODED, LANES), BF16, "block"), ((nblocks, 2, REF_ROWS, HALF), F32, "block"), ((nblocks, 8, HALF), F32, "block")],
+        [
+            pltpu.VMEM((1, bit_rows, LANES), BF16),
+            pltpu.VMEM((2, REF_ROWS, LANES), F32),
+            pltpu.VMEM((2, REF_ROWS, HALF), F32),
+        ],
+    )
+    images.append(last)
     got = gather_slots(stat, False)
 
     wide = ((nblocks, REF_ROWS, LANES), F32, "block")

time: 44.2 us -> 43.9 us (level)
    pallas_call x12 -> x11, Pallas kernels: 16.8 us -> 16.4 us  [call(): pl.pallas_call(body, out_shape=tuple((jax.ShapeDtypeStruct(shape, dtype)...]
where the time goes in v5:
time: 43.9 us; the launch traced here: 43.7 us
  Pallas kernels  16.4 us (37%)
  starting transfers between devices  14.8 us (34%)
  waiting for transfers between devices  10.6 us (24%)
  local copies, waits for them, and re-layouts  1.08 us (2%)
  between operations  0.77 us (2%)
    pallas_call x11, Pallas kernels, call(): pl.pallas_call(body, out_shape=tuple((jax.ShapeDtypeStruct(shape, dtype)...  16.4 us
    ppermute x10, starting transfers between devices, swap(): lax.ppermute(x, axis, [(i, i ^ bits) for i in range(lax.axis_size(axis))])  14.8 us
    ppermute x10, waiting for transfers between devices, swap(): lax.ppermute(x, axis, [(i, i ^ bits) for i in range(lax.axis_size(axis))])  10.6 us
  transfers between devices with their start and end apart: 10, of which 5 were waited for; matrix products, arithmetic and copies ran while one was open for 2% of the time, Pallas kernels for 16%

profile of v5, /device:TPU:0, one launch (start us, length us, event | category | flops | bytes accessed | tf_op | source)
XLA Modules:
  0.0 43.7 jit_solution(8007251029501944130)
XLA Ops:
  0.6 0.0 copy-start
  0.6 0.0 copy-start.2
  0.7 2.2 %particle_turns.1 = bf16[304,256]{1,0:T(8,128)(2,1)} custom-call(bf16[4,18432]{1,0:T(4,128)(2,1)} %a_0_.1, s32[4,32]{1,0:T(4,128)} %a_1_.1, s32[3,2,4]{2,1,0:T(2,128)} %bitcast.25), custom_call_target="tpu_custom_call" | custom-call | flops 1000000000 | bytes 1000000 | tf_op jit(solution)/shard_map/particle_turns/pallas_call | solution.py:403
  2.9 4.1 %collective-permute-start.1 = (bf16[304,256]{1,0:T(8,128)(2,1)}, bf16[304,256]{1,0:T(8,128)(2,1)S(1)}, u32[]{:S(2)}, u32[]{:S(2)}) collective-permute-start(bf16[304,256]{1,0:T(8,128)(2,1)} %particle_turns.1), channel_id=1, source_target_pairs={{0,8},{2,10},{4,12},{6,14},{8,0},{10,2},{12,4},{14,6},{1,9},{3,11}... | collective-permute-start | bytes 466952 | tf_op jit(solution)/shard_map/ppermute | solution.py:371
  7.0 1.6 %collective-permute-start = (bf16[304,256]{1,0:T(8,128)(2,1)}, bf16[304,256]{1,0:T(8,128)(2,1)S(1)}, u32[]{:S(2)}, u32[]{:S(2)}) collective-permute-start(bf16[304,256]{1,0:T(8,128)(2,1)} %particle_turns.1), channel_id=1, source_target_pairs={{0,4},{2,6},{4,0},{6,2},{8,12},{10,14},{12,8},{14,10},{1,5},{3,7},... | collective-permute-start | bytes 466952 | tf_op jit(solution)/shard_map/ppermute | solution.py:371
  8.6 0.0 copy-done
  8.6 1.5 %collective-permute-start.3 = (bf16[8,18432]{1,0:T(8,128)(2,1)S(1)}, bf16[8,18432]{1,0:T(8,128)(2,1)S(1)}, u32[]{:S(2)}, u32[]{:S(2)}) collective-permute-start(bf16[8,18432]{1,0:T(8,128)(2,1)S(1)} %copy-done), channel_id=1, source_target_pairs={{0,2},{2,0},{4,6},{6,4},{8,10},{10,8},{12,14},{14,12},{1,3},{3,1},... | collective-permute-start | bytes 884744 | tf_op jit(solution)/shard_map/ppermute | solution.py:371
  10.1 0.0 copy-done.2
  10.1 0.1 reshape.7
  10.1 0.1 copy.7
  10.2 0.1 reshape_reshape.3
  10.3 0.0 copy-start.1
  10.4 0.6 %own_references.1 = (bf16[1152,256]{1,0:T(8,128)(2,1)S(1)}, f32[144,128]{1,0:T(8,128)S(1)}, f32[144,128]{1,0:T(8,128)S(1)}) custom-call(bf16[8,18432]{1,0:T(8,128)(2,1)S(1)} %copy-done, f32[1,256]{1,0:T(1,128)S(1)} %constant_dynamic-update-slice_fusion.w_ref), custom_call_target="tpu_custom_call" | custom-call | flops 1000000000 | bytes 1000000 | tf_op jit(solution)/shard_map/own_references/pallas_call | solution.py:403
  11.0 0.3 copy-done.1
  11.3 0.4 shifted.3
  11.7 3.0 %collective-permute-done.1 = bf16[304,256]{1,0:T(8,128)(2,1)S(1)} collective-permute-done((bf16[304,256]{1,0:T(8,128)(2,1)}, bf16[304,256]{1,0:T(8,128)(2,1)S(1)}, u32[]{:S(2)}, u32[]{:S(2)}) %collective-permute-start.1) | collective-permute-done | bytes 155680 | tf_op jit(solution)/shard_map/ppermute | solution.py:371
  14.7 0.7 %collective-permute-start.2 = (bf16[304,256]{1,0:T(8,128)(2,1)S(1)}, bf16[304,256]{1,0:T(8,128)(2,1)S(1)}, u32[]{:S(2)}, u32[]{:S(2)}) collective-permute-start(bf16[304,256]{1,0:T(8,128)(2,1)S(1)} %collective-permute-done.1), channel_id=1, source_target_pairs={{0,4},{2,6},{4,0},{6,2},{8,12},{10,14},{12,8},{14,10},{1,5},{3,7},... | collective-permute-start | bytes 466952 | tf_op jit(solution)/shard_map/ppermute | solution.py:371
  15.4 0.4 shifted.5
  15.8 0.0 collective-permute-done
  15.8 0.4 shifted.4
  16.2 0.5 %collective-permute-done.3.x_ref = bf16[8,18432]{1,0:T(8,128)(2,1)S(1)} collective-permute-done((bf16[8,18432]{1,0:T(8,128)(2,1)S(1)}, bf16[8,18432]{1,0:T(8,128)(2,1)S(1)}, u32[]{:S(2)}, u32[]{:S(2)}) %collective-permute-start.3) | collective-permute-done | bytes 294944 | tf_op jit(solution)/shard_map/ppermute | solution.py:371
  16.8 0.6 %far_references.1.a_10_ = bf16[1152,256]{1,0:T(8,128)(2,1)S(1)} custom-call(bf16[8,18432]{1,0:T(8,128)(2,1)S(1)} %collective-permute-done.3.x_ref, f32[1,256]{1,0:T(1,128)S(1)} %constant_dynamic-update-slice_fusion.w_ref), custom_call_target="tpu_custom_call" | custom-call | flops 1000000000 | bytes 1000000 | tf_op jit(solution)/shard_map/far_references/pallas_call | solution.py:403
  17.3 2.6 %collective-permute-done.2 = bf16[304,256]{1,0:T(8,128)(2,1)S(1)} collective-permute-done((bf16[304,256]{1,0:T(8,128)(2,1)S(1)}, bf16[304,256]{1,0:T(8,128)(2,1)S(1)}, u32[]{:S(2)}, u32[]{:S(2)}) %collective-permute-start.2) | collective-permute-done | bytes 155680 | tf_op jit(solution)/shard_map/ppermute | solution.py:371
  19.9 3.9 %scores.1 = (bf16[1,18,48,256]{3,2,1,0:T(8,128)(2,1)S(1)}, f32[1,2,576,128]{3,2,1,0:T(8,128)S(1)}, f32[1,8,128]{2,1,0:T(8,128)S(1)}) custom-call(bf16[1,18,48,256]{3,2,1,0:T(8,128)(2,1)S(1)} %get-tuple-element.23.a_0_.a_6_, bf16[1,18,48,256]{3,2,1,0:T(8,128)(2,1)S(1)} %get-tuple-element.24.a_1_.a_7_, ...), custom_call_target="tpu_custom_call" | custom-call | flops 1000000000 | bytes 1000000 | tf_op jit(solution)/shard_map/scores/pallas_call | solution.py:403
  23.8 3.0 %collective-permute-start.6 = (f32[1,8,128]{2,1,0:T(8,128)S(1)}, f32[1,8,128]{2,1,0:T(8,128)S(1)}, u32[]{:S(2)}, u32[]{:S(2)}) collective-permute-start(f32[1,8,128]{2,1,0:T(8,128)S(1)} %get-tuple-element.30.a_4_), channel_id=1, source_target_pairs={{0,8},{2,10},{4,12},{6,14},{8,0},{10,2},{12,4},{14,6},{1,9},{3,11}... | collective-permute-start | bytes 12296 | tf_op jit(solution)/shard_map/ppermute | solution.py:371
  26.8 1.2 %collective-permute-start.5 = (f32[1,8,128]{2,1,0:T(8,128)S(1)}, f32[1,8,128]{2,1,0:T(8,128)S(1)}, u32[]{:S(2)}, u32[]{:S(2)}) collective-permute-start(f32[1,8,128]{2,1,0:T(8,128)S(1)} %get-tuple-element.30.a_4_), channel_id=1, source_target_pairs={{0,12},{2,14},{4,8},{6,10},{8,4},{10,6},{12,0},{14,2},{1,13},{3,15... | collective-permute-start | bytes 12296 | tf_op jit(solution)/shard_map/ppermute | solution.py:371
  28.0 0.5 %collective-permute-start.4 = (f32[1,8,128]{2,1,0:T(8,128)S(1)}, f32[1,8,128]{2,1,0:T(8,128)S(1)}, u32[]{:S(2)}, u32[]{:S(2)}) collective-permute-start(f32[1,8,128]{2,1,0:T(8,128)S(1)} %get-tuple-element.30.a_4_), channel_id=1, source_target_pairs={{0,4},{2,6},{4,0},{6,2},{8,12},{10,14},{12,8},{14,10},{1,5},{3,7},... | collective-permute-start | bytes 12296 | tf_op jit(solution)/shard_map/ppermute | solution.py:371
  28.6 2.9 %spread.1 = (f32[1,576,256]{2,1,0:T(8,128)S(1)}, f32[1,576,256]{2,1,0:T(8,128)S(1)}) custom-call(f32[1,2,576,128]{3,2,1,0:T(8,128)S(1)} %get-tuple-element.31.e_ref), custom_call_target="tpu_custom_call" | custom-call | flops 1000000000 | bytes 1000000 | tf_op jit(solution)/shard_map/spread/pallas_call | solution.py:403
  31.4 0.0 collective-permute-done.6
  31.5 0.8 %collective-permute-done.5 = f32[1,8,128]{2,1,0:T(8,128)S(1)} collective-permute-done((f32[1,8,128]{2,1,0:T(8,128)S(1)}, f32[1,8,128]{2,1,0:T(8,128)S(1)}, u32[]{:S(2)}, u32[]{:S(2)}) %collective-permute-start.5) | collective-permute-done | bytes 4128 | tf_op jit(solution)/shard_map/ppermute | solution.py:371
  32.2 0.0 collective-permute-done.4
  32.2 1.9 %far_sums.1 = (f32[576,128]{1,0:T(8,128)S(1)}, f32[576,128]{1,0:T(8,128)S(1)}) custom-call(f32[1,1,8,128]{3,2,1,0:T(8,128)S(1)} %bitcast.16, f32[1,1,8,128]{3,2,1,0:T(8,128)S(1)} %bitcast.22, f32[1,1,8,128]{3,2,1,0:T(8,128)S(1)} %bitcast.20, f32[1,1,8,128]{3,2,1,0:T(8,128)S(1)} %bitcast.18, f32[1,8,128]{2,1,0:T(8,128)S(1)} %get-tuple-element.30.a_4_, ...), custom_call_target="tpu_custom_call" | custom-call | flops 4000000000 | bytes 4000000 | tf_op jit(solution)/shard_map/far_sums/pallas_call | solution.py:403
  34.1 0.1 collective-permute-start.8
  34.2 1.9 %own_sums.1 = (f32[576,128]{1,0:T(8,128)S(1)}, f32[576,128]{1,0:T(8,128)S(1)}, f32[8,128]{1,0:T(8,128)S(1)}) custom-call(f32[1,1,8,128]{3,2,1,0:T(8,128)S(1)} %bitcast.17, f32[1,1,8,128]{3,2,1,0:T(8,128)S(1)} %bitcast.23, f32[1,1,8,128]{3,2,1,0:T(8,128)S(1)} %bitcast.21, f32[1,1,8,128]{3,2,1,0:T(8,128)S(1)} %bitcast.19, ...), custom_call_target="tpu_custom_call" | custom-call | flops 4000000000 | bytes 4000000 | tf_op jit(solution)/shard_map/own_sums/pallas_call | solution.py:403
  36.0 0.6 %collective-permute-start.7 = (f32[576,128]{1,0:T(8,128)S(1)}, f32[576,128]{1,0:T(8,128)S(1)}, u32[]{:S(2)}, u32[]{:S(2)}) collective-permute-start(f32[576,128]{1,0:T(8,128)S(1)} %get-tuple-element.35), channel_id=1, source_target_pairs={{0,1},{1,0},{2,3},{3,2},{4,5},{5,4},{6,7},{7,6},{8,9},{9,8},{10,11... | collective-permute-start | bytes 884744 | tf_op jit(solution)/shard_map/ppermute | solution.py:371
  36.6 0.0 collective-permute-done.8
  36.6 1.6 %collective-permute-start.9 = (bf16[576,128]{1,0:T(8,128)(2,1)S(1)}, bf16[576,128]{1,0:T(8,128)(2,1)S(1)}, u32[]{:S(2)}, u32[]{:S(2)}) collective-permute-start(bf16[576,128]{1,0:T(8,128)(2,1)S(1)} %add_convert_fusion), channel_id=1, source_target_pairs={{0,2},{2,0},{4,6},{6,4},{8,10},{10,8},{12,14},{14,12},{1,3},{3,1},... | collective-permute-start | bytes 442376 | tf_op jit(solution)/shard_map/ppermute | solution.py:371
  38.2 0.5 %slice_bitcast_fusion = f32[4]{0:T(128)} fusion(f32[8,128]{1,0:T(8,128)S(1)} %get-tuple-element.39), kind=kLoop, calls=%fused_computation.3 | loop fusion | bytes 32 | tf_op jit(solution)/shard_map/squeeze | solution.py:521
  38.7 0.0 collective-permute-done.7.b_ref
  38.7 3.8 %collective-permute-done.9.c_ref = bf16[576,128]{1,0:T(8,128)(2,1)S(1)} collective-permute-done((bf16[576,128]{1,0:T(8,128)(2,1)S(1)}, bf16[576,128]{1,0:T(8,128)(2,1)S(1)}, u32[]{:S(2)}, u32[]{:S(2)}) %collective-permute-start.9) | collective-permute-done | bytes 147488 | tf_op jit(solution)/shard_map/ppermute | solution.py:371
  42.5 1.2 %flat_rows.1 = f32[8,9216]{1,0:T(8,128)} custom-call(f32[576,128]{1,0:T(8,128)S(1)} %get-tuple-element.34.a_ref, f32[576,128]{1,0:T(8,128)S(1)} %collective-permute-done.7.b_ref, bf16[576,128]{1,0:T(8,128)(2,1)S(1)} %collective-permute-done.9.c_ref), custom_call_target="tpu_custom_call" | custom-call | flops 1000000000 | bytes 1000000 | tf_op jit(solution)/shard_map/flat_rows/pallas_call | solution.py:403
  (4 shorter events, 0.1 us)
Async XLA Ops:
  0.6 7.9 %copy-start = (bf16[8,18432]{1,0:T(8,128)(2,1)S(1)}, bf16[8,18432]{1,0:T(8,128)(2,1)}, u32[]{:S(2)}) copy-start(bf16[8,18432]{1,0:T(8,128)(2,1)} %x_ref.1) | copy-start | bytes 884740
  0.6 9.4 %copy-start.2 = (f32[64]{0:T(128)S(1)}, f32[64]{0:T(128)}, u32[]{:S(2)}) copy-start(f32[64]{0:T(128)} %param.9) | copy-start | bytes 772
  2.9 11.8 %collective-permute-start.1 = (bf16[304,256]{1,0:T(8,128)(2,1)}, bf16[304,256]{1,0:T(8,128)(2,1)S(1)}, u32[]{:S(2)}, u32[]{:S(2)}) collective-permute-start(bf16[304,256]{1,0:T(8,128)(2,1)} %particle_turns.1), channel_id=1, source_target_pairs={{0,8},{2,10},{4,12},{6,14},{8,0},{10,2},{12,4},{14,6},{1,9},{3,11}... | collective-permute-start | bytes 466952 | tf_op jit(solution)/shard_map/ppermute | solution.py:371
  7.0 8.8 %collective-permute-start = (bf16[304,256]{1,0:T(8,128)(2,1)}, bf16[304,256]{1,0:T(8,128)(2,1)S(1)}, u32[]{:S(2)}, u32[]{:S(2)}) collective-permute-start(bf16[304,256]{1,0:T(8,128)(2,1)} %particle_turns.1), channel_id=1, source_target_pairs={{0,4},{2,6},{4,0},{6,2},{8,12},{10,14},{12,8},{14,10},{1,5},{3,7},... | collective-permute-start | bytes 466952 | tf_op jit(solution)/shard_map/ppermute | solution.py:371
  8.6 8.2 %collective-permute-start.3 = (bf16[8,18432]{1,0:T(8,128)(2,1)S(1)}, bf16[8,18432]{1,0:T(8,128)(2,1)S(1)}, u32[]{:S(2)}, u32[]{:S(2)}) collective-permute-start(bf16[8,18432]{1,0:T(8,128)(2,1)S(1)} %copy-done), channel_id=1, source_target_pairs={{0,2},{2,0},{4,6},{6,4},{8,10},{10,8},{12,14},{14,12},{1,3},{3,1},... | collective-permute-start | bytes 884744 | tf_op jit(solution)/shard_map/ppermute | solution.py:371
  10.3 0.9 %copy-start.1 = (bf16[304,256]{1,0:T(8,128)(2,1)S(1)}, bf16[304,256]{1,0:T(8,128)(2,1)}, u32[]{:S(2)}) copy-start(bf16[304,256]{1,0:T(8,128)(2,1)} %particle_turns.1) | copy-start | bytes 466948
  14.7 5.2 %collective-permute-start.2 = (bf16[304,256]{1,0:T(8,128)(2,1)S(1)}, bf16[304,256]{1,0:T(8,128)(2,1)S(1)}, u32[]{:S(2)}, u32[]{:S(2)}) collective-permute-start(bf16[304,256]{1,0:T(8,128)(2,1)S(1)} %collective-permute-done.1), channel_id=1, source_target_pairs={{0,4},{2,6},{4,0},{6,2},{8,12},{10,14},{12,8},{14,10},{1,5},{3,7},... | collective-permute-start | bytes 466952 | tf_op jit(solution)/shard_map/ppermute | solution.py:371
  23.8 7.6 %collective-permute-start.6 = (f32[1,8,128]{2,1,0:T(8,128)S(1)}, f32[1,8,128]{2,1,0:T(8,128)S(1)}, u32[]{:S(2)}, u32[]{:S(2)}) collective-permute-start(f32[1,8,128]{2,1,0:T(8,128)S(1)} %get-tuple-element.30.a_4_), channel_id=1, source_target_pairs={{0,8},{2,10},{4,12},{6,14},{8,0},{10,2},{12,4},{14,6},{1,9},{3,11}... | collective-permute-start | bytes 12296 | tf_op jit(solution)/shard_map/ppermute | solution.py:371
  26.8 5.4 %collective-permute-start.5 = (f32[1,8,128]{2,1,0:T(8,128)S(1)}, f32[1,8,128]{2,1,0:T(8,128)S(1)}, u32[]{:S(2)}, u32[]{:S(2)}) collective-permute-start(f32[1,8,128]{2,1,0:T(8,128)S(1)} %get-tuple-element.30.a_4_), channel_id=1, source_target_pairs={{0,12},{2,14},{4,8},{6,10},{8,4},{10,6},{12,0},{14,2},{1,13},{3,15... | collective-permute-start | bytes 12296 | tf_op jit(solution)/shard_map/ppermute | solution.py:371
  28.0 4.2 %collective-permute-start.4 = (f32[1,8,128]{2,1,0:T(8,128)S(1)}, f32[1,8,128]{2,1,0:T(8,128)S(1)}, u32[]{:S(2)}, u32[]{:S(2)}) collective-permute-start(f32[1,8,128]{2,1,0:T(8,128)S(1)} %get-tuple-element.30.a_4_), channel_id=1, source_target_pairs={{0,4},{2,6},{4,0},{6,2},{8,12},{10,14},{12,8},{14,10},{1,5},{3,7},... | collective-permute-start | bytes 12296 | tf_op jit(solution)/shard_map/ppermute | solution.py:371
  34.1 2.5 %collective-permute-start.8 = (f32[576,128]{1,0:T(8,128)S(1)}, f32[576,128]{1,0:T(8,128)S(1)}, u32[]{:S(2)}, u32[]{:S(2)}) collective-permute-start(f32[576,128]{1,0:T(8,128)S(1)} %get-tuple-element.38), channel_id=1, source_target_pairs={{0,1},{1,0},{2,3},{3,2},{4,5},{5,4},{6,7},{7,6},{8,9},{9,8},{10,11... | collective-permute-start | bytes 884744 | tf_op jit(solution)/shard_map/ppermute | solution.py:371
  36.0 2.7 %collective-permute-start.7 = (f32[576,128]{1,0:T(8,128)S(1)}, f32[576,128]{1,0:T(8,128)S(1)}, u32[]{:S(2)}, u32[]{:S(2)}) collective-permute-start(f32[576,128]{1,0:T(8,128)S(1)} %get-tuple-element.35), channel_id=1, source_target_pairs={{0,1},{1,0},{2,3},{3,2},{4,5},{5,4},{6,7},{7,6},{8,9},{9,8},{10,11... | collective-permute-start | bytes 884744 | tf_op jit(solution)/shard_map/ppermute | solution.py:371
  36.6 5.8 %collective-permute-start.9 = (bf16[576,128]{1,0:T(8,128)(2,1)S(1)}, bf16[576,128]{1,0:T(8,128)(2,1)S(1)}, u32[]{:S(2)}, u32[]{:S(2)}) collective-permute-start(bf16[576,128]{1,0:T(8,128)(2,1)S(1)} %add_convert_fusion), channel_id=1, source_target_pairs={{0,2},{2,0},{4,6},{6,4},{8,10},{10,8},{12,14},{14,12},{1,3},{3,1},... | collective-permute-start | bytes 442376 | tf_op jit(solution)/shard_map/ppermute | solution.py:371
